TPU v7x, 256 devices: a whole 4x4x8 slice. The times are simulated.
256 devices in a mesh: dp: 8 (over y_lo, x), expert: 32 (over y_hi, z, core).
Axes of the slice: x: 4, y: 4 (y_hi: 2, y_lo: 2; y = y_hi * 2 + y_lo), z: 8, core: 2. Of those that a mesh axis runs over, the one named last changes fastest.
Arguments:
- tokens: bfloat16 [512, 256, 1280], P(('dp', 'expert')), may hold values from -40 to 40
- router: bfloat16 [32, 1280], replicated, may hold values from -1 to 1
- w_in: bfloat16 [32, 1280, 5120], P('expert', None, 'dp'), may hold values from -0.15625 to 0.15625
- w_out: bfloat16 [32, 5120, 1280], P('expert', 'dp'), may hold values from -0.078125 to 0.078125
- cotangent: bfloat16 [512, 256, 1280], P(('dp', 'expert')), may hold values from -6 to 6
Outputs:
- output: bfloat16 [512, 256, 1280], P(('dp', 'expert'))
- grad_tokens: bfloat16 [512, 256, 1280], P(('dp', 'expert'))
- grad_router: float32 [32, 1280], replicated
- grad_in: bfloat16 [32, 1280, 5120], P('expert', None, 'dp')
- grad_out: bfloat16 [32, 5120, 1280], P('expert', 'dp')
All inputs are finite; a program needn't handle non-finite values.
Results may differ from a plain program's by a relative error of at most 0.03.
Values may be sent and summed in bfloat16 or wider, within the bound.
No kernel may reach another device: no remote copies, remote signals or barrier semaphores. Data moves between devices by JAX's collectives and lax.ppermute only.
A program may use at most 64 MiB of HBM per device.

v0:
```python
import jax
import jax.numpy as jnp
from jax import lax
from jax.sharding import PartitionSpec as P


def expert_forward(rows, w_in, w_out):
    preact = jnp.einsum("bed,edf->bef", rows, w_in, preferred_element_type=jnp.float32)
    hidden = jax.nn.gelu(preact).astype(jnp.bfloat16)
    partial_out = jnp.einsum(
        "bef,efd->bed", hidden, w_out, preferred_element_type=jnp.float32
    ).astype(jnp.bfloat16)
    return (preact, hidden, partial_out)


def expert_backward(rows, grad_rows, preact, hidden, w_in, w_out):
    grad_hidden = jnp.einsum("bed,efd->bef", grad_rows, w_out, preferred_element_type=jnp.float32)
    grad_out = jnp.einsum(
        "bef,bed->efd", hidden, grad_rows, preferred_element_type=jnp.float32
    ).astype(jnp.bfloat16)
    _, pullback = jax.vjp(jax.nn.gelu, preact)
    grad_preact = pullback(grad_hidden)[0].astype(jnp.bfloat16)
    grad_in = jnp.einsum(
        "bed,bef->edf", rows, grad_preact, preferred_element_type=jnp.float32
    ).astype(jnp.bfloat16)
    partial_in = jnp.einsum(
        "bef,edf->bed", grad_preact, w_in, preferred_element_type=jnp.float32
    ).astype(jnp.bfloat16)
    return (grad_in, grad_out, partial_in)


def shards(tokens, router, w_in, w_out, cotangent):
    logits = jnp.einsum("bmd,sd->bsm", tokens, router, preferred_element_type=jnp.float32)
    disp_prob = jax.nn.softmax(logits, axis=2)
    comb_prob = jax.nn.softmax(logits, axis=1)
    dispatch = disp_prob.astype(jnp.bfloat16)
    combine = comb_prob.astype(jnp.bfloat16)
    slots_in = jnp.einsum(
        "bsm,bmd->bsd", dispatch, tokens, preferred_element_type=jnp.float32
    ).astype(jnp.bfloat16)
    grad_slots_out = jnp.einsum(
        "bsm,bmd->bsd", combine, cotangent, preferred_element_type=jnp.float32
    ).astype(jnp.bfloat16)
    sent_in = lax.all_to_all(slots_in, "expert", split_axis=1, concat_axis=0, tiled=True)
    rows = lax.all_gather(sent_in, "dp", axis=0, tiled=True)
    preact, hidden, partial_out = expert_forward(rows, w_in, w_out)
    summed_out = (
        lax.psum_scatter(partial_out, "dp", scatter_dimension=0, tiled=True)
        .astype(jnp.float32)
        .astype(jnp.bfloat16)
    )
    slots_out = lax.all_to_all(summed_out, "expert", split_axis=0, concat_axis=1, tiled=True)
    sent_grad = lax.all_to_all(grad_slots_out, "expert", split_axis=1, concat_axis=0, tiled=True)
    grad_rows = lax.all_gather(sent_grad, "dp", axis=0, tiled=True)
    grad_in, grad_out, partial_in = expert_backward(rows, grad_rows, preact, hidden, w_in, w_out)
    summed_in = (
        lax.psum_scatter(partial_in, "dp", scatter_dimension=0, tiled=True)
        .astype(jnp.float32)
        .astype(jnp.bfloat16)
    )
    grad_slots_in = lax.all_to_all(summed_in, "expert", split_axis=0, concat_axis=1, tiled=True)
    output = jnp.einsum(
        "bsm,bsd->bmd", combine, slots_out, preferred_element_type=jnp.float32
    ).astype(jnp.bfloat16)
    grad_comb = jnp.einsum("bmd,bsd->bsm", cotangent, slots_out, preferred_element_type=jnp.float32)
    grad_disp = jnp.einsum(
        "bmd,bsd->bsm", tokens, grad_slots_in, preferred_element_type=jnp.float32
    )
    grad_logits = comb_prob * (grad_comb - jnp.sum(comb_prob * grad_comb, axis=1, keepdims=True))
    grad_logits = grad_logits + disp_prob * (
        grad_disp - jnp.sum(disp_prob * grad_disp, axis=2, keepdims=True)
    )
    grad_logits = grad_logits.astype(jnp.bfloat16)
    grad_tokens = jnp.einsum(
        "bsm,bsd->bmd", dispatch, grad_slots_in, preferred_element_type=jnp.float32
    )
    grad_tokens = grad_tokens + jnp.einsum(
        "bsm,sd->bmd", grad_logits, router, preferred_element_type=jnp.float32
    )
    grad_tokens = grad_tokens.astype(jnp.bfloat16)
    router_term = jnp.einsum("bsm,bmd->sd", grad_logits, tokens, preferred_element_type=jnp.float32)
    grad_router = lax.psum(router_term, ("dp", "expert"))
    return (output, grad_tokens, grad_router, grad_in, grad_out)


def solution(mesh):
    placed = (
        P(("dp", "expert"), None, None),
        P(),
        P("expert", None, "dp"),
        P("expert", "dp", None),
        P(("dp", "expert"), None, None),
    )
    return jax.shard_map(
        shards,
        mesh=mesh,
        in_specs=placed,
        out_specs=(
            P(("dp", "expert"), None, None),
            P(("dp", "expert"), None, None),
            P(),
            P("expert", None, "dp"),
            P("expert", "dp", None),
        ),
        check_vma=False,
    )
```

profile of v0, /device:TPU:1, one launch (start us, length us, event | category | flops | bytes accessed | tf_op | source)
XLA Modules:
  0.0 488.2 jit_solution(12948460789498233205)
XLA Ops:
  7.2 2.0 convolution_bitcast_fusion.1
  10.5 23.6 %all_to_all.72 = bf16[2,32,1280]{2,0,1:T(2,128)(2,1)S(1)} all-to-all(bf16[2,32,1280]{2,0,1:T(2,128)(2,1)S(1)} %copy.20), channel_id=1, replica_groups=mesh['dp'=8,'expert'=32] {'expert'}, dimensions={1} | all-to-all | bytes 327680 | tf_op jit(solution)/shard_map/all_to_all | solution.py:44
  35.6 1.6 convolution_convert_fusion.5
  37.4 15.6 %all_to_all.73 = bf16[2,32,1280]{2,0,1:T(2,128)(2,1)S(1)} all-to-all(bf16[2,32,1280]{2,0,1:T(2,128)(2,1)S(1)} %copy.23), channel_id=1, replica_groups=mesh['dp'=8,'expert'=32] {'expert'}, dimensions={1} | all-to-all | bytes 327680 | tf_op jit(solution)/shard_map/all_to_all | solution.py:53
  53.9 13.8 %all-gather.3.cloned.1.call-done = bf16[512,1,1280]{2,0,1:T(8,128)(2,1)} async-done(((bf16[64,1,1280]{2,0,1:T(8,128)(2,1)}), bf16[512,1,1280]{2,0,1:T(8,128)(2,1)}) %all-gather.3.cloned.1.call-update) | async-done | bytes 1310736 | tf_op jit(solution)/shard_map/all_gather | solution.py:45
  67.7 3.0 fusion.15
  71.7 2.5 fusion.7
  74.3 37.3 %all-gather.5.cloned.1.call-done = bf16[512,1,1280]{2,0,1:T(8,128)(2,1)} async-done(((bf16[64,1,1280]{2,0,1:T(8,128)(2,1)}), bf16[512,1,1280]{2,0,1:T(8,128)(2,1)}) %all-gather.5.cloned.1.call-update) | async-done | bytes 1310736 | tf_op jit(solution)/shard_map/all_gather | solution.py:54
  111.6 3.5 fusion.38
  116.0 2.3 fusion.8
  118.3 38.3 %reduce-scatter.3.cloned.1.call-done = bf16[64,1,1280]{2,0,1:T(8,128)(2,1)} async-done(((bf16[512,1,1280]{2,0,1:T(8,128)(2,1)}), bf16[64,1,1280]{2,0,1:T(8,128)(2,1)}) %reduce-scatter.3.cloned.1.call-update) | async-done | bytes 163856 | tf_op jit(solution)/shard_map/reduce_scatter | solution.py:48
  159.5 14.8 %all-to-all-start.1 = ((bf16[32,2,1280]{2,1,0:T(2,128)(2,1)}), bf16[32,2,1280]{2,1,0:T(2,128)(2,1)S(1)}, u32[]{:S(2)}, u32[]{:S(2)}) async-start(bf16[32,2,1280]{2,1,0:T(2,128)(2,1)} %reshape.60), calls=%async_computation.2 | async-start | bytes 327680 | tf_op jit(solution)/shard_map/all_to_all | solution.py:52
  174.2 4.0 fusion.6
  178.3 22.9 %reduce-scatter.5.cloned.1.call-done = bf16[64,1,1280]{2,0,1:T(8,128)(2,1)} async-done(((bf16[512,1,1280]{2,0,1:T(8,128)(2,1)}), bf16[64,1,1280]{2,0,1:T(8,128)(2,1)}) %reduce-scatter.5.cloned.1.call-update) | async-done | bytes 163856 | tf_op jit(solution)/shard_map/reduce_scatter | solution.py:57
  203.5 14.9 %all-to-all-start.3 = ((bf16[32,2,1280]{2,1,0:T(2,128)(2,1)}), bf16[32,2,1280]{2,1,0:T(2,128)(2,1)}, u32[]{:S(2)}, u32[]{:S(2)}) async-start(bf16[32,2,1280]{2,1,0:T(2,128)(2,1)} %reshape.62), calls=%async_computation.5 | async-start | bytes 327680 | tf_op jit(solution)/shard_map/all_to_all | solution.py:61
  218.7 3.9 fusion.5
  223.7 2.4 fusion.57
  226.1 3.5 all-to-all-done.3
  231.1 1.6 reduce.1
  235.6 1.9 convolution_bitcast_fusion
  237.5 3.0 fusion.51
  240.5 3.4 fusion.4
  244.0 1.6 convolution_convert_fusion.4
  245.6 234.5 %all-reduce.2.cloned.1.call-done = f32[32,1280]{1,0:T(8,128)} async-done(((f32[32,1280]{1,0:T(8,128)}), f32[32,1280]{1,0:T(8,128)}) %all-reduce.2.cloned.1.call-update) | async-done | bytes 163856 | tf_op jit(solution)/shard_map/psum | solution.py:82
  (55 shorter events, 18.2 us)
Async XLA Ops:
  7.2 64.6 %copy-start = (bf16[1,640,1280]{2,1,0:T(8,128)(2,1)S(1)}, bf16[1,640,1280]{2,1,0:T(8,128)(2,1)}, u32[]{:S(2)}) copy-start(bf16[1,640,1280]{2,1,0:T(8,128)(2,1)} %param.8) | copy-start | bytes 4915204
  7.2 2.8 copy-start.1
  7.2 60.5 %all-gather.3.cloned.1.call-start = ((), (), s32[]{:S(2)}) async-start(), calls=%async_computation.6 | async-start | bytes 1474560 | tf_op jit(solution)/shard_map/all_gather | solution.py:45
  9.9 25.0 %copy-start.7 = (f32[2,32]{1,0:T(2,128)}, f32[2,32]{1,0:T(2,128)S(1)}, u32[]{:S(2)}) copy-start(f32[2,32]{1,0:T(2,128)S(1)} %get-tuple-element.5) | copy-start | bytes 772
  34.9 76.7 %all-gather.5.cloned.1.call-start = ((), (), s32[]{:S(2)}) async-start(), calls=%async_computation.8 | async-start | bytes 1474560 | tf_op jit(solution)/shard_map/all_gather | solution.py:54
  35.6 18.2 %copy-start.5 = (f32[2,256]{1,0:T(2,128)}, f32[2,256]{1,0:T(2,128)S(1)}, u32[]{:S(2)}) copy-start(f32[2,256]{1,0:T(2,128)S(1)} %get-tuple-element.7) | copy-start | bytes 6148
  53.8 102.8 %reduce-scatter.3.cloned.1.call-start = ((), (), s32[]{:S(2)}) async-start(), calls=%async_computation.7 | async-start | bytes 1474560 | tf_op jit(solution)/shard_map/reduce_scatter | solution.py:48
  70.7 1.1 copy-start.11
  74.2 127.0 %reduce-scatter.5.cloned.1.call-start = ((), (), s32[]{:S(2)}) async-start(), calls=%async_computation.9 | async-start | bytes 1474560 | tf_op jit(solution)/shard_map/reduce_scatter | solution.py:57
  111.6 4.4 copy-start.9
  115.1 0.8 copy-start.10
  159.5 44.1 %all-to-all-start.1 = ((bf16[32,2,1280]{2,1,0:T(2,128)(2,1)}), bf16[32,2,1280]{2,1,0:T(2,128)(2,1)S(1)}, u32[]{:S(2)}, u32[]{:S(2)}) async-start(bf16[32,2,1280]{2,1,0:T(2,128)(2,1)} %reshape.60), calls=%async_computation.2 | async-start | bytes 327680 | tf_op jit(solution)/shard_map/all_to_all | solution.py:52
  203.5 26.1 %all-to-all-start.3 = ((bf16[32,2,1280]{2,1,0:T(2,128)(2,1)}), bf16[32,2,1280]{2,1,0:T(2,128)(2,1)}, u32[]{:S(2)}, u32[]{:S(2)}) async-start(bf16[32,2,1280]{2,1,0:T(2,128)(2,1)} %reshape.62), calls=%async_computation.5 | async-start | bytes 327680 | tf_op jit(solution)/shard_map/all_to_all | solution.py:61
  218.4 261.6 %all-reduce.2.cloned.1.call-start = ((), (), s32[]{:S(2)}) async-start(), calls=%async_computation.10 | async-start | bytes 327680 | tf_op jit(solution)/shard_map/psum | solution.py:82
  232.7 2.9 copy-start.3
  233.7 0.8 copy-start.4
  234.2 3.4 copy-start.2
  237.5 3.0 copy-start.8
  240.5 3.4 copy-start.6
Sparse Core Ops, SparseCore 0:
  35.0 32.5 all-gather.2
  70.0 41.5 all-gather.4
  114.7 41.8 reduce-scatter.2
  159.6 41.5 reduce-scatter.4
  240.6 239.3 all-reduce.1
where the time goes:
time: 489 us; the launch traced here: 488 us
  waiting for transfers between devices  350 us (72%)
  blocking collectives  39.3 us (8%)
  matrix products  36 us (7%)
  starting transfers between devices  30.1 us (6%)
  between operations  14 us (3%)
  local copies, waits for them, and re-layouts  10.3 us (2%)
  other arithmetic  8.22 us (2%)
    psum x1, waiting for transfers between devices, shards(): grad_router = lax.psum(router_term, ('dp', 'expert'))  234 us
    reduce_scatter x1, waiting for transfers between devices, shards(): lax.psum_scatter(partial_out, 'dp', scatter_dimension=0, tiled=True)  38.3 us
    all_gather x1, waiting for transfers between devices, shards(): grad_rows = lax.all_gather(sent_grad, 'dp', axis=0, tiled=True)  37.3 us
    all_to_all x1, blocking collectives, shards(): lax.all_to_all(slots_in, 'expert', split_axis=1, concat_axis=0, tiled=True)  23.6 us
    reduce_scatter x1, waiting for transfers between devices, shards(): lax.psum_scatter(partial_in, 'dp', scatter_dimension=0, tiled=True)  22.9 us
    all_to_all x1, blocking collectives, shards(): lax.all_to_all(grad_slots_out, 'expert', split_axis=1, concat_axis=0, til...  15.6 us
    all_to_all x1, starting transfers between devices, shards(): lax.all_to_all(summed_in, 'expert', split_axis=0, concat_axis=1, tiled=True)  14.9 us
    all_to_all x1, starting transfers between devices, shards(): lax.all_to_all(summed_out, 'expert', split_axis=0, concat_axis=1, tiled=T...  14.8 us
  transfers between devices with their start and end apart: 7, of which 6 were waited for; matrix products, arithmetic and copies ran while one was open for 7% of the time, Pallas kernels for 0%

commit v1 on v0

v1 whole, which is shorter than its diff:
```python
import jax
import jax.numpy as jnp
from jax import lax
from jax.sharding import PartitionSpec as P

BF16 = jnp.bfloat16
F32 = jnp.float32
D = 1280


def dot(spec, a, b):
    return jnp.einsum(spec, a, b, preferred_element_type=F32)


def exchange(x, axis):
    return lax.all_to_all(x, axis, split_axis=0, concat_axis=0, tiled=True)


def copies_to_all(x, axis, n):
    return exchange(jnp.broadcast_to(x[None], (n,) + x.shape), axis)


def sum_over_all(term):
    part = jnp.sum(exchange(term, "expert"), axis=0)
    part = jnp.sum(copies_to_all(part, "dp", 8), axis=0)
    return copies_to_all(part, "expert", 32)


def experts(rows, grad_rows, w_in, w_out):
    preact = dot("bd,df->bf", rows, w_in)
    hidden = jax.nn.gelu(preact).astype(BF16)
    partial_out = dot("bf,fd->bd", hidden, w_out).astype(BF16)
    grad_hidden = dot("bd,fd->bf", grad_rows, w_out)
    _, pullback = jax.vjp(jax.nn.gelu, preact)
    grad_preact = pullback(grad_hidden)[0].astype(BF16)
    partial_in = dot("bf,df->bd", grad_preact, w_in).astype(BF16)
    grad_out = dot("bf,bd->fd", hidden, grad_rows).astype(BF16)
    grad_in = dot("bd,bf->df", rows, grad_preact).astype(BF16)
    return (partial_out, partial_in, grad_in, grad_out)


def shards(tokens, router, w_in, w_out, cotangent):
    logits = dot("bmd,sd->bsm", tokens, router)
    disp_prob = jax.nn.softmax(logits, axis=2)
    comb_prob = jax.nn.softmax(logits, axis=1)
    dispatch = disp_prob.astype(BF16)
    combine = comb_prob.astype(BF16)
    slots_in = dot("bsm,bmd->sbd", dispatch, tokens).astype(BF16)
    grad_slots_out = dot("bsm,bmd->sbd", combine, cotangent).astype(BF16)
    sent = exchange(jnp.concatenate([slots_in, grad_slots_out], axis=2), "expert")
    rows = copies_to_all(sent.reshape(64, 2 * D), "dp", 8).reshape(512, 2 * D)
    partial_out, partial_in, grad_in, grad_out = experts(
        rows[:, :D], rows[:, D:], w_in[0], w_out[0]
    )
    partial = jnp.concatenate([partial_out, partial_in], axis=1).reshape(8, 64, 2 * D)
    summed = jnp.sum(exchange(partial, "dp").astype(F32), axis=0).astype(BF16)
    back = exchange(summed.reshape(32, 2, 2 * D), "expert")
    slots_out = back[:, :, :D]
    grad_slots_in = back[:, :, D:]
    grad_comb = dot("bmd,sbd->bsm", cotangent, slots_out)
    grad_disp = dot("bmd,sbd->bsm", tokens, grad_slots_in)
    grad_logits = comb_prob * (grad_comb - jnp.sum(comb_prob * grad_comb, axis=1, keepdims=True))
    grad_logits = grad_logits + disp_prob * (
        grad_disp - jnp.sum(disp_prob * grad_disp, axis=2, keepdims=True)
    )
    grad_logits = grad_logits.astype(BF16)
    router_term = dot("bsm,bmd->sd", grad_logits, tokens)
    grad_router = sum_over_all(router_term)
    output = dot("bsm,sbd->bmd", combine, slots_out).astype(BF16)
    grad_tokens = dot("bsm,sbd->bmd", dispatch, grad_slots_in)
    grad_tokens = grad_tokens + dot("bsm,sd->bmd", grad_logits, router)
    return (output, grad_tokens.astype(BF16), grad_router, grad_in[None], grad_out[None])


def solution(mesh):
    placed = (
        P(("dp", "expert"), None, None),
        P(),
        P("expert", None, "dp"),
        P("expert", "dp", None),
        P(("dp", "expert"), None, None),
    )
    return jax.shard_map(
        shards,
        mesh=mesh,
        in_specs=placed,
        out_specs=(placed[0], placed[0], P(), placed[2], placed[3]),
        check_vma=False,
    )
```

time: 489 us -> 189 us (0.39)
  waiting for transfers between devices: 350 us -> 25.9 us
  blocking collectives: 39.3 us -> 94.5 us
  between operations: 14 us -> 0.81 us
  matrix products: 36 us -> 29.7 us
  starting transfers between devices: 30.1 us -> 25.1 us
    psum x1 -> x0, waiting for transfers between devices: 234 us -> none  [shards(): grad_router = lax.psum(router_term, ('dp', 'expert'))]
    reduce_scatter x2 -> x0, waiting for transfers between devices: 61.2 us -> none  [the longest x1 38.3 us: shards(): lax.psum_scatter(partial_out, 'dp', scatter_dimension=0, tiled=True)]
    all_to_all x2 -> x3, blocking collectives: 39.3 us -> 94.5 us  [exchange(): return lax.all_to_all(x, axis, split_axis=0, concat_axis=0, tiled=True)]
    all_gather x2 -> x0, waiting for transfers between devices: 51.1 us -> none  [the longest x1 37.3 us: shards(): grad_rows = lax.all_gather(sent_grad, 'dp', axis=0, tiled=True)]
    all_to_all x2 -> x4, waiting for transfers between devices: 3.47 us -> 25.9 us  [exchange(): return lax.all_to_all(x, axis, split_axis=0, concat_axis=0, tiled=True)]
    dot_general x15, matrix products: 36 us -> 29.7 us  [dot(): return jnp.einsum(spec, a, b, preferred_element_type=F32)]
    unnamed x29 -> x17, local copies, waits for them, and re-layouts: 6.91 us -> 1.04 us
    all_to_all x2 -> x4, starting transfers between devices: 29.7 us -> 25.1 us  [exchange(): return lax.all_to_all(x, axis, split_axis=0, concat_axis=0, tiled=True)]
  transfers between devices with their start and end apart: 7 -> 4, of which waited for: 6 -> 4; matrix products, arithmetic and copies ran while one was open for 7% -> 8% of each run, Pallas kernels for 0% -> 0%
where the time goes in v1:
time: 189 us; the launch traced here: 188 us
  blocking collectives  94.5 us (50%)
  matrix products  29.7 us (16%)
  waiting for transfers between devices  25.9 us (14%)
  starting transfers between devices  25.1 us (13%)
  local copies, waits for them, and re-layouts  7.7 us (4%)
  other arithmetic  4.35 us (2%)
    all_to_all x3, blocking collectives, exchange(): return lax.all_to_all(x, axis, split_axis=0, concat_axis=0, tiled=True)  94.5 us
    dot_general x15, matrix products, dot(): return jnp.einsum(spec, a, b, preferred_element_type=F32)  29.7 us
    all_to_all x4, waiting for transfers between devices, exchange(): return lax.all_to_all(x, axis, split_axis=0, concat_axis=0, tiled=True)  25.9 us
    all_to_all x4, starting transfers between devices, exchange(): return lax.all_to_all(x, axis, split_axis=0, concat_axis=0, tiled=True)  25.1 us
  transfers between devices with their start and end apart: 4, of which 4 were waited for; matrix products, arithmetic and copies ran while one was open for 8% of the time, Pallas kernels for 0%

profile of v1, /device:TPU:1, one launch (start us, length us, event | category | flops | bytes accessed | tf_op | source)
XLA Modules:
  0.0 188.0 jit_solution(1716360574843260948)
XLA Ops:
  0.7 2.0 %convolution_bitcast_fusion.1 = f32[2,32,256]{2,1,0:T(8,128)S(1)} fusion(bf16[2,256,1280]{2,1,0:T(8,128)(2,1)} %param.5, bf16[32,1280]{1,0:T(8,128)(2,1)} %param.6), kind=kOutput, calls=%fused_computation.41 | convolution fusion | flops 41943040 | bytes 1458176 | tf_op jit(solution)/shard_map/bmd,sd->bsm/dot_general | solution.py:12
  4.0 1.7 fusion.8
  6.0 27.0 %all_to_all.44 = bf16[32,2,2560]{2,1,0:T(2,128)(2,1)S(1)} all-to-all(bf16[32,2,2560]{2,1,0:T(2,128)(2,1)S(1)} %copy.20), channel_id=1, replica_groups=mesh['dp'=8,'expert'=32] {'expert'}, dimensions={0} | all-to-all | bytes 655360 | tf_op jit(solution)/shard_map/all_to_all | solution.py:16
  35.1 34.4 %all_to_all.45 = bf16[8,64,2560]{2,1,0:T(8,128)(2,1)S(1)} all-to-all(bf16[8,64,2560]{2,1,0:T(8,128)(2,1)S(1)} %broadcast_in_dim.13), channel_id=1, replica_groups=mesh['dp'=8,'expert'=32] {'dp'}, dimensions={0} | all-to-all | bytes 5242880 | tf_op jit(solution)/shard_map/all_to_all | solution.py:16
  71.0 1.7 fusion.21
  72.8 1.4 convolution_convert_fusion.3
  75.6 33.1 %all_to_all.46 = bf16[8,64,2560]{2,1,0:T(8,128)(2,1)} all-to-all(bf16[8,64,2560]{2,1,0:T(8,128)(2,1)S(1)} %bitcast.49), channel_id=1, replica_groups=mesh['dp'=8,'expert'=32] {'dp'}, dimensions={0} | all-to-all | bytes 5242880 | tf_op jit(solution)/shard_map/all_to_all | solution.py:16
  108.7 2.1 %reduce_sum.68 = bf16[64,2560]{1,0:T(8,128)(2,1)S(1)} reduce(bf16[8,64,2560]{2,1,0:T(8,128)(2,1)} %all_to_all.46, bf16[]{:T(256)} %constant.19.clone.1), dimensions={0}, to_apply=%region_4.0 | reduce | flops 1146880 | bytes 2949122 | tf_op jit(solution)/shard_map/reduce_sum | solution.py:56
  111.7 9.4 %all-to-all-start.3 = ((bf16[32,2,2560]{2,1,0:T(2,128)(2,1)}), bf16[32,2,2560]{2,1,0:T(2,128)(2,1)}, u32[]{:S(2)}, u32[]{:S(2)}) async-start(bf16[32,2,2560]{2,1,0:T(2,128)(2,1)} %reshape.42), calls=%async_computation.3 | async-start | bytes 655360 | tf_op jit(solution)/shard_map/all_to_all | solution.py:16
  121.1 4.0 %fusion.6 = bf16[1,640,1280]{2,1,0:T(8,128)(2,1)} fusion(bf16[512,2560]{1,0:T(8,128)(2,1)} %bitcast.52, f32[512,640]{1,0:T(8,128)} %copy-done.7), kind=kOutput, calls=%fused_computation.12 | convolution fusion | flops 842629120 | bytes 4259840 | tf_op jit(solution)/shard_map/bf,bd->fd/dot_general | solution.py:12
  125.1 10.5 %all-to-all-done.3 = bf16[32,2,2560]{2,1,0:T(2,128)(2,1)} async-done(((bf16[32,2,2560]{2,1,0:T(2,128)(2,1)}), bf16[32,2,2560]{2,1,0:T(2,128)(2,1)}, u32[]{:S(2)}, u32[]{:S(2)}) %all-to-all-start.3) | async-done | bytes 327712 | tf_op jit(solution)/shard_map/all_to_all | solution.py:16
  135.6 1.2 fusion.58
  136.8 2.4 %fusion.42 = f32[2,32,256]{2,1,0:T(8,128)} fusion(bf16[2,256,1280]{2,1,0:T(8,128)(2,1)} %param.9, bf16[32,2,1280]{2,1,0:T(2,128)(2,1)S(1)} %get-tuple-element.6), kind=kOutput, calls=%fused_computation.56 | convolution fusion | flops 41943040 | bytes 1540096 | tf_op jit(solution)/shard_map/bmd,sbd->bsm/dot_general | solution.py:12
  140.6 1.3 convolution_bitcast_fusion
  142.7 5.3 %all-to-all-start.4 = ((f32[32,1,1280]{2,1,0:T(1,128)}), f32[32,1,1280]{2,1,0:T(1,128)S(1)}, u32[]{:S(2)}, u32[]{:S(2)}) async-start(f32[32,1,1280]{2,1,0:T(1,128)} %copy.23), calls=%async_computation.4 | async-start | bytes 327680 | tf_op jit(solution)/shard_map/all_to_all | solution.py:16
  148.1 3.9 %fusion.5 = bf16[1,1280,640]{2,1,0:T(8,128)(2,1)} fusion(bf16[512,640]{1,0:T(8,128)(2,1)} %copy-done.6, bf16[512,2560]{1,0:T(8,128)(2,1)} %bitcast.53), kind=kOutput, calls=%fused_computation.11 | convolution fusion | flops 839680000 | bytes 3604480 | tf_op jit(solution)/shard_map/bd,bf->df/dot_general | solution.py:12
  152.0 3.0 %fusion.38 = f32[2,256,1280]{2,1,0:T(8,128)} fusion(f32[2,32,256]{2,1,0:T(8,128)S(1)} %copy-done.4, f32[2,32,256]{2,1,0:T(8,128)} %fusion.42, bf16[32,1280]{1,0:T(8,128)(2,1)S(1)} %copy-done.3, f32[2,32,256]{2,1,0:T(8,128)} %get-tuple-element.8, f32[2,256]{1,0:T(2,128)S(1)} %get-tuple-element.7), kind=kOutput, calls=%fused_computation.50 | convolution fusion | flops 42058272 | bytes 2902016 | tf_op jit(solution)/shard_map/bsm,sd->bmd/dot_general | solution.py:12
  155.0 4.3 %all-to-all-done.4 = f32[32,1,1280]{2,1,0:T(1,128)S(1)} async-done(((f32[32,1,1280]{2,1,0:T(1,128)}), f32[32,1,1280]{2,1,0:T(1,128)S(1)}, u32[]{:S(2)}, u32[]{:S(2)}) %all-to-all-start.4) | async-done | bytes 163872 | tf_op jit(solution)/shard_map/all_to_all | solution.py:16
  160.0 3.3 %all-to-all-start.5 = ((f32[8,1,1280]{2,1,0:T(1,128)}), f32[8,1,1280]{2,1,0:T(1,128)S(1)}, u32[]{:S(2)}, u32[]{:S(2)}) async-start(f32[8,1,1280]{2,1,0:T(1,128)} %broadcast_in_dim.14), calls=%async_computation.5 | async-start | bytes 81920 | tf_op jit(solution)/shard_map/all_to_all | solution.py:16
  163.4 1.6 convolution_convert_fusion.4
  165.0 3.4 %all-to-all-done.5 = f32[8,1,1280]{2,1,0:T(1,128)S(1)} async-done(((f32[8,1,1280]{2,1,0:T(1,128)}), f32[8,1,1280]{2,1,0:T(1,128)S(1)}, u32[]{:S(2)}, u32[]{:S(2)}) %all-to-all-start.5) | async-done | bytes 40992 | tf_op jit(solution)/shard_map/all_to_all | solution.py:16
  169.2 7.0 %all-to-all-start.6 = ((f32[32,1,1280]{2,1,0:T(1,128)}), f32[32,1,1280]{2,1,0:T(1,128)S(1)}, u32[]{:S(2)}, u32[]{:S(2)}) async-start(f32[32,1,1280]{2,1,0:T(1,128)} %broadcast_in_dim.15), calls=%async_computation.6 | async-start | bytes 327680 | tf_op jit(solution)/shard_map/all_to_all | solution.py:16
  176.3 3.4 %fusion.4 = bf16[2,256,1280]{2,1,0:T(8,128)(2,1)} fusion(f32[2,256,1280]{2,1,0:T(8,128)} %fusion.38, bf16[32,2,1280]{2,1,0:T(2,128)(2,1)S(1)} %get-tuple-element.5, f32[2,32]{1,0:T(2,128)S(1)} %get-tuple-element.9, f32[2,32,256]{2,1,0:T(8,128)S(1)} %convolution_bitcast_fusion.1), kind=kOutput, calls=%fused_computation.9 | convolution fusion | flops 43303232 | bytes 4161792 | tf_op jit(solution)/shard_map/bsm,sbd->bmd/dot_general | solution.py:12
  179.7 7.7 %all-to-all-done.6 = f32[32,1,1280]{2,1,0:T(1,128)S(1)} async-done(((f32[32,1,1280]{2,1,0:T(1,128)}), f32[32,1,1280]{2,1,0:T(1,128)S(1)}, u32[]{:S(2)}, u32[]{:S(2)}) %all-to-all-start.6) | async-done | bytes 163872 | tf_op jit(solution)/shard_map/all_to_all | solution.py:16
  (35 shorter events, 11.9 us)
Async XLA Ops:
  0.6 70.4 %copy-start = (bf16[1,640,1280]{2,1,0:T(8,128)(2,1)S(1)}, bf16[1,640,1280]{2,1,0:T(8,128)(2,1)}, u32[]{:S(2)}) copy-start(bf16[1,640,1280]{2,1,0:T(8,128)(2,1)} %param.8) | copy-start | bytes 4915204
  0.6 3.0 %copy-start.1 = (bf16[2,256,1280]{2,1,0:T(8,128)(2,1)S(1)}, bf16[2,256,1280]{2,1,0:T(8,128)(2,1)}, u32[]{:S(2)}) copy-start(bf16[2,256,1280]{2,1,0:T(8,128)(2,1)} %param.5) | copy-start | bytes 3932164
  35.1 34.4 %copy-start.5 = (bf16[1,1280,640]{2,1,0:T(8,128)(2,1)S(1)}, bf16[1,1280,640]{2,1,0:T(8,128)(2,1)}, u32[]{:S(2)}) copy-start(bf16[1,1280,640]{2,1,0:T(8,128)(2,1)} %param.7) | copy-start | bytes 4915204
  69.5 1.5 copy-start.2
  71.0 1.8 copy-start.7
  72.8 1.4 copy-start.6
  111.7 23.9 %all-to-all-start.3 = ((bf16[32,2,2560]{2,1,0:T(2,128)(2,1)}), bf16[32,2,2560]{2,1,0:T(2,128)(2,1)}, u32[]{:S(2)}, u32[]{:S(2)}) async-start(bf16[32,2,2560]{2,1,0:T(2,128)(2,1)} %reshape.42), calls=%async_computation.3 | async-start | bytes 655360 | tf_op jit(solution)/shard_map/all_to_all | solution.py:16
  142.7 16.5 %all-to-all-start.4 = ((f32[32,1,1280]{2,1,0:T(1,128)}), f32[32,1,1280]{2,1,0:T(1,128)S(1)}, u32[]{:S(2)}, u32[]{:S(2)}) async-start(f32[32,1,1280]{2,1,0:T(1,128)} %copy.23), calls=%async_computation.4 | async-start | bytes 327680 | tf_op jit(solution)/shard_map/all_to_all | solution.py:16
  148.1 3.9 %copy-start.3 = (bf16[32,1280]{1,0:T(8,128)(2,1)S(1)}, bf16[32,1280]{1,0:T(8,128)(2,1)}, u32[]{:S(2)}) copy-start(bf16[32,1280]{1,0:T(8,128)(2,1)} %param.6) | copy-start | bytes 245764
  148.1 3.9 %copy-start.4 = (f32[2,32,256]{2,1,0:T(8,128)S(1)}, f32[2,32,256]{2,1,0:T(8,128)}, u32[]{:S(2)}) copy-start(f32[2,32,256]{2,1,0:T(8,128)} %fusion.36) | copy-start | bytes 196612
  160.0 8.4 %all-to-all-start.5 = ((f32[8,1,1280]{2,1,0:T(1,128)}), f32[8,1,1280]{2,1,0:T(1,128)S(1)}, u32[]{:S(2)}, u32[]{:S(2)}) async-start(f32[8,1,1280]{2,1,0:T(1,128)} %broadcast_in_dim.14), calls=%async_computation.5 | async-start | bytes 81920 | tf_op jit(solution)/shard_map/all_to_all | solution.py:16
  169.2 18.1 %all-to-all-start.6 = ((f32[32,1,1280]{2,1,0:T(1,128)}), f32[32,1,1280]{2,1,0:T(1,128)S(1)}, u32[]{:S(2)}, u32[]{:S(2)}) async-start(f32[32,1,1280]{2,1,0:T(1,128)} %broadcast_in_dim.15), calls=%async_computation.6 | async-start | bytes 327680 | tf_op jit(solution)/shard_map/all_to_all | solution.py:16

commit v2 on v1

v2 whole, which is shorter than its diff:
```python
import functools

import jax
import jax.numpy as jnp
from jax import lax
from jax.experimental import pallas as pl
from jax.experimental.pallas import tpu as pltpu
from jax.sharding import Mesh, PartitionSpec as P

BF16 = jnp.bfloat16
F32 = jnp.float32
D = 1280
M = 256
SLOTS = 32
HID = 640
AXES = ("yl", "x", "yh", "z", "c")
DP = ("yl", "x")
EXPERT = ("yh", "z", "c")
PLANE = ("yl", "x", "c")
COLUMN = ("yh", "z")
VMEM = pl.BlockSpec(memory_space=pltpu.VMEM)
SMEM = pl.BlockSpec(memory_space=pltpu.SMEM)
PARAMS = pltpu.CompilerParams(vmem_limit_bytes=16 * 2**20)


def cost(flops, size):
    return pl.CostEstimate(flops=flops, bytes_accessed=size, transcendentals=0)


def mm(a, b):
    return jnp.dot(a, b, preferred_element_type=F32)


def mm_nt(a, b):
    return lax.dot_general(a, b, (((1,), (1,)), ((), ())), preferred_element_type=F32)


def mm_tn(a, b):
    return lax.dot_general(a, b, (((0,), (0,)), ((), ())), preferred_element_type=F32)


def add(*terms):
    total = terms[0].astype(F32)
    for term in terms[1:]:
        total = total + term.astype(F32)
    return total.astype(BF16)


def exchange(x, axes):
    return lax.all_to_all(x, axes, split_axis=0, concat_axis=0, tiled=True)


def x_up(a):
    return lax.ppermute(a, "x", [(i, (i + 1) % 4) for i in range(4)])


def x_down(a):
    return lax.ppermute(a, "x", [(i, (i + 3) % 4) for i in range(4)])


def y_swap(a):
    return lax.ppermute(a, "yl", [(0, 1), (1, 0)])


def core_swap(a):
    return lax.ppermute(a, "c", [(0, 1), (1, 0)])


def natural_row(r, core):
    slot = 2 * (r >> 3) + (((r >> 2) & 1) ^ core)
    return ((r >> 1) & 1) * 64 + (r & 1) * 32 + slot


def to_message(core, rows):
    r = lax.broadcasted_iota(jnp.int32, (128, 128), 0)
    n = lax.broadcasted_iota(jnp.int32, (128, 128), 1)
    pick = (n == natural_row(r, core)).astype(F32).astype(BF16)
    return mm(pick, rows).astype(BF16)


def from_message(core, message):
    n = lax.broadcasted_iota(jnp.int32, (128, 128), 0)
    r = lax.broadcasted_iota(jnp.int32, (128, 128), 1)
    pick = (n == natural_row(r, core)).astype(F32).astype(BF16)
    return mm(pick, message).astype(BF16)


def route_kernel(core, tokens, router, cotangent, message, probs, rows):
    image = pl.program_id(0)
    tok = tokens[0]
    logits = mm_nt(router[...], tok)
    disp = jnp.exp(logits - jnp.max(logits, axis=1, keepdims=True))
    disp = disp / jnp.sum(disp, axis=1, keepdims=True)
    comb = jnp.exp(logits - jnp.max(logits, axis=0, keepdims=True))
    comb = comb / jnp.sum(comb, axis=0, keepdims=True)
    probs[0, 0] = disp
    probs[0, 1] = comb
    first = pl.multiple_of(image * SLOTS, SLOTS)
    rows[pl.ds(first, SLOTS), :] = mm(disp.astype(BF16), tok).astype(BF16)
    rows[pl.ds(64 + first, SLOTS), :] = mm(comb.astype(BF16), cotangent[0]).astype(BF16)

    @pl.when(image == 1)
    def _():
        message[...] = to_message(core[0], rows[...])


def route(core, tokens, router, cotangent):
    image = pl.BlockSpec((1, M, D), lambda b: (b, 0, 0))
    probs = pl.BlockSpec((1, 2, SLOTS, M), lambda b: (b, 0, 0, 0))
    return pl.pallas_call(
        route_kernel,
        grid=(2,),
        in_specs=[SMEM, image, pl.BlockSpec((SLOTS, D), lambda b: (0, 0)), image],
        out_specs=[pl.BlockSpec((128, D), lambda b: (0, 0)), probs],
        out_shape=[
            jax.ShapeDtypeStruct((128, D), BF16),
            jax.ShapeDtypeStruct((2, 2, SLOTS, M), F32),
        ],
        scratch_shapes=[pltpu.VMEM((128, D), BF16)],
        compiler_params=pltpu.CompilerParams(vmem_limit_bytes=56 * 2**20),
        cost_estimate=cost(10**9, 3 * 10**6),
    )(core, tokens, router, cotangent)


def experts_kernel(n, *refs):
    held, (w_in, w_out) = refs[:n], refs[n : n + 2]
    sent, (hidden, grad_preact) = refs[n + 2 : 2 * n + 2], refs[2 * n + 2 :]
    rows = jnp.concatenate([h[:, :D] for h in held], axis=0)
    grad_rows = jnp.concatenate([h[:, D:] for h in held], axis=0)
    x = mm(rows, w_in[...])
    square = x * x
    scale = 0.7978845608028654
    t = jnp.tanh(scale * (x + 0.044715 * (square * x)))
    half = 0.5 * (1.0 + t)
    hid = (x * half).astype(BF16)
    slope = half + 0.5 * x * (1.0 - t * t) * (scale * (1.0 + 0.134145 * square))
    hidden[...] = hid
    grad = (mm_nt(grad_rows, w_out[...]) * slope).astype(BF16)
    grad_preact[...] = grad
    out = mm(hid, w_out[...]).astype(BF16)
    inner = mm_nt(grad, w_in[...]).astype(BF16)
    first = 0
    for s in sent:
        last = first + s.shape[0]
        s[:, :D] = out[first:last]
        s[:, D:] = inner[first:last]
        first = last


def experts(held, w_in, w_out):
    n = len(held)
    total = sum(h.shape[0] for h in held)
    shapes = [jax.ShapeDtypeStruct(h.shape, BF16) for h in held]
    shapes += [jax.ShapeDtypeStruct((total, HID), BF16)] * 2
    results = pl.pallas_call(
        functools.partial(experts_kernel, n),
        in_specs=[VMEM] * (n + 2),
        out_specs=[VMEM] * (n + 2),
        out_shape=shapes,
        compiler_params=PARAMS,
        cost_estimate=cost(8 * total * D * HID, 4 * 10**6),
    )(*held, w_in, w_out)
    return results[:n], results[n], results[n + 1]


def pack_kernel(stay, go, message):
    rows = jnp.concatenate([stay[:, :D], stay[:, D:], go[:, :D], go[:, D:]], axis=0)
    r = lax.broadcasted_iota(jnp.int32, (128, 128), 0)
    n = lax.broadcasted_iota(jnp.int32, (128, 128), 1)
    pick = n == ((r >> 2) & 1) * 64 + ((r >> 1) & 1) * 32 + (r >> 3) * 2 + (r & 1)
    message[...] = mm(pick.astype(F32).astype(BF16), rows).astype(BF16)


def pack(stay, go):
    return pl.pallas_call(
        pack_kernel,
        in_specs=[VMEM] * 2,
        out_specs=VMEM,
        out_shape=jax.ShapeDtypeStruct((128, D), BF16),
        compiler_params=PARAMS,
        cost_estimate=cost(10**8, 10**6),
    )(stay, go)


def gate_kernel(core, message, tokens, cotangent, probs, slots, gates, term):
    rows = from_message(core[0], message[...])
    slots[...] = rows
    total = jnp.zeros((SLOTS, D), F32)
    for b in range(2):
        disp, comb = probs[b, 0], probs[b, 1]
        grad_comb = mm_nt(rows[b * 32 : b * 32 + 32], cotangent[b])
        grad_disp = mm_nt(rows[64 + b * 32 : 96 + b * 32], tokens[b])
        grad = comb * (grad_comb - jnp.sum(comb * grad_comb, axis=0, keepdims=True))
        grad += disp * (grad_disp - jnp.sum(disp * grad_disp, axis=1, keepdims=True))
        grad = grad.astype(BF16)
        gates[b] = grad
        total += mm(grad, tokens[b])
    total = total.astype(BF16)
    for e in range(16):
        term[e] = total[2 * e : 2 * e + 2]


def gate(core, message, tokens, cotangent, probs):
    return pl.pallas_call(
        gate_kernel,
        in_specs=[SMEM] + [VMEM] * 4,
        out_specs=[VMEM] * 3,
        out_shape=[
            jax.ShapeDtypeStruct((128, D), BF16),
            jax.ShapeDtypeStruct((2, SLOTS, M), BF16),
            jax.ShapeDtypeStruct((16, 2, D), BF16),
        ],
        compiler_params=PARAMS,
        cost_estimate=cost(10**9, 3 * 10**6),
    )(core, message, tokens, cotangent, probs)


def spread_kernel(slots, gates, probs, router, output, grad_tokens):
    first = pl.multiple_of(pl.program_id(0) * SLOTS, SLOTS)
    slots_out = slots[pl.ds(first, SLOTS), :]
    grad_slots_in = slots[pl.ds(64 + first, SLOTS), :]
    output[0] = mm_tn(probs[0, 1].astype(BF16), slots_out).astype(BF16)
    grad = mm_tn(probs[0, 0].astype(BF16), grad_slots_in) + mm_tn(gates[0], router[...])
    grad_tokens[0] = grad.astype(BF16)


def spread(slots, gates, probs, router):
    image = pl.BlockSpec((1, M, D), lambda b: (b, 0, 0))
    shares = pl.BlockSpec((1, 2, SLOTS, M), lambda b: (b, 0, 0, 0))
    return pl.pallas_call(
        spread_kernel,
        grid=(2,),
        in_specs=[
            pl.BlockSpec((128, D), lambda b: (0, 0)),
            pl.BlockSpec((1, SLOTS, M), lambda b: (b, 0, 0)),
            shares,
            pl.BlockSpec((SLOTS, D), lambda b: (0, 0)),
        ],
        out_specs=[image, image],
        out_shape=[jax.ShapeDtypeStruct((2, M, D), BF16)] * 2,
        compiler_params=PARAMS,
        cost_estimate=cost(10**9, 3 * 10**6),
    )(slots, gates, probs, router)


def low(a):
    return a[:32]


def high(a):
    return a[32:]


def join(a, b):
    return jnp.concatenate([a, b])


def sum_over_all(term):
    part = exchange(term, PLANE)
    part = jnp.sum(part.astype(F32), axis=0).astype(BF16)
    part = exchange(jnp.broadcast_to(part[None], (16, 2, D)), COLUMN)
    part = jnp.sum(part.astype(F32), axis=0).astype(BF16)
    part = exchange(jnp.broadcast_to(part[None], (16, 2, D)), PLANE)
    return part.reshape(SLOTS, D).astype(F32)


def shards(tokens, router, w_in, w_out, cotangent):
    core = lax.axis_index("c").astype(jnp.int32).reshape(1)
    w_in, w_out = w_in[0], w_out[0]
    message, probs = route(core, tokens, router, cotangent)

    arrived = exchange(message.reshape(16, 8, D), COLUMN)
    arrived = arrived.reshape(16, 2, 2, 2, D).transpose(1, 0, 3, 2, 4).reshape(2, 32, 2 * D)
    own = join(arrived[0], core_swap(arrived[1]))

    down, up, side = x_up(own), x_down(own), y_swap(own)
    first = x_up(join(low(side), low(down)))
    second = x_down(join(low(side), high(up)))
    third = y_swap(join(high(down), high(up)))
    near = experts((own, down, up, side), w_in, w_out)
    first, third, near = lax.optimization_barrier((first, third, near))
    far_low = x_up(low(first))
    far_high = x_down(high(third))
    middle = experts((first, second, third), w_in, w_out)
    far_low, far_high, middle = lax.optimization_barrier((far_low, far_high, middle))
    far = experts((far_low, far_high), w_in, w_out)

    (own_sum, down_sum, up_sum, side_sum), (first_sum, second_sum, third_sum) = near[0], middle[0]
    low_sum, high_sum = far[0]
    low_in, high_in = x_down(low_sum), x_up(high_sum)
    second_in = x_up(second_sum)
    first_in = x_down(join(add(low(first_sum), low_in), high(first_sum)))
    third_in = y_swap(join(low(third_sum), add(high(third_sum), high_in)))
    side_in = y_swap(join(add(low(side_sum), low(first_in), low(second_in)), high(side_sum)))
    down_in = x_down(
        join(add(low(down_sum), high(first_in)), add(high(down_sum), low(third_in)))
    )
    up_in = x_up(join(low(up_sum), add(high(up_sum), high(second_in), high(third_in))))
    summed = add(own_sum, down_in, up_in, side_in)

    leaving = pack(low(summed), core_swap(high(summed)))
    returned = exchange(leaving.reshape(16, 8, D), COLUMN).reshape(128, D)
    slots, gates, term = gate(core, returned, tokens, cotangent, probs)
    grad_router = sum_over_all(term)
    output, grad_tokens = spread(slots, gates, probs, router)

    rows = jnp.concatenate([own, down, up, side, first, second, third, far_low, far_high])
    hidden = jnp.concatenate([near[1], middle[1], far[1]])
    grad_preact = jnp.concatenate([near[2], middle[2], far[2]])
    grad_in = mm_tn(rows[:, :D], grad_preact).astype(BF16)
    grad_out = mm_tn(hidden, rows[:, D:]).astype(BF16)
    return (output, grad_tokens, grad_router, grad_in[None], grad_out[None])


def solution(mesh):
    fine = Mesh(mesh.devices.reshape(2, 4, 2, 8, 2), AXES)
    images = P(AXES, None, None)
    placed = (images, P(), P(EXPERT, None, DP), P(EXPERT, DP, None), images)
    return jax.shard_map(
        shards,
        mesh=fine,
        in_specs=placed,
        out_specs=(images, images, P(), placed[2], placed[3]),
        check_vma=False,
    )
```

time: 189 us -> 154 us (0.81)
  blocking collectives: 94.5 us -> 23 us
  starting transfers between devices: 25.1 us -> 52.1 us
  matrix products: 29.7 us -> 7.47 us
  waiting for transfers between devices: 25.9 us -> 46.6 us
  Pallas kernels: 0 us -> 15.4 us
  other arithmetic: 4.35 us -> 0.8 us
    all_to_all x3 -> x1, blocking collectives: 94.5 us -> 23 us  [exchange(): return lax.all_to_all(x, axes, split_axis=0, concat_axis=0, tiled=True)]
    ppermute x0 -> x18, starting transfers between devices: none -> 31.6 us  [the longest x6 13.5 us: x_down(): return lax.ppermute(a, 'x', [(i, (i + 3) % 4) for i in range(4)])]
    ppermute x0 -> x18, waiting for transfers between devices: none -> 25.8 us  [the longest x6 17.2 us: x_up(): return lax.ppermute(a, 'x', [(i, (i + 1) % 4) for i in range(4)])]
    dot_general x15 -> x2, matrix products: 29.7 us -> 7.47 us  [mm_tn(): lax.dot_general(a, b, (((0,), (0,)), ((), ())), preferred_element_type=F32)]
    pallas_call x0 -> x7, Pallas kernels: none -> 15.4 us  [the longest x3 5.83 us: experts(): pl.pallas_call(functools.partial(experts_kernel, n), in_specs=[VMEM] * (n...]
    all_to_all x4, waiting for transfers between devices: 25.9 us -> 20.8 us  [exchange(): return lax.all_to_all(x, axes, split_axis=0, concat_axis=0, tiled=True)]
    all_to_all x4, starting transfers between devices: 25.1 us -> 20.5 us  [exchange(): return lax.all_to_all(x, axes, split_axis=0, concat_axis=0, tiled=True)]
    unnamed x17 -> x43, local copies, waits for them, and re-layouts: 1.04 us -> 3.28 us
  transfers between devices with their start and end apart: 4 -> 22, of which waited for: 4 -> 13; matrix products, arithmetic and copies ran while one was open for 8% -> 6% of each run, Pallas kernels for 0% -> 4%
where the time goes in v2:
time: 154 us; the launch traced here: 153 us
  starting transfers between devices  52.1 us (34%)
  waiting for transfers between devices  46.6 us (30%)
  blocking collectives  23 us (15%)
  Pallas kernels  15.4 us (10%)
  matrix products  7.47 us (5%)
  local copies, waits for them, and re-layouts  6.57 us (4%)
    all_to_all x1, blocking collectives, exchange(): return lax.all_to_all(x, axes, split_axis=0, concat_axis=0, tiled=True)  23 us
    all_to_all x4, waiting for transfers between devices, exchange(): return lax.all_to_all(x, axes, split_axis=0, concat_axis=0, tiled=True)  20.8 us
    all_to_all x4, starting transfers between devices, exchange(): return lax.all_to_all(x, axes, split_axis=0, concat_axis=0, tiled=True)  20.5 us
    ppermute x6, waiting for transfers between devices, x_up(): return lax.ppermute(a, 'x', [(i, (i + 1) % 4) for i in range(4)])  17.2 us
    ppermute x6, starting transfers between devices, x_down(): return lax.ppermute(a, 'x', [(i, (i + 3) % 4) for i in range(4)])  13.5 us
    ppermute x2, starting transfers between devices, core_swap(): return lax.ppermute(a, 'c', [(0, 1), (1, 0)])  12.5 us
    dot_general x2, matrix products, mm_tn(): lax.dot_general(a, b, (((0,), (0,)), ((), ())), preferred_element_type=F32)  7.47 us
    ppermute x6, waiting for transfers between devices, x_down(): return lax.ppermute(a, 'x', [(i, (i + 3) % 4) for i in range(4)])  6.67 us
  transfers between devices with their start and end apart: 22, of which 13 were waited for; matrix products, arithmetic and copies ran while one was open for 6% of the time, Pallas kernels for 4%

profile of v2, /device:TPU:1, one launch (start us, length us, event | category | flops | bytes accessed | tf_op | source)
XLA Modules:
  0.0 153.1 jit_solution(14609020821311881184)
XLA Ops:
  0.6 4.4 %shard_map.92 = (bf16[128,1280]{1,0:T(8,128)(2,1)}, f32[2,2,32,256]{3,2,1,0:T(8,128)}) custom-call(s32[1]{0:T(128)} %bitcast.core, bf16[2,256,1280]{2,1,0:T(8,128)(2,1)} %tokens.3, bf16[32,1280]{1,0:T(8,128)(2,1)} %router.3, bf16[2,256,1280]{2,1,0:T(8,128)(2,1)} %cotangent.3), custom_call_target="tpu_custom_call" | custom-call | flops 1000000000 | bytes 3000000 | tf_op jit(solution)/shard_map/pallas_call | solution.py:110
  5.0 23.0 %all_to_all.25 = bf16[16,8,1280]{2,1,0:T(8,128)(2,1)S(1)} all-to-all(bf16[16,8,1280]{2,1,0:T(8,128)(2,1)} %bitcast.30), channel_id=1, replica_groups=mesh['yl'=2,'x'=4,'yh'=2,'z'=8,'c'=2] {'yh','z'}, dimensions={0} | all-to-all | bytes 655360 | tf_op jit(solution)/shard_map/all_to_all | solution.py:50
  28.5 2.7 %collective-permute-start = (bf16[32,2560]{1,0:T(8,128)(2,1)S(1)}, bf16[32,2560]{1,0:T(8,128)(2,1)S(1)}, u32[]{:S(2)}, u32[]{:S(2)}) collective-permute-start(bf16[32,2560]{1,0:T(8,128)(2,1)S(1)} %bitcast.31), channel_id=1, source_target_pairs={{0,1},{1,0},{2,3},{3,2},{4,5},{5,4},{6,7},{7,6},{8,9},{9,8},{10,11... | collective-permute-start | bytes 491528 | tf_op jit(solution)/shard_map/ppermute | solution.py:66
  35.4 7.1 %collective-permute-done.2.refs_1_ = bf16[64,2560]{1,0:T(8,128)(2,1)S(1)} collective-permute-done((bf16[64,2560]{1,0:T(8,128)(2,1)S(1)}, bf16[64,2560]{1,0:T(8,128)(2,1)S(1)}, u32[]{:S(2)}, u32[]{:S(2)}) %collective-permute-start.2) | collective-permute-done | bytes 327712 | tf_op jit(solution)/shard_map/ppermute | solution.py:54
  46.3 2.2 %shard_map.93 = (bf16[64,2560]{1,0:T(8,128)(2,1)S(1)}, bf16[64,2560]{1,0:T(8,128)(2,1)S(1)}, bf16[64,2560]{1,0:T(8,128)(2,1)S(1)}, bf16[64,2560]{1,0:T(8,128)(2,...) custom-call(bf16[64,2560]{1,0:T(8,128)(2,1)S(1)} %get-tuple-element.90.refs_0_, ...), custom_call_target="tpu_custom_call" | custom-call | flops 1677721600 | bytes 4000000 | tf_op jit(solution)/shard_map/pallas_call | solution.py:155
  48.6 3.0 %collective-permute-done.3.refs_0_ = bf16[64,2560]{1,0:T(8,128)(2,1)S(1)} collective-permute-done((bf16[64,2560]{1,0:T(8,128)(2,1)S(1)}, bf16[64,2560]{1,0:T(8,128)(2,1)S(1)}, u32[]{:S(2)}, u32[]{:S(2)}) %collective-permute-start.3) | collective-permute-done | bytes 327712 | tf_op jit(solution)/shard_map/ppermute | solution.py:54
  51.8 2.9 %collective-permute-start.7 = (bf16[32,2560]{1,0:T(8,128)(2,1)S(1)}, bf16[32,2560]{1,0:T(8,128)(2,1)S(1)}, u32[]{:S(2)}, u32[]{:S(2)}) collective-permute-start(bf16[32,2560]{1,0:T(8,128)(2,1)S(1)} %slice.96), channel_id=1, source_target_pairs={{0,96},{32,0},{64,32},{96,64},{1,97},{33,1},{65,33},{97,65},{2,98}... | collective-permute-start | bytes 491528 | tf_op jit(solution)/shard_map/ppermute | solution.py:58
  59.4 2.6 %collective-permute-start.9 = (bf16[32,2560]{1,0:T(8,128)(2,1)S(1)}, bf16[32,2560]{1,0:T(8,128)(2,1)S(1)}, u32[]{:S(2)}, u32[]{:S(2)}) collective-permute-start(bf16[32,2560]{1,0:T(8,128)(2,1)S(1)} %get-tuple-element.61), channel_id=1, source_target_pairs={{0,96},{32,0},{64,32},{96,64},{1,97},{33,1},{65,33},{97,65},{2,98}... | collective-permute-start | bytes 491528 | tf_op jit(solution)/shard_map/ppermute | solution.py:58
  62.1 2.4 %collective-permute-done.11 = bf16[32,2560]{1,0:T(8,128)(2,1)S(1)} collective-permute-done((bf16[32,2560]{1,0:T(8,128)(2,1)S(1)}, bf16[32,2560]{1,0:T(8,128)(2,1)S(1)}, u32[]{:S(2)}, u32[]{:S(2)}) %collective-permute-start.11) | collective-permute-done | bytes 163872 | tf_op jit(solution)/shard_map/ppermute | solution.py:54
  65.2 2.3 %collective-permute-start.10 = (bf16[64,2560]{1,0:T(8,128)(2,1)S(1)}, bf16[64,2560]{1,0:T(8,128)(2,1)S(1)}, u32[]{:S(2)}, u32[]{:S(2)}) collective-permute-start(bf16[64,2560]{1,0:T(8,128)(2,1)S(1)} %pad_maximum_fusion.3), channel_id=1, source_target_pairs={{0,96},{32,0},{64,32},{96,64},{1,97},{33,1},{65,33},{97,65},{2,98}... | collective-permute-start | bytes 983048 | tf_op jit(solution)/shard_map/ppermute | solution.py:58
  67.5 4.3 %collective-permute-done.14 = bf16[64,2560]{1,0:T(8,128)(2,1)S(1)} collective-permute-done((bf16[64,2560]{1,0:T(8,128)(2,1)S(1)}, bf16[64,2560]{1,0:T(8,128)(2,1)S(1)}, u32[]{:S(2)}, u32[]{:S(2)}) %collective-permute-start.14) | collective-permute-done | bytes 327712 | tf_op jit(solution)/shard_map/ppermute | solution.py:54
  72.9 2.6 %collective-permute-start.13 = (bf16[64,2560]{1,0:T(8,128)(2,1)S(1)}, bf16[64,2560]{1,0:T(8,128)(2,1)S(1)}, u32[]{:S(2)}, u32[]{:S(2)}) collective-permute-start(bf16[64,2560]{1,0:T(8,128)(2,1)S(1)} %pad_maximum_fusion.5), channel_id=1, source_target_pairs={{0,96},{32,0},{64,32},{96,64},{1,97},{33,1},{65,33},{97,65},{2,98}... | collective-permute-start | bytes 983048 | tf_op jit(solution)/shard_map/ppermute | solution.py:58
  76.5 5.9 %collective-permute-done.13 = bf16[64,2560]{1,0:T(8,128)(2,1)S(1)} collective-permute-done((bf16[64,2560]{1,0:T(8,128)(2,1)S(1)}, bf16[64,2560]{1,0:T(8,128)(2,1)S(1)}, u32[]{:S(2)}, u32[]{:S(2)}) %collective-permute-start.13) | collective-permute-done | bytes 327712 | tf_op jit(solution)/shard_map/ppermute | solution.py:58
  82.9 9.8 %collective-permute-start.17 = (bf16[32,2560]{1,0:T(8,128)(2,1)S(1)}, bf16[32,2560]{1,0:T(8,128)(2,1)S(1)}, u32[]{:S(2)}, u32[]{:S(2)}) collective-permute-start(bf16[32,2560]{1,0:T(8,128)(2,1)S(1)} %get-tuple-element.79), channel_id=1, source_target_pairs={{0,1},{1,0},{2,3},{3,2},{4,5},{5,4},{6,7},{7,6},{8,9},{9,8},{10,11... | collective-permute-start | bytes 491528 | tf_op jit(solution)/shard_map/ppermute | solution.py:66
  94.7 4.5 %all-to-all-start.1 = ((bf16[16,8,1280]{2,1,0:T(8,128)(2,1)}), bf16[16,8,1280]{2,1,0:T(8,128)(2,1)S(1)}, u32[]{:S(2)}, u32[]{:S(2)}) async-start(bf16[16,8,1280]{2,1,0:T(8,128)(2,1)} %bitcast.7), calls=%async_computation.1 | async-start | bytes 655360 | tf_op jit(solution)/shard_map/all_to_all | solution.py:50
  100.6 10.0 %all-to-all-done.1 = bf16[16,8,1280]{2,1,0:T(8,128)(2,1)S(1)} async-done(((bf16[16,8,1280]{2,1,0:T(8,128)(2,1)}), bf16[16,8,1280]{2,1,0:T(8,128)(2,1)S(1)}, u32[]{:S(2)}, u32[]{:S(2)}) %all-to-all-start.1) | async-done | bytes 327712 | tf_op jit(solution)/shard_map/all_to_all | solution.py:50
  114.3 5.9 %all-to-all-start.2 = ((bf16[16,2,1280]{2,1,0:T(2,128)(2,1)}), bf16[16,2,1280]{2,1,0:T(2,128)(2,1)S(1)}, u32[]{:S(2)}, u32[]{:S(2)}) async-start(bf16[16,2,1280]{2,1,0:T(2,128)(2,1)} %get-tuple-element.72), calls=%async_computation.2 | async-start | bytes 163840 | tf_op jit(solution)/shard_map/all_to_all | solution.py:50
  120.2 3.9 %fusion = bf16[1,1280,640]{2,1,0:T(8,128)(2,1)} fusion(bf16[512,2560]{1,0:T(8,128)(2,1)} %constant_dynamic-update-slice_fusion.2, bf16[64,640]{1,0:T(8,128)(2,1)S(1)} %get-tuple-element.75, bf16[192,640]{1,0:T(8,128)(2,1)} %copy-done.7, bf16[256,640]{1,0:T(8,128)(2,1)} %copy-done.14), kind=kOutput, calls=%fused_computation.2 | convolution fusion | flops 841646080 | bytes 3604480 | tf_op jit(solution)/shard_map/dot_general | solution.py:39
  126.7 5.0 %all-to-all-start.3 = ((bf16[16,2,1280]{2,1,0:T(2,128)(2,1)}), bf16[16,2,1280]{2,1,0:T(2,128)(2,1)S(1)}, u32[]{:S(2)}, u32[]{:S(2)}) async-start(bf16[16,2,1280]{2,1,0:T(2,128)(2,1)} %broadcast_in_dim.8), calls=%async_computation.3 | async-start | bytes 163840 | tf_op jit(solution)/shard_map/all_to_all | solution.py:50
  131.8 3.6 %fusion.1 = bf16[1,640,1280]{2,1,0:T(8,128)(2,1)} fusion(bf16[512,2560]{1,0:T(8,128)(2,1)} %constant_dynamic-update-slice_fusion.2, bf16[64,640]{1,0:T(8,128)(2,1)S(1)} %get-tuple-element.78, bf16[192,640]{1,0:T(8,128)(2,1)S(1)} %copy-done.6, bf16[256,640]{1,0:T(8,128)(2,1)S(1)} %copy-done.13), kind=kOutput, calls=%fused_computation.3 | convolution fusion | flops 841646080 | bytes 3604480 | tf_op jit(solution)/shard_map/dot_general | solution.py:39
  135.3 5.3 %all-to-all-done.3 = bf16[16,2,1280]{2,1,0:T(2,128)(2,1)S(1)} async-done(((bf16[16,2,1280]{2,1,0:T(2,128)(2,1)}), bf16[16,2,1280]{2,1,0:T(2,128)(2,1)S(1)}, u32[]{:S(2)}, u32[]{:S(2)}) %all-to-all-start.3) | async-done | bytes 81952 | tf_op jit(solution)/shard_map/all_to_all | solution.py:50
  141.4 5.1 %all-to-all-start.4 = ((bf16[16,2,1280]{2,1,0:T(2,128)(2,1)}), bf16[16,2,1280]{2,1,0:T(2,128)(2,1)S(1)}, u32[]{:S(2)}, u32[]{:S(2)}) async-start(bf16[16,2,1280]{2,1,0:T(2,128)(2,1)} %broadcast_in_dim.9), calls=%async_computation.4 | async-start | bytes 163840 | tf_op jit(solution)/shard_map/all_to_all | solution.py:50
  146.5 2.3 %shard_map.98 = (bf16[2,256,1280]{2,1,0:T(8,128)(2,1)}, bf16[2,256,1280]{2,1,0:T(8,128)(2,1)}) custom-call(bf16[128,1280]{1,0:T(8,128)(2,1)S(1)} %copy-done.9, bf16[2,32,256]{2,1,0:T(8,128)(2,1)S(1)} %get-tuple-element.69.gates, f32[2,2,32,256]{3,2,1,0:T(8,128)S(1)} %copy-done.11, bf16[32,1280]{1,0:T(8,128)(2,1)S(1)} %copy-done.4), custom_call_target="tpu_custom_call" | custom-call | flops 1000000000 | bytes 3000000 | tf_op jit(solution)/shard_map/pallas_call | solution.py:230
  148.8 3.6 %all-to-all-done.4 = bf16[16,2,1280]{2,1,0:T(2,128)(2,1)S(1)} async-done(((bf16[16,2,1280]{2,1,0:T(2,128)(2,1)}), bf16[16,2,1280]{2,1,0:T(2,128)(2,1)S(1)}, u32[]{:S(2)}, u32[]{:S(2)}) %all-to-all-start.4) | async-done | bytes 81952 | tf_op jit(solution)/shard_map/all_to_all | solution.py:50
  (103 shorter events, 27.5 us)
Async XLA Ops:
  28.5 3.7 %collective-permute-start = (bf16[32,2560]{1,0:T(8,128)(2,1)S(1)}, bf16[32,2560]{1,0:T(8,128)(2,1)S(1)}, u32[]{:S(2)}, u32[]{:S(2)}) collective-permute-start(bf16[32,2560]{1,0:T(8,128)(2,1)S(1)} %bitcast.31), channel_id=1, source_target_pairs={{0,1},{1,0},{2,3},{3,2},{4,5},{5,4},{6,7},{7,6},{8,9},{9,8},{10,11... | collective-permute-start | bytes 491528 | tf_op jit(solution)/shard_map/ppermute | solution.py:66
  32.3 10.2 %collective-permute-start.2 = (bf16[64,2560]{1,0:T(8,128)(2,1)S(1)}, bf16[64,2560]{1,0:T(8,128)(2,1)S(1)}, u32[]{:S(2)}, u32[]{:S(2)}) collective-permute-start(bf16[64,2560]{1,0:T(8,128)(2,1)S(1)} %get-tuple-element.90.refs_0_), channel_id=1, source_target_pairs={{0,32},{32,64},{64,96},{96,0},{1,33},{33,65},{65,97},{97,1},{2,34}... | collective-permute-start | bytes 983048 | tf_op jit(solution)/shard_map/ppermute | solution.py:54
  33.6 9.0 %collective-permute-start.1 = (bf16[64,2560]{1,0:T(8,128)(2,1)S(1)}, bf16[64,2560]{1,0:T(8,128)(2,1)S(1)}, u32[]{:S(2)}, u32[]{:S(2)}) collective-permute-start(bf16[64,2560]{1,0:T(8,128)(2,1)S(1)} %get-tuple-element.90.refs_0_), channel_id=1, source_target_pairs={{0,128},{128,0},{1,129},{129,1},{2,130},{130,2},{3,131},{131,3},{4... | collective-permute-start | bytes 983048 | tf_op jit(solution)/shard_map/ppermute | solution.py:62
  34.0 8.6 %collective-permute-start.4 = (bf16[64,2560]{1,0:T(8,128)(2,1)S(1)}, bf16[64,2560]{1,0:T(8,128)(2,1)S(1)}, u32[]{:S(2)}, u32[]{:S(2)}) collective-permute-start(bf16[64,2560]{1,0:T(8,128)(2,1)S(1)} %get-tuple-element.90.refs_0_), channel_id=1, source_target_pairs={{0,96},{32,0},{64,32},{96,64},{1,97},{33,1},{65,33},{97,65},{2,98}... | collective-permute-start | bytes 983048 | tf_op jit(solution)/shard_map/ppermute | solution.py:58
  42.7 9.0 %collective-permute-start.3 = (bf16[64,2560]{1,0:T(8,128)(2,1)S(1)}, bf16[64,2560]{1,0:T(8,128)(2,1)S(1)}, u32[]{:S(2)}, u32[]{:S(2)}) collective-permute-start(bf16[64,2560]{1,0:T(8,128)(2,1)S(1)} %get-tuple-element.95), channel_id=1, source_target_pairs={{0,32},{32,64},{64,96},{96,0},{1,33},{33,65},{65,97},{97,1},{2,34}... | collective-permute-start | bytes 983048 | tf_op jit(solution)/shard_map/ppermute | solution.py:54
  43.7 8.0 %collective-permute-start.5 = (bf16[64,2560]{1,0:T(8,128)(2,1)S(1)}, bf16[64,2560]{1,0:T(8,128)(2,1)S(1)}, u32[]{:S(2)}, u32[]{:S(2)}) collective-permute-start(bf16[64,2560]{1,0:T(8,128)(2,1)S(1)} %get-tuple-element.94), channel_id=1, source_target_pairs={{0,128},{128,0},{1,129},{129,1},{2,130},{130,2},{3,131},{131,3},{4... | collective-permute-start | bytes 983048 | tf_op jit(solution)/shard_map/ppermute | solution.py:62
  44.7 10.0 %collective-permute-start.8 = (bf16[64,2560]{1,0:T(8,128)(2,1)S(1)}, bf16[64,2560]{1,0:T(8,128)(2,1)S(1)}, u32[]{:S(2)}, u32[]{:S(2)}) collective-permute-start(bf16[64,2560]{1,0:T(8,128)(2,1)S(1)} %get-tuple-element.93), channel_id=1, source_target_pairs={{0,96},{32,0},{64,32},{96,64},{1,97},{33,1},{65,33},{97,65},{2,98}... | collective-permute-start | bytes 983048 | tf_op jit(solution)/shard_map/ppermute | solution.py:58
  51.7 5.8 %collective-permute-start.6 = (bf16[32,2560]{1,0:T(8,128)(2,1)S(1)}, bf16[32,2560]{1,0:T(8,128)(2,1)S(1)}, u32[]{:S(2)}, u32[]{:S(2)}) collective-permute-start(bf16[32,2560]{1,0:T(8,128)(2,1)S(1)} %slice.95), channel_id=1, source_target_pairs={{0,32},{32,64},{64,96},{96,0},{1,33},{33,65},{65,97},{97,1},{2,34}... | collective-permute-start | bytes 491528 | tf_op jit(solution)/shard_map/ppermute | solution.py:54
  51.8 5.7 %collective-permute-start.7 = (bf16[32,2560]{1,0:T(8,128)(2,1)S(1)}, bf16[32,2560]{1,0:T(8,128)(2,1)S(1)}, u32[]{:S(2)}, u32[]{:S(2)}) collective-permute-start(bf16[32,2560]{1,0:T(8,128)(2,1)S(1)} %slice.96), channel_id=1, source_target_pairs={{0,96},{32,0},{64,32},{96,64},{1,97},{33,1},{65,33},{97,65},{2,98}... | collective-permute-start | bytes 491528 | tf_op jit(solution)/shard_map/ppermute | solution.py:58
  59.1 5.5 %collective-permute-start.11 = (bf16[32,2560]{1,0:T(8,128)(2,1)S(1)}, bf16[32,2560]{1,0:T(8,128)(2,1)S(1)}, u32[]{:S(2)}, u32[]{:S(2)}) collective-permute-start(bf16[32,2560]{1,0:T(8,128)(2,1)S(1)} %get-tuple-element.63), channel_id=1, source_target_pairs={{0,32},{32,64},{64,96},{96,0},{1,33},{33,65},{65,97},{97,1},{2,34}... | collective-permute-start | bytes 491528 | tf_op jit(solution)/shard_map/ppermute | solution.py:54
  59.4 5.8 %collective-permute-start.9 = (bf16[32,2560]{1,0:T(8,128)(2,1)S(1)}, bf16[32,2560]{1,0:T(8,128)(2,1)S(1)}, u32[]{:S(2)}, u32[]{:S(2)}) collective-permute-start(bf16[32,2560]{1,0:T(8,128)(2,1)S(1)} %get-tuple-element.61), channel_id=1, source_target_pairs={{0,96},{32,0},{64,32},{96,64},{1,97},{33,1},{65,33},{97,65},{2,98}... | collective-permute-start | bytes 491528 | tf_op jit(solution)/shard_map/ppermute | solution.py:58
  62.0 9.9 %collective-permute-start.14 = (bf16[64,2560]{1,0:T(8,128)(2,1)S(1)}, bf16[64,2560]{1,0:T(8,128)(2,1)S(1)}, u32[]{:S(2)}, u32[]{:S(2)}) collective-permute-start(bf16[64,2560]{1,0:T(8,128)(2,1)S(1)} %get-tuple-element.65), channel_id=1, source_target_pairs={{0,32},{32,64},{64,96},{96,0},{1,33},{33,65},{65,97},{97,1},{2,34}... | collective-permute-start | bytes 983048 | tf_op jit(solution)/shard_map/ppermute | solution.py:54
  64.6 7.3 %collective-permute-start.12 = (bf16[64,2560]{1,0:T(8,128)(2,1)S(1)}, bf16[64,2560]{1,0:T(8,128)(2,1)S(1)}, u32[]{:S(2)}, u32[]{:S(2)}) collective-permute-start(bf16[64,2560]{1,0:T(8,128)(2,1)S(1)} %pad_maximum_fusion.4), channel_id=1, source_target_pairs={{0,128},{128,0},{1,129},{129,1},{2,130},{130,2},{3,131},{131,3},{4... | collective-permute-start | bytes 983048 | tf_op jit(solution)/shard_map/ppermute | solution.py:62
  65.2 7.4 %collective-permute-start.10 = (bf16[64,2560]{1,0:T(8,128)(2,1)S(1)}, bf16[64,2560]{1,0:T(8,128)(2,1)S(1)}, u32[]{:S(2)}, u32[]{:S(2)}) collective-permute-start(bf16[64,2560]{1,0:T(8,128)(2,1)S(1)} %pad_maximum_fusion.3), channel_id=1, source_target_pairs={{0,96},{32,0},{64,32},{96,64},{1,97},{33,1},{65,33},{97,65},{2,98}... | collective-permute-start | bytes 983048 | tf_op jit(solution)/shard_map/ppermute | solution.py:58
  72.9 9.6 %collective-permute-start.13 = (bf16[64,2560]{1,0:T(8,128)(2,1)S(1)}, bf16[64,2560]{1,0:T(8,128)(2,1)S(1)}, u32[]{:S(2)}, u32[]{:S(2)}) collective-permute-start(bf16[64,2560]{1,0:T(8,128)(2,1)S(1)} %pad_maximum_fusion.5), channel_id=1, source_target_pairs={{0,96},{32,0},{64,32},{96,64},{1,97},{33,1},{65,33},{97,65},{2,98}... | collective-permute-start | bytes 983048 | tf_op jit(solution)/shard_map/ppermute | solution.py:58
  75.5 7.2 %collective-permute-start.15 = (bf16[64,2560]{1,0:T(8,128)(2,1)S(1)}, bf16[64,2560]{1,0:T(8,128)(2,1)S(1)}, u32[]{:S(2)}, u32[]{:S(2)}) collective-permute-start(bf16[64,2560]{1,0:T(8,128)(2,1)S(1)} %pad_maximum_fusion.6), channel_id=1, source_target_pairs={{0,32},{32,64},{64,96},{96,0},{1,33},{33,65},{65,97},{97,1},{2,34}... | collective-permute-start | bytes 983048 | tf_op jit(solution)/shard_map/ppermute | solution.py:54
  75.6 7.1 %collective-permute-start.16 = (bf16[64,2560]{1,0:T(8,128)(2,1)S(1)}, bf16[64,2560]{1,0:T(8,128)(2,1)S(1)}, u32[]{:S(2)}, u32[]{:S(2)}) collective-permute-start(bf16[64,2560]{1,0:T(8,128)(2,1)S(1)} %pad_maximum_fusion.7), channel_id=1, source_target_pairs={{0,128},{128,0},{1,129},{129,1},{2,130},{130,2},{3,131},{131,3},{4... | collective-permute-start | bytes 983048 | tf_op jit(solution)/shard_map/ppermute | solution.py:62
  76.5 34.2 %copy-start.2 = (bf16[2,256,1280]{2,1,0:T(8,128)(2,1)S(1)}, bf16[2,256,1280]{2,1,0:T(8,128)(2,1)}, u32[]{:S(2)}) copy-start(bf16[2,256,1280]{2,1,0:T(8,128)(2,1)} %tokens.3) | copy-start | bytes 3932164
  76.5 34.2 %copy-start.3 = (bf16[2,256,1280]{2,1,0:T(8,128)(2,1)S(1)}, bf16[2,256,1280]{2,1,0:T(8,128)(2,1)}, u32[]{:S(2)}) copy-start(bf16[2,256,1280]{2,1,0:T(8,128)(2,1)} %cotangent.3) | copy-start | bytes 3932164
  82.9 10.8 %collective-permute-start.17 = (bf16[32,2560]{1,0:T(8,128)(2,1)S(1)}, bf16[32,2560]{1,0:T(8,128)(2,1)S(1)}, u32[]{:S(2)}, u32[]{:S(2)}) collective-permute-start(bf16[32,2560]{1,0:T(8,128)(2,1)S(1)} %get-tuple-element.79), channel_id=1, source_target_pairs={{0,1},{1,0},{2,3},{3,2},{4,5},{5,4},{6,7},{7,6},{8,9},{9,8},{10,11... | collective-permute-start | bytes 491528 | tf_op jit(solution)/shard_map/ppermute | solution.py:66
  94.7 15.9 %all-to-all-start.1 = ((bf16[16,8,1280]{2,1,0:T(8,128)(2,1)}), bf16[16,8,1280]{2,1,0:T(8,128)(2,1)S(1)}, u32[]{:S(2)}, u32[]{:S(2)}) async-start(bf16[16,8,1280]{2,1,0:T(8,128)(2,1)} %bitcast.7), calls=%async_computation.1 | async-start | bytes 655360 | tf_op jit(solution)/shard_map/all_to_all | solution.py:50
  114.3 11.7 %all-to-all-start.2 = ((bf16[16,2,1280]{2,1,0:T(2,128)(2,1)}), bf16[16,2,1280]{2,1,0:T(2,128)(2,1)S(1)}, u32[]{:S(2)}, u32[]{:S(2)}) async-start(bf16[16,2,1280]{2,1,0:T(2,128)(2,1)} %get-tuple-element.72), calls=%async_computation.2 | async-start | bytes 163840 | tf_op jit(solution)/shard_map/all_to_all | solution.py:50
  126.7 13.9 %all-to-all-start.3 = ((bf16[16,2,1280]{2,1,0:T(2,128)(2,1)}), bf16[16,2,1280]{2,1,0:T(2,128)(2,1)S(1)}, u32[]{:S(2)}, u32[]{:S(2)}) async-start(bf16[16,2,1280]{2,1,0:T(2,128)(2,1)} %broadcast_in_dim.8), calls=%async_computation.3 | async-start | bytes 163840 | tf_op jit(solution)/shard_map/all_to_all | solution.py:50
  141.4 11.0 %all-to-all-start.4 = ((bf16[16,2,1280]{2,1,0:T(2,128)(2,1)}), bf16[16,2,1280]{2,1,0:T(2,128)(2,1)S(1)}, u32[]{:S(2)}, u32[]{:S(2)}) async-start(bf16[16,2,1280]{2,1,0:T(2,128)(2,1)} %broadcast_in_dim.9), calls=%async_computation.4 | async-start | bytes 163840 | tf_op jit(solution)/shard_map/all_to_all | solution.py:50
  (14 other events, 122.3 us)

commit v3 on v2

--- a/solution.py
+++ b/solution.py
@@ -122,7 +122,7 @@
     )(core, tokens, router, cotangent)
 
 
-def experts_kernel(n, *refs):
+def experts_kernel(n, order, *refs):
     held, (w_in, w_out) = refs[:n], refs[n : n + 2]
     sent, (hidden, grad_preact) = refs[n + 2 : 2 * n + 2], refs[2 * n + 2 :]
     rows = jnp.concatenate([h[:, :D] for h in held], axis=0)
@@ -141,19 +141,21 @@
     inner = mm_nt(grad, w_in[...]).astype(BF16)
     first = 0
     for s in sent:
-        last = first + s.shape[0]
-        s[:, :D] = out[first:last]
-        s[:, D:] = inner[first:last]
-        first = last
-
-
-def experts(held, w_in, w_out):
+        for at in range(0, s.shape[0], 32):
+            block = order[first] * 32
+            s[at : at + 32, :D] = out[block : block + 32]
+            s[at : at + 32, D:] = inner[block : block + 32]
+            first += 1
+
+
+def experts(held, w_in, w_out, order=None):
     n = len(held)
     total = sum(h.shape[0] for h in held)
+    order = order or tuple(range(total // 32))
     shapes = [jax.ShapeDtypeStruct(h.shape, BF16) for h in held]
     shapes += [jax.ShapeDtypeStruct((total, HID), BF16)] * 2
     results = pl.pallas_call(
-        functools.partial(experts_kernel, n),
+        functools.partial(experts_kernel, n, order),
         in_specs=[VMEM] * (n + 2),
         out_specs=[VMEM] * (n + 2),
         out_shape=shapes,
@@ -182,9 +184,23 @@
     )(stay, go)
 
 
-def gate_kernel(core, message, tokens, cotangent, probs, slots, gates, term):
+def hold_kernel(probs, out):
+    out[...] = probs[...]
+
+
+def hold(probs):
+    return pl.pallas_call(
+        hold_kernel,
+        in_specs=[VMEM],
+        out_specs=VMEM,
+        out_shape=jax.ShapeDtypeStruct(probs.shape, F32),
+        compiler_params=PARAMS,
+        cost_estimate=cost(10**6, 10**6),
+    )(probs)
+
+
+def gate_kernel(core, message, tokens, cotangent, probs, gates, term):
     rows = from_message(core[0], message[...])
-    slots[...] = rows
     total = jnp.zeros((SLOTS, D), F32)
     for b in range(2):
         disp, comb = probs[b, 0], probs[b, 1]
@@ -204,9 +220,8 @@
     return pl.pallas_call(
         gate_kernel,
         in_specs=[SMEM] + [VMEM] * 4,
-        out_specs=[VMEM] * 3,
+        out_specs=[VMEM] * 2,
         out_shape=[
-            jax.ShapeDtypeStruct((128, D), BF16),
             jax.ShapeDtypeStruct((2, SLOTS, M), BF16),
             jax.ShapeDtypeStruct((16, 2, D), BF16),
         ],
@@ -215,32 +230,39 @@
     )(core, message, tokens, cotangent, probs)
 
 
-def spread_kernel(slots, gates, probs, router, output, grad_tokens):
-    first = pl.multiple_of(pl.program_id(0) * SLOTS, SLOTS)
-    slots_out = slots[pl.ds(first, SLOTS), :]
-    grad_slots_in = slots[pl.ds(64 + first, SLOTS), :]
+def spread_kernel(core, message, gates, probs, router, output, grad_tokens, rows):
+    image = pl.program_id(0)
+
+    @pl.when(image == 0)
+    def _():
+        rows[...] = from_message(core[0], message[...])
+
+    first = pl.multiple_of(image * SLOTS, SLOTS)
+    slots_out = rows[pl.ds(first, SLOTS), :]
+    grad_slots_in = rows[pl.ds(64 + first, SLOTS), :]
     output[0] = mm_tn(probs[0, 1].astype(BF16), slots_out).astype(BF16)
     grad = mm_tn(probs[0, 0].astype(BF16), grad_slots_in) + mm_tn(gates[0], router[...])
     grad_tokens[0] = grad.astype(BF16)
 
 
-def spread(slots, gates, probs, router):
+def spread(core, message, gates, probs, router):
     image = pl.BlockSpec((1, M, D), lambda b: (b, 0, 0))
-    shares = pl.BlockSpec((1, 2, SLOTS, M), lambda b: (b, 0, 0, 0))
     return pl.pallas_call(
         spread_kernel,
         grid=(2,),
         in_specs=[
+            SMEM,
             pl.BlockSpec((128, D), lambda b: (0, 0)),
             pl.BlockSpec((1, SLOTS, M), lambda b: (b, 0, 0)),
-            shares,
+            pl.BlockSpec((1, 2, SLOTS, M), lambda b: (b, 0, 0, 0)),
             pl.BlockSpec((SLOTS, D), lambda b: (0, 0)),
         ],
         out_specs=[image, image],
         out_shape=[jax.ShapeDtypeStruct((2, M, D), BF16)] * 2,
+        scratch_shapes=[pltpu.VMEM((128, D), BF16)],
         compiler_params=PARAMS,
         cost_estimate=cost(10**9, 3 * 10**6),
-    )(slots, gates, probs, router)
+    )(core, message, gates, probs, router)
 
 
 def low(a):
@@ -275,34 +297,39 @@
 
     down, up, side = x_up(own), x_down(own), y_swap(own)
     first = x_up(join(low(side), low(down)))
-    second = x_down(join(low(side), high(up)))
     third = y_swap(join(high(down), high(up)))
     near = experts((own, down, up, side), w_in, w_out)
-    first, third, near = lax.optimization_barrier((first, third, near))
+    late, near = lax.optimization_barrier((join(low(side), high(up)), near))
+    second = x_down(late)
     far_low = x_up(low(first))
     far_high = x_down(high(third))
-    middle = experts((first, second, third), w_in, w_out)
-    far_low, far_high, middle = lax.optimization_barrier((far_low, far_high, middle))
     far = experts((far_low, far_high), w_in, w_out)
+    first, far = lax.optimization_barrier((first, far))
+    middle = experts((first, second, third), w_in, w_out, (0, 1, 5, 3, 4, 2))
 
     (own_sum, down_sum, up_sum, side_sum), (first_sum, second_sum, third_sum) = near[0], middle[0]
     low_sum, high_sum = far[0]
-    low_in, high_in = x_down(low_sum), x_up(high_sum)
-    second_in = x_up(second_sum)
+    low_in, high_in, third_in = x_down(low_sum), x_up(high_sum), y_swap(third_sum)
     first_in = x_down(join(add(low(first_sum), low_in), high(first_sum)))
-    third_in = y_swap(join(low(third_sum), add(high(third_sum), high_in)))
-    side_in = y_swap(join(add(low(side_sum), low(first_in), low(second_in)), high(side_sum)))
+    second_in = x_up(join(add(low(second_sum), high_in), high(second_sum)))
     down_in = x_down(
         join(add(low(down_sum), high(first_in)), add(high(down_sum), low(third_in)))
     )
-    up_in = x_up(join(low(up_sum), add(high(up_sum), high(second_in), high(third_in))))
+    up_in = x_up(
+        join(add(low(up_sum), high(third_in)), add(high(up_sum), high(second_in)))
+    )
+    side_in = y_swap(
+        join(add(low(side_sum), low(first_in)), add(high(side_sum), low(second_in)))
+    )
     summed = add(own_sum, down_in, up_in, side_in)
 
     leaving = pack(low(summed), core_swap(high(summed)))
+    leaving, probs = lax.optimization_barrier((leaving, probs))
+    probs = hold(probs)
     returned = exchange(leaving.reshape(16, 8, D), COLUMN).reshape(128, D)
-    slots, gates, term = gate(core, returned, tokens, cotangent, probs)
+    gates, term = gate(core, returned, tokens, cotangent, probs)
     grad_router = sum_over_all(term)
-    output, grad_tokens = spread(slots, gates, probs, router)
+    output, grad_tokens = spread(core, returned, gates, probs, router)
 
     rows = jnp.concatenate([own, down, up, side, first, second, third, far_low, far_high])
     hidden = jnp.concatenate([near[1], middle[1], far[1]])

time: 154 us -> 149 us (0.968)
  local copies, waits for them, and re-layouts: 6.57 us -> 4.26 us
    ppermute x6, waiting for transfers between devices: 6.67 us -> 0.68 us  [x_down(): return lax.ppermute(a, 'x', [(i, (i + 3) % 4) for i in range(4)])]
    ppermute x4, waiting for transfers between devices: 0.01 us -> 4.89 us  [y_swap(): return lax.ppermute(a, 'yl', [(0, 1), (1, 0)])]
    ppermute x2, starting transfers between devices: 12.5 us -> 8.95 us  [core_swap(): return lax.ppermute(a, 'c', [(0, 1), (1, 0)])]
    unnamed x43 -> x41, local copies, waits for them, and re-layouts: 3.28 us -> 0.99 us
    ppermute x6, starting transfers between devices: 13.5 us -> 15.1 us  [x_down(): return lax.ppermute(a, 'x', [(i, (i + 3) % 4) for i in range(4)])]
    pallas_call x4 -> x5, Pallas kernels: 8.11 us -> 8.35 us  [the longest x3 5.82 us: experts(): pl.pallas_call(functools.partial(experts_kernel, n, order), in_specs=[VME...]
  transfers between devices with their start and end apart: 22 -> 22, of which waited for: 13 -> 15; matrix products, arithmetic and copies ran while one was open for 6% -> 6% of each run, Pallas kernels for 4% -> 6%
where the time goes in v3:
time: 149 us
  starting transfers between devices  51.2 us (34%)
  waiting for transfers between devices  45.4 us (30%)
  blocking collectives  23 us (15%)
  Pallas kernels  15.7 us (11%)
  matrix products  7.44 us (5%)
  local copies, waits for them, and re-layouts  4.26 us (3%)
    all_to_all x1, blocking collectives, exchange(): return lax.all_to_all(x, axes, split_axis=0, concat_axis=0, tiled=True)  23 us
    all_to_all x4, starting transfers between devices, exchange(): return lax.all_to_all(x, axes, split_axis=0, concat_axis=0, tiled=True)  22 us
    all_to_all x4, waiting for transfers between devices, exchange(): return lax.all_to_all(x, axes, split_axis=0, concat_axis=0, tiled=True)  20.6 us
    ppermute x6, waiting for transfers between devices, x_up(): return lax.ppermute(a, 'x', [(i, (i + 1) % 4) for i in range(4)])  17.2 us
    ppermute x6, starting transfers between devices, x_down(): return lax.ppermute(a, 'x', [(i, (i + 3) % 4) for i in range(4)])  15.1 us
    ppermute x2, starting transfers between devices, core_swap(): return lax.ppermute(a, 'c', [(0, 1), (1, 0)])  8.95 us
    dot_general x2, matrix products, mm_tn(): lax.dot_general(a, b, (((0,), (0,)), ((), ())), preferred_element_type=F32)  7.44 us
    pallas_call x3, Pallas kernels, experts(): pl.pallas_call(functools.partial(experts_kernel, n, order), in_specs=[VME...  5.82 us
  transfers between devices with their start and end apart: 22, of which 15 were waited for; matrix products, arithmetic and copies ran while one was open for 6% of the time, Pallas kernels for 6%

profile of v3, /device:TPU:1, one launch (start us, length us, event | category | flops | bytes accessed | tf_op | source)
XLA Modules:
  0.0 148.8 jit_solution(13474705327598692062)
XLA Ops:
  0.6 4.4 %shard_map.92 = (bf16[128,1280]{1,0:T(8,128)(2,1)}, f32[2,2,32,256]{3,2,1,0:T(8,128)}) custom-call(s32[1]{0:T(128)} %bitcast.core, bf16[2,256,1280]{2,1,0:T(8,128)(2,1)} %tokens.3, bf16[32,1280]{1,0:T(8,128)(2,1)} %router.3, bf16[2,256,1280]{2,1,0:T(8,128)(2,1)} %cotangent.3), custom_call_target="tpu_custom_call" | custom-call | flops 1000000000 | bytes 3000000 | tf_op jit(solution)/shard_map/pallas_call | solution.py:110
  5.0 23.0 %all_to_all.25 = bf16[16,8,1280]{2,1,0:T(8,128)(2,1)S(1)} all-to-all(bf16[16,8,1280]{2,1,0:T(8,128)(2,1)} %bitcast.31), channel_id=1, replica_groups=mesh['yl'=2,'x'=4,'yh'=2,'z'=8,'c'=2] {'yh','z'}, dimensions={0} | all-to-all | bytes 655360 | tf_op jit(solution)/shard_map/all_to_all | solution.py:50
  28.5 2.7 %collective-permute-start = (bf16[32,2560]{1,0:T(8,128)(2,1)S(1)}, bf16[32,2560]{1,0:T(8,128)(2,1)S(1)}, u32[]{:S(2)}, u32[]{:S(2)}) collective-permute-start(bf16[32,2560]{1,0:T(8,128)(2,1)S(1)} %bitcast.32), channel_id=1, source_target_pairs={{0,1},{1,0},{2,3},{3,2},{4,5},{5,4},{6,7},{7,6},{8,9},{9,8},{10,11... | collective-permute-start | bytes 491528 | tf_op jit(solution)/shard_map/ppermute | solution.py:66
  35.4 7.1 %collective-permute-done.3.refs_1_ = bf16[64,2560]{1,0:T(8,128)(2,1)S(1)} collective-permute-done((bf16[64,2560]{1,0:T(8,128)(2,1)S(1)}, bf16[64,2560]{1,0:T(8,128)(2,1)S(1)}, u32[]{:S(2)}, u32[]{:S(2)}) %collective-permute-start.3) | collective-permute-done | bytes 327712 | tf_op jit(solution)/shard_map/ppermute | solution.py:54
  46.3 2.7 %collective-permute-start.8 = (bf16[64,2560]{1,0:T(8,128)(2,1)S(1)}, bf16[64,2560]{1,0:T(8,128)(2,1)S(1)}, u32[]{:S(2)}, u32[]{:S(2)}) collective-permute-start(bf16[64,2560]{1,0:T(8,128)(2,1)S(1)} %get-tuple-element.54), channel_id=1, source_target_pairs={{0,96},{32,0},{64,32},{96,64},{1,97},{33,1},{65,33},{97,65},{2,98}... | collective-permute-start | bytes 983048 | tf_op jit(solution)/shard_map/ppermute | solution.py:58
  49.0 3.1 %collective-permute-done.4.refs_0_ = bf16[64,2560]{1,0:T(8,128)(2,1)S(1)} collective-permute-done((bf16[64,2560]{1,0:T(8,128)(2,1)S(1)}, bf16[64,2560]{1,0:T(8,128)(2,1)S(1)}, u32[]{:S(2)}, u32[]{:S(2)}) %collective-permute-start.4) | collective-permute-done | bytes 327712 | tf_op jit(solution)/shard_map/ppermute | solution.py:54
  52.2 2.7 %collective-permute-start.7 = (bf16[32,2560]{1,0:T(8,128)(2,1)S(1)}, bf16[32,2560]{1,0:T(8,128)(2,1)S(1)}, u32[]{:S(2)}, u32[]{:S(2)}) collective-permute-start(bf16[32,2560]{1,0:T(8,128)(2,1)S(1)} %slice.123), channel_id=1, source_target_pairs={{0,96},{32,0},{64,32},{96,64},{1,97},{33,1},{65,33},{97,65},{2,98}... | collective-permute-start | bytes 491528 | tf_op jit(solution)/shard_map/ppermute | solution.py:58
  55.0 2.6 %collective-permute-done.5.refs_0_ = bf16[32,2560]{1,0:T(8,128)(2,1)S(1)} collective-permute-done((bf16[32,2560]{1,0:T(8,128)(2,1)S(1)}, bf16[32,2560]{1,0:T(8,128)(2,1)S(1)}, u32[]{:S(2)}, u32[]{:S(2)}) %collective-permute-start.5) | collective-permute-done | bytes 163872 | tf_op jit(solution)/shard_map/ppermute | solution.py:54
  60.3 3.0 %collective-permute-start.9 = (bf16[32,2560]{1,0:T(8,128)(2,1)S(1)}, bf16[32,2560]{1,0:T(8,128)(2,1)S(1)}, u32[]{:S(2)}, u32[]{:S(2)}) collective-permute-start(bf16[32,2560]{1,0:T(8,128)(2,1)S(1)} %get-tuple-element.56), channel_id=1, source_target_pairs={{0,96},{32,0},{64,32},{96,64},{1,97},{33,1},{65,33},{97,65},{2,98}... | collective-permute-start | bytes 491528 | tf_op jit(solution)/shard_map/ppermute | solution.py:58
  67.0 2.7 %collective-permute-start.10 = (bf16[64,2560]{1,0:T(8,128)(2,1)S(1)}, bf16[64,2560]{1,0:T(8,128)(2,1)S(1)}, u32[]{:S(2)}, u32[]{:S(2)}) collective-permute-start(bf16[64,2560]{1,0:T(8,128)(2,1)S(1)} %pad_maximum_fusion.3), channel_id=1, source_target_pairs={{0,96},{32,0},{64,32},{96,64},{1,97},{33,1},{65,33},{97,65},{2,98}... | collective-permute-start | bytes 983048 | tf_op jit(solution)/shard_map/ppermute | solution.py:58
  71.4 2.6 %collective-permute-done.14 = bf16[64,2560]{1,0:T(8,128)(2,1)S(1)} collective-permute-done((bf16[64,2560]{1,0:T(8,128)(2,1)S(1)}, bf16[64,2560]{1,0:T(8,128)(2,1)S(1)}, u32[]{:S(2)}, u32[]{:S(2)}) %collective-permute-start.14) | collective-permute-done | bytes 327712 | tf_op jit(solution)/shard_map/ppermute | solution.py:54
  75.3 2.5 %collective-permute-start.12 = (bf16[64,2560]{1,0:T(8,128)(2,1)S(1)}, bf16[64,2560]{1,0:T(8,128)(2,1)S(1)}, u32[]{:S(2)}, u32[]{:S(2)}) collective-permute-start(bf16[64,2560]{1,0:T(8,128)(2,1)S(1)} %pad_maximum_fusion.4), channel_id=1, source_target_pairs={{0,96},{32,0},{64,32},{96,64},{1,97},{33,1},{65,33},{97,65},{2,98}... | collective-permute-start | bytes 983048 | tf_op jit(solution)/shard_map/ppermute | solution.py:58
  77.9 2.4 %collective-permute-done.16 = bf16[64,2560]{1,0:T(8,128)(2,1)S(1)} collective-permute-done((bf16[64,2560]{1,0:T(8,128)(2,1)S(1)}, bf16[64,2560]{1,0:T(8,128)(2,1)S(1)}, u32[]{:S(2)}, u32[]{:S(2)}) %collective-permute-start.16) | collective-permute-done | bytes 327712 | tf_op jit(solution)/shard_map/ppermute | solution.py:62
  82.4 6.3 %collective-permute-start.17 = (bf16[32,2560]{1,0:T(8,128)(2,1)S(1)}, bf16[32,2560]{1,0:T(8,128)(2,1)S(1)}, u32[]{:S(2)}, u32[]{:S(2)}) collective-permute-start(bf16[32,2560]{1,0:T(8,128)(2,1)S(1)} %get-tuple-element.75), channel_id=1, source_target_pairs={{0,1},{1,0},{2,3},{3,2},{4,5},{5,4},{6,7},{7,6},{8,9},{9,8},{10,11... | collective-permute-start | bytes 491528 | tf_op jit(solution)/shard_map/ppermute | solution.py:66
  90.6 4.6 %all-to-all-start.1 = ((bf16[16,8,1280]{2,1,0:T(8,128)(2,1)}), bf16[16,8,1280]{2,1,0:T(8,128)(2,1)S(1)}, u32[]{:S(2)}, u32[]{:S(2)}) async-start(bf16[16,8,1280]{2,1,0:T(8,128)(2,1)} %bitcast.7), calls=%async_computation.1 | async-start | bytes 655360 | tf_op jit(solution)/shard_map/all_to_all | solution.py:50
  96.6 10.0 %all-to-all-done.1 = bf16[16,8,1280]{2,1,0:T(8,128)(2,1)S(1)} async-done(((bf16[16,8,1280]{2,1,0:T(8,128)(2,1)}), bf16[16,8,1280]{2,1,0:T(8,128)(2,1)S(1)}, u32[]{:S(2)}, u32[]{:S(2)}) %all-to-all-start.1) | async-done | bytes 327712 | tf_op jit(solution)/shard_map/all_to_all | solution.py:50
  108.6 7.3 %all-to-all-start.2 = ((bf16[16,2,1280]{2,1,0:T(2,128)(2,1)}), bf16[16,2,1280]{2,1,0:T(2,128)(2,1)S(1)}, u32[]{:S(2)}, u32[]{:S(2)}) async-start(bf16[16,2,1280]{2,1,0:T(2,128)(2,1)} %get-tuple-element.68), calls=%async_computation.2 | async-start | bytes 163840 | tf_op jit(solution)/shard_map/all_to_all | solution.py:50
  115.9 3.9 %fusion = bf16[1,1280,640]{2,1,0:T(8,128)(2,1)} fusion(bf16[512,2560]{1,0:T(8,128)(2,1)} %constant_dynamic-update-slice_fusion.2, bf16[64,640]{1,0:T(8,128)(2,1)S(1)} %copy-done.7, bf16[192,640]{1,0:T(8,128)(2,1)} %copy-done.10, bf16[256,640]{1,0:T(8,128)(2,1)} %copy-done.13), kind=kOutput, calls=%fused_computation.2 | convolution fusion | flops 841646080 | bytes 3604480 | tf_op jit(solution)/shard_map/dot_general | solution.py:39
  122.5 5.0 %all-to-all-start.3 = ((bf16[16,2,1280]{2,1,0:T(2,128)(2,1)}), bf16[16,2,1280]{2,1,0:T(2,128)(2,1)S(1)}, u32[]{:S(2)}, u32[]{:S(2)}) async-start(bf16[16,2,1280]{2,1,0:T(2,128)(2,1)} %broadcast_in_dim.8), calls=%async_computation.3 | async-start | bytes 163840 | tf_op jit(solution)/shard_map/all_to_all | solution.py:50
  127.5 3.6 %fusion.1 = bf16[1,640,1280]{2,1,0:T(8,128)(2,1)} fusion(bf16[512,2560]{1,0:T(8,128)(2,1)} %constant_dynamic-update-slice_fusion.2, bf16[64,640]{1,0:T(8,128)(2,1)S(1)} %get-tuple-element.74, bf16[192,640]{1,0:T(8,128)(2,1)S(1)} %copy-done.9, bf16[256,640]{1,0:T(8,128)(2,1)S(1)} %copy-done.12), kind=kOutput, calls=%fused_computation.3 | convolution fusion | flops 841646080 | bytes 3604480 | tf_op jit(solution)/shard_map/dot_general | solution.py:39
  131.1 5.3 %all-to-all-done.3 = bf16[16,2,1280]{2,1,0:T(2,128)(2,1)S(1)} async-done(((bf16[16,2,1280]{2,1,0:T(2,128)(2,1)}), bf16[16,2,1280]{2,1,0:T(2,128)(2,1)S(1)}, u32[]{:S(2)}, u32[]{:S(2)}) %all-to-all-start.3) | async-done | bytes 81952 | tf_op jit(solution)/shard_map/all_to_all | solution.py:50
  137.1 5.1 %all-to-all-start.4 = ((bf16[16,2,1280]{2,1,0:T(2,128)(2,1)}), bf16[16,2,1280]{2,1,0:T(2,128)(2,1)S(1)}, u32[]{:S(2)}, u32[]{:S(2)}) async-start(bf16[16,2,1280]{2,1,0:T(2,128)(2,1)} %broadcast_in_dim.9), calls=%async_computation.4 | async-start | bytes 163840 | tf_op jit(solution)/shard_map/all_to_all | solution.py:50
  142.2 2.5 %shard_map.99 = (bf16[2,256,1280]{2,1,0:T(8,128)(2,1)}, bf16[2,256,1280]{2,1,0:T(8,128)(2,1)}) custom-call(s32[1]{0:T(128)} %bitcast.core, bf16[128,1280]{1,0:T(8,128)(2,1)S(1)} %bitcast.26, bf16[2,32,256]{2,1,0:T(8,128)(2,1)S(1)} %get-tuple-element.65.gates, f32[2,2,32,256]{3,2,1,0:T(8,128)S(1)} %shard_map.97.probs, bf16[32,1280]{1,0:T(8,128)(2,1)S(1)} %copy-done.5), custom_call_target="tpu_custom_call" | custom-call | flops 1000000000 | bytes 3000000 | tf_op jit(solution)/shard_map/pallas_call | solution.py:250
  144.8 3.4 %all-to-all-done.4 = bf16[16,2,1280]{2,1,0:T(2,128)(2,1)S(1)} async-done(((bf16[16,2,1280]{2,1,0:T(2,128)(2,1)}), bf16[16,2,1280]{2,1,0:T(2,128)(2,1)S(1)}, u32[]{:S(2)}, u32[]{:S(2)}) %all-to-all-start.4) | async-done | bytes 81952 | tf_op jit(solution)/shard_map/all_to_all | solution.py:50
  (100 shorter events, 29.4 us)
Async XLA Ops:
  28.5 3.7 %collective-permute-start = (bf16[32,2560]{1,0:T(8,128)(2,1)S(1)}, bf16[32,2560]{1,0:T(8,128)(2,1)S(1)}, u32[]{:S(2)}, u32[]{:S(2)}) collective-permute-start(bf16[32,2560]{1,0:T(8,128)(2,1)S(1)} %bitcast.32), channel_id=1, source_target_pairs={{0,1},{1,0},{2,3},{3,2},{4,5},{5,4},{6,7},{7,6},{8,9},{9,8},{10,11... | collective-permute-start | bytes 491528 | tf_op jit(solution)/shard_map/ppermute | solution.py:66
  32.3 10.2 %collective-permute-start.3 = (bf16[64,2560]{1,0:T(8,128)(2,1)S(1)}, bf16[64,2560]{1,0:T(8,128)(2,1)S(1)}, u32[]{:S(2)}, u32[]{:S(2)}) collective-permute-start(bf16[64,2560]{1,0:T(8,128)(2,1)S(1)} %get-tuple-element.88.refs_0_), channel_id=1, source_target_pairs={{0,32},{32,64},{64,96},{96,0},{1,33},{33,65},{65,97},{97,1},{2,34}... | collective-permute-start | bytes 983048 | tf_op jit(solution)/shard_map/ppermute | solution.py:54
  33.6 9.0 %collective-permute-start.2 = (bf16[64,2560]{1,0:T(8,128)(2,1)S(1)}, bf16[64,2560]{1,0:T(8,128)(2,1)S(1)}, u32[]{:S(2)}, u32[]{:S(2)}) collective-permute-start(bf16[64,2560]{1,0:T(8,128)(2,1)S(1)} %get-tuple-element.88.refs_0_), channel_id=1, source_target_pairs={{0,96},{32,0},{64,32},{96,64},{1,97},{33,1},{65,33},{97,65},{2,98}... | collective-permute-start | bytes 983048 | tf_op jit(solution)/shard_map/ppermute | solution.py:58
  35.1 8.3 %collective-permute-start.1 = (bf16[64,2560]{1,0:T(8,128)(2,1)S(1)}, bf16[64,2560]{1,0:T(8,128)(2,1)S(1)}, u32[]{:S(2)}, u32[]{:S(2)}) collective-permute-start(bf16[64,2560]{1,0:T(8,128)(2,1)S(1)} %get-tuple-element.88.refs_0_), channel_id=1, source_target_pairs={{0,128},{128,0},{1,129},{129,1},{2,130},{130,2},{3,131},{131,3},{4... | collective-permute-start | bytes 983048 | tf_op jit(solution)/shard_map/ppermute | solution.py:62
  43.4 8.7 %collective-permute-start.4 = (bf16[64,2560]{1,0:T(8,128)(2,1)S(1)}, bf16[64,2560]{1,0:T(8,128)(2,1)S(1)}, u32[]{:S(2)}, u32[]{:S(2)}) collective-permute-start(bf16[64,2560]{1,0:T(8,128)(2,1)S(1)} %get-tuple-element.92), channel_id=1, source_target_pairs={{0,32},{32,64},{64,96},{96,0},{1,33},{33,65},{65,97},{97,1},{2,34}... | collective-permute-start | bytes 983048 | tf_op jit(solution)/shard_map/ppermute | solution.py:54
  43.6 8.6 %collective-permute-start.6 = (bf16[64,2560]{1,0:T(8,128)(2,1)S(1)}, bf16[64,2560]{1,0:T(8,128)(2,1)S(1)}, u32[]{:S(2)}, u32[]{:S(2)}) collective-permute-start(bf16[64,2560]{1,0:T(8,128)(2,1)S(1)} %get-tuple-element.93), channel_id=1, source_target_pairs={{0,128},{128,0},{1,129},{129,1},{2,130},{130,2},{3,131},{131,3},{4... | collective-permute-start | bytes 983048 | tf_op jit(solution)/shard_map/ppermute | solution.py:62
  46.3 17.0 %collective-permute-start.8 = (bf16[64,2560]{1,0:T(8,128)(2,1)S(1)}, bf16[64,2560]{1,0:T(8,128)(2,1)S(1)}, u32[]{:S(2)}, u32[]{:S(2)}) collective-permute-start(bf16[64,2560]{1,0:T(8,128)(2,1)S(1)} %get-tuple-element.54), channel_id=1, source_target_pairs={{0,96},{32,0},{64,32},{96,64},{1,97},{33,1},{65,33},{97,65},{2,98}... | collective-permute-start | bytes 983048 | tf_op jit(solution)/shard_map/ppermute | solution.py:58
  52.1 5.5 %collective-permute-start.5 = (bf16[32,2560]{1,0:T(8,128)(2,1)S(1)}, bf16[32,2560]{1,0:T(8,128)(2,1)S(1)}, u32[]{:S(2)}, u32[]{:S(2)}) collective-permute-start(bf16[32,2560]{1,0:T(8,128)(2,1)S(1)} %slice.121), channel_id=1, source_target_pairs={{0,32},{32,64},{64,96},{96,0},{1,33},{33,65},{65,97},{97,1},{2,34}... | collective-permute-start | bytes 491528 | tf_op jit(solution)/shard_map/ppermute | solution.py:54
  52.2 6.0 %collective-permute-start.7 = (bf16[32,2560]{1,0:T(8,128)(2,1)S(1)}, bf16[32,2560]{1,0:T(8,128)(2,1)S(1)}, u32[]{:S(2)}, u32[]{:S(2)}) collective-permute-start(bf16[32,2560]{1,0:T(8,128)(2,1)S(1)} %slice.123), channel_id=1, source_target_pairs={{0,96},{32,0},{64,32},{96,64},{1,97},{33,1},{65,33},{97,65},{2,98}... | collective-permute-start | bytes 491528 | tf_op jit(solution)/shard_map/ppermute | solution.py:58
  59.9 6.9 %collective-permute-start.13 = (bf16[32,2560]{1,0:T(8,128)(2,1)S(1)}, bf16[32,2560]{1,0:T(8,128)(2,1)S(1)}, u32[]{:S(2)}, u32[]{:S(2)}) collective-permute-start(bf16[32,2560]{1,0:T(8,128)(2,1)S(1)} %get-tuple-element.60), channel_id=1, source_target_pairs={{0,32},{32,64},{64,96},{96,0},{1,33},{33,65},{65,97},{97,1},{2,34}... | collective-permute-start | bytes 491528 | tf_op jit(solution)/shard_map/ppermute | solution.py:54
  60.3 6.6 %collective-permute-start.9 = (bf16[32,2560]{1,0:T(8,128)(2,1)S(1)}, bf16[32,2560]{1,0:T(8,128)(2,1)S(1)}, u32[]{:S(2)}, u32[]{:S(2)}) collective-permute-start(bf16[32,2560]{1,0:T(8,128)(2,1)S(1)} %get-tuple-element.56), channel_id=1, source_target_pairs={{0,96},{32,0},{64,32},{96,64},{1,97},{33,1},{65,33},{97,65},{2,98}... | collective-permute-start | bytes 491528 | tf_op jit(solution)/shard_map/ppermute | solution.py:58
  65.4 6.0 %collective-permute-start.11 = (bf16[64,2560]{1,0:T(8,128)(2,1)S(1)}, bf16[64,2560]{1,0:T(8,128)(2,1)S(1)}, u32[]{:S(2)}, u32[]{:S(2)}) collective-permute-start(bf16[64,2560]{1,0:T(8,128)(2,1)S(1)} %get-tuple-element.57), channel_id=1, source_target_pairs={{0,128},{128,0},{1,129},{129,1},{2,130},{130,2},{3,131},{131,3},{4... | collective-permute-start | bytes 983048 | tf_op jit(solution)/shard_map/ppermute | solution.py:62
  66.8 7.2 %collective-permute-start.14 = (bf16[64,2560]{1,0:T(8,128)(2,1)S(1)}, bf16[64,2560]{1,0:T(8,128)(2,1)S(1)}, u32[]{:S(2)}, u32[]{:S(2)}) collective-permute-start(bf16[64,2560]{1,0:T(8,128)(2,1)S(1)} %pad_maximum_fusion.5), channel_id=1, source_target_pairs={{0,32},{32,64},{64,96},{96,0},{1,33},{33,65},{65,97},{97,1},{2,34}... | collective-permute-start | bytes 983048 | tf_op jit(solution)/shard_map/ppermute | solution.py:54
  67.0 7.0 %collective-permute-start.10 = (bf16[64,2560]{1,0:T(8,128)(2,1)S(1)}, bf16[64,2560]{1,0:T(8,128)(2,1)S(1)}, u32[]{:S(2)}, u32[]{:S(2)}) collective-permute-start(bf16[64,2560]{1,0:T(8,128)(2,1)S(1)} %pad_maximum_fusion.3), channel_id=1, source_target_pairs={{0,96},{32,0},{64,32},{96,64},{1,97},{33,1},{65,33},{97,65},{2,98}... | collective-permute-start | bytes 983048 | tf_op jit(solution)/shard_map/ppermute | solution.py:58
  74.3 6.0 %collective-permute-start.16 = (bf16[64,2560]{1,0:T(8,128)(2,1)S(1)}, bf16[64,2560]{1,0:T(8,128)(2,1)S(1)}, u32[]{:S(2)}, u32[]{:S(2)}) collective-permute-start(bf16[64,2560]{1,0:T(8,128)(2,1)S(1)} %pad_maximum_fusion.7), channel_id=1, source_target_pairs={{0,128},{128,0},{1,129},{129,1},{2,130},{130,2},{3,131},{131,3},{4... | collective-permute-start | bytes 983048 | tf_op jit(solution)/shard_map/ppermute | solution.py:62
  74.7 7.5 %collective-permute-start.15 = (bf16[64,2560]{1,0:T(8,128)(2,1)S(1)}, bf16[64,2560]{1,0:T(8,128)(2,1)S(1)}, u32[]{:S(2)}, u32[]{:S(2)}) collective-permute-start(bf16[64,2560]{1,0:T(8,128)(2,1)S(1)} %pad_maximum_fusion.6), channel_id=1, source_target_pairs={{0,32},{32,64},{64,96},{96,0},{1,33},{33,65},{65,97},{97,1},{2,34}... | collective-permute-start | bytes 983048 | tf_op jit(solution)/shard_map/ppermute | solution.py:54
  75.3 6.9 %collective-permute-start.12 = (bf16[64,2560]{1,0:T(8,128)(2,1)S(1)}, bf16[64,2560]{1,0:T(8,128)(2,1)S(1)}, u32[]{:S(2)}, u32[]{:S(2)}) collective-permute-start(bf16[64,2560]{1,0:T(8,128)(2,1)S(1)} %pad_maximum_fusion.4), channel_id=1, source_target_pairs={{0,96},{32,0},{64,32},{96,64},{1,97},{33,1},{65,33},{97,65},{2,98}... | collective-permute-start | bytes 983048 | tf_op jit(solution)/shard_map/ppermute | solution.py:58
  77.9 28.8 %copy-start.3 = (bf16[2,256,1280]{2,1,0:T(8,128)(2,1)S(1)}, bf16[2,256,1280]{2,1,0:T(8,128)(2,1)}, u32[]{:S(2)}) copy-start(bf16[2,256,1280]{2,1,0:T(8,128)(2,1)} %tokens.3) | copy-start | bytes 3932164
  77.9 28.7 %copy-start.4 = (bf16[2,256,1280]{2,1,0:T(8,128)(2,1)S(1)}, bf16[2,256,1280]{2,1,0:T(8,128)(2,1)}, u32[]{:S(2)}) copy-start(bf16[2,256,1280]{2,1,0:T(8,128)(2,1)} %cotangent.3) | copy-start | bytes 3932164
  82.4 7.3 %collective-permute-start.17 = (bf16[32,2560]{1,0:T(8,128)(2,1)S(1)}, bf16[32,2560]{1,0:T(8,128)(2,1)S(1)}, u32[]{:S(2)}, u32[]{:S(2)}) collective-permute-start(bf16[32,2560]{1,0:T(8,128)(2,1)S(1)} %get-tuple-element.75), channel_id=1, source_target_pairs={{0,1},{1,0},{2,3},{3,2},{4,5},{5,4},{6,7},{7,6},{8,9},{9,8},{10,11... | collective-permute-start | bytes 491528 | tf_op jit(solution)/shard_map/ppermute | solution.py:66
  90.6 16.0 %all-to-all-start.1 = ((bf16[16,8,1280]{2,1,0:T(8,128)(2,1)}), bf16[16,8,1280]{2,1,0:T(8,128)(2,1)S(1)}, u32[]{:S(2)}, u32[]{:S(2)}) async-start(bf16[16,8,1280]{2,1,0:T(8,128)(2,1)} %bitcast.7), calls=%async_computation.1 | async-start | bytes 655360 | tf_op jit(solution)/shard_map/all_to_all | solution.py:50
  108.6 13.1 %all-to-all-start.2 = ((bf16[16,2,1280]{2,1,0:T(2,128)(2,1)}), bf16[16,2,1280]{2,1,0:T(2,128)(2,1)S(1)}, u32[]{:S(2)}, u32[]{:S(2)}) async-start(bf16[16,2,1280]{2,1,0:T(2,128)(2,1)} %get-tuple-element.68), calls=%async_computation.2 | async-start | bytes 163840 | tf_op jit(solution)/shard_map/all_to_all | solution.py:50
  122.5 13.9 %all-to-all-start.3 = ((bf16[16,2,1280]{2,1,0:T(2,128)(2,1)}), bf16[16,2,1280]{2,1,0:T(2,128)(2,1)S(1)}, u32[]{:S(2)}, u32[]{:S(2)}) async-start(bf16[16,2,1280]{2,1,0:T(2,128)(2,1)} %broadcast_in_dim.8), calls=%async_computation.3 | async-start | bytes 163840 | tf_op jit(solution)/shard_map/all_to_all | solution.py:50
  137.1 11.0 %all-to-all-start.4 = ((bf16[16,2,1280]{2,1,0:T(2,128)(2,1)}), bf16[16,2,1280]{2,1,0:T(2,128)(2,1)S(1)}, u32[]{:S(2)}, u32[]{:S(2)}) async-start(bf16[16,2,1280]{2,1,0:T(2,128)(2,1)} %broadcast_in_dim.9), calls=%async_computation.4 | async-start | bytes 163840 | tf_op jit(solution)/shard_map/all_to_all | solution.py:50
  (13 other events, 155.9 us)

commit v4 on v3

--- a/solution.py
+++ b/solution.py
@@ -165,6 +165,31 @@
     return results[:n], results[n], results[n + 1]
 
 
+def grads_kernel(n, m, *refs):
+    pieces, acts, (grad_in, grad_out) = refs[:n], refs[n : n + 2 * m], refs[n + 2 * m :]
+    rows = jnp.concatenate([p[:, :D] for p in pieces], axis=0)
+    grad_preact = jnp.concatenate([a[...] for a in acts[m:]], axis=0)
+    grad_in[...] = mm_tn(rows, grad_preact).astype(BF16)
+    hidden = jnp.concatenate([a[...] for a in acts[:m]], axis=0)
+    grad_rows = jnp.concatenate([p[:, D:] for p in pieces], axis=0)
+    grad_out[...] = mm_tn(hidden, grad_rows).astype(BF16)
+
+
+def weight_grads(pieces, hidden, grad_preact):
+    n, m = len(pieces), len(hidden)
+    return pl.pallas_call(
+        functools.partial(grads_kernel, n, m),
+        in_specs=[VMEM] * (n + 2 * m),
+        out_specs=[VMEM] * 2,
+        out_shape=[
+            jax.ShapeDtypeStruct((D, HID), BF16),
+            jax.ShapeDtypeStruct((HID, D), BF16),
+        ],
+        compiler_params=PARAMS,
+        cost_estimate=cost(4 * 512 * D * HID, 8 * 10**6),
+    )(*pieces, *hidden, *grad_preact)
+
+
 def pack_kernel(stay, go, message):
     rows = jnp.concatenate([stay[:, :D], stay[:, D:], go[:, :D], go[:, D:]], axis=0)
     r = lax.broadcasted_iota(jnp.int32, (128, 128), 0)
@@ -197,6 +222,22 @@
         compiler_params=PARAMS,
         cost_estimate=cost(10**6, 10**6),
     )(probs)
+
+
+def hold_inputs_kernel(tokens, cotangent, tokens_out, cotangent_out):
+    tokens_out[...] = tokens[...]
+    cotangent_out[...] = cotangent[...]
+
+
+def hold_inputs(tokens, cotangent):
+    return pl.pallas_call(
+        hold_inputs_kernel,
+        in_specs=[VMEM] * 2,
+        out_specs=[VMEM] * 2,
+        out_shape=[jax.ShapeDtypeStruct((2, M, D), BF16)] * 2,
+        compiler_params=PARAMS,
+        cost_estimate=cost(10**6, 5 * 10**6),
+    )(tokens, cotangent)
 
 
 def gate_kernel(core, message, tokens, cotangent, probs, gates, term):
@@ -324,18 +365,19 @@
     summed = add(own_sum, down_in, up_in, side_in)
 
     leaving = pack(low(summed), core_swap(high(summed)))
-    leaving, probs = lax.optimization_barrier((leaving, probs))
+    pieces = (own, down, up, side, far_low, far_high, first, second, third)
+    acts = [(call[1], call[2]) for call in (near, far, middle)]
+    leaving, probs, pieces, acts = lax.optimization_barrier((leaving, probs, pieces, acts))
     probs = hold(probs)
+    grad_in, grad_out = weight_grads(pieces, [a[0] for a in acts], [a[1] for a in acts])
     returned = exchange(leaving.reshape(16, 8, D), COLUMN).reshape(128, D)
-    gates, term = gate(core, returned, tokens, cotangent, probs)
+    near_by = lax.optimization_barrier((tokens, cotangent, grad_in))
+    near_by = hold_inputs(near_by[0], near_by[1])
+    returned, near_by, grad_in = lax.optimization_barrier((returned, near_by, grad_in))
+    gates, term = gate(core, returned, near_by[0], near_by[1], probs)
     grad_router = sum_over_all(term)
     output, grad_tokens = spread(core, returned, gates, probs, router)
 
-    rows = jnp.concatenate([own, down, up, side, first, second, third, far_low, far_high])
-    hidden = jnp.concatenate([near[1], middle[1], far[1]])
-    grad_preact = jnp.concatenate([near[2], middle[2], far[2]])
-    grad_in = mm_tn(rows[:, :D], grad_preact).astype(BF16)
-    grad_out = mm_tn(hidden, rows[:, D:]).astype(BF16)
     return (output, grad_tokens, grad_router, grad_in[None], grad_out[None])
 
 

time: 149 us -> 148 us (level)
  blocking collectives: 23 us -> 49.6 us
  starting transfers between devices: 51.2 us -> 38.4 us
  waiting for transfers between devices: 45.4 us -> 33.2 us
  matrix products: 7.44 us -> 0 us
  Pallas kernels: 15.7 us -> 18.6 us
    all_to_all x1 -> x3, blocking collectives: 23 us -> 49.6 us  [exchange(): return lax.all_to_all(x, axes, split_axis=0, concat_axis=0, tiled=True)]
    all_to_all x4 -> x2, waiting for transfers between devices: 20.6 us -> 8.25 us  [exchange(): return lax.all_to_all(x, axes, split_axis=0, concat_axis=0, tiled=True)]
    all_to_all x4 -> x2, starting transfers between devices: 22 us -> 9.78 us  [exchange(): return lax.all_to_all(x, axes, split_axis=0, concat_axis=0, tiled=True)]
    dot_general x2 -> x0, matrix products: 7.44 us -> none  [mm_tn(): lax.dot_general(a, b, (((0,), (0,)), ((), ())), preferred_element_type=F32)]
    pallas_call x0 -> x2, Pallas kernels: none -> 3.58 us  [the longest x1 3.41 us: weight_grads(): pl.pallas_call(functools.partial(grads_kernel, n, m), in_specs=[VMEM] * (...]
    unnamed x41 -> x27, local copies, waits for them, and re-layouts: 0.99 us -> 3.69 us
  transfers between devices with their start and end apart: 22 -> 20, of which waited for: 15 -> 13; matrix products, arithmetic and copies ran while one was open for 6% -> 0% of each run, Pallas kernels for 6% -> 8%
where the time goes in v4:
time: 148 us; the launch traced here: 147 us
  blocking collectives  49.6 us (34%)
  starting transfers between devices  38.4 us (26%)
  waiting for transfers between devices  33.2 us (22%)
  Pallas kernels  18.6 us (13%)
  local copies, waits for them, and re-layouts  5.66 us (4%)
    all_to_all x3, blocking collectives, exchange(): return lax.all_to_all(x, axes, split_axis=0, concat_axis=0, tiled=True)  49.6 us
    ppermute x6, waiting for transfers between devices, x_up(): return lax.ppermute(a, 'x', [(i, (i + 1) % 4) for i in range(4)])  15.9 us
    ppermute x6, starting transfers between devices, x_down(): return lax.ppermute(a, 'x', [(i, (i + 3) % 4) for i in range(4)])  15.8 us
    all_to_all x2, starting transfers between devices, exchange(): return lax.all_to_all(x, axes, split_axis=0, concat_axis=0, tiled=True)  9.78 us
    ppermute x2, starting transfers between devices, core_swap(): return lax.ppermute(a, 'c', [(0, 1), (1, 0)])  8.56 us
    all_to_all x2, waiting for transfers between devices, exchange(): return lax.all_to_all(x, axes, split_axis=0, concat_axis=0, tiled=True)  8.25 us
    pallas_call x3, Pallas kernels, experts(): pl.pallas_call(functools.partial(experts_kernel, n, order), in_specs=[VME...  5.82 us
    ppermute x4, waiting for transfers between devices, y_swap(): return lax.ppermute(a, 'yl', [(0, 1), (1, 0)])  5.64 us
  transfers between devices with their start and end apart: 20, of which 13 were waited for; matrix products, arithmetic and copies ran while one was open for 0% of the time, Pallas kernels for 8%

profile of v4, /device:TPU:1, one launch (start us, length us, event | category | flops | bytes accessed | tf_op | source)
XLA Modules:
  0.0 147.3 jit_solution(4627763379592461258)
XLA Ops:
  0.6 4.4 %shard_map.92 = (bf16[128,1280]{1,0:T(8,128)(2,1)}, f32[2,2,32,256]{3,2,1,0:T(8,128)}) custom-call(s32[1]{0:T(128)} %bitcast.core, bf16[2,256,1280]{2,1,0:T(8,128)(2,1)} %tokens.2, bf16[32,1280]{1,0:T(8,128)(2,1)} %router.3, bf16[2,256,1280]{2,1,0:T(8,128)(2,1)} %cotangent.2), custom_call_target="tpu_custom_call" | custom-call | flops 1000000000 | bytes 3000000 | tf_op jit(solution)/shard_map/pallas_call | solution.py:110
  5.0 23.0 %all_to_all.25 = bf16[16,8,1280]{2,1,0:T(8,128)(2,1)S(1)} all-to-all(bf16[16,8,1280]{2,1,0:T(8,128)(2,1)} %bitcast.29), channel_id=1, replica_groups=mesh['yl'=2,'x'=4,'yh'=2,'z'=8,'c'=2] {'yh','z'}, dimensions={0} | all-to-all | bytes 655360 | tf_op jit(solution)/shard_map/all_to_all | solution.py:50
  28.5 2.7 %collective-permute-start = (bf16[32,2560]{1,0:T(8,128)(2,1)S(1)}, bf16[32,2560]{1,0:T(8,128)(2,1)S(1)}, u32[]{:S(2)}, u32[]{:S(2)}) collective-permute-start(bf16[32,2560]{1,0:T(8,128)(2,1)S(1)} %bitcast.30), channel_id=1, source_target_pairs={{0,1},{1,0},{2,3},{3,2},{4,5},{5,4},{6,7},{7,6},{8,9},{9,8},{10,11... | collective-permute-start | bytes 491528 | tf_op jit(solution)/shard_map/ppermute | solution.py:66
  35.4 7.1 %collective-permute-done.3.refs_1_ = bf16[64,2560]{1,0:T(8,128)(2,1)S(1)} collective-permute-done((bf16[64,2560]{1,0:T(8,128)(2,1)S(1)}, bf16[64,2560]{1,0:T(8,128)(2,1)S(1)}, u32[]{:S(2)}, u32[]{:S(2)}) %collective-permute-start.3) | collective-permute-done | bytes 327712 | tf_op jit(solution)/shard_map/ppermute | solution.py:54
  44.0 2.2 %shard_map.93 = (bf16[64,2560]{1,0:T(8,128)(2,1)S(1)}, bf16[64,2560]{1,0:T(8,128)(2,1)S(1)}, bf16[64,2560]{1,0:T(8,128)(2,1)S(1)}, bf16[64,2560]{1,0:T(8,128)(2,...) custom-call(bf16[64,2560]{1,0:T(8,128)(2,1)S(1)} %constant_dynamic-update-slice_fusion.refs_0_, ...), custom_call_target="tpu_custom_call" | custom-call | flops 1677721600 | bytes 4000000 | tf_op jit(solution)/shard_map/pallas_call | solution.py:157
  47.0 2.6 %collective-permute-start.8 = (bf16[64,2560]{1,0:T(8,128)(2,1)S(1)}, bf16[64,2560]{1,0:T(8,128)(2,1)S(1)}, u32[]{:S(2)}, u32[]{:S(2)}) collective-permute-start(bf16[64,2560]{1,0:T(8,128)(2,1)S(1)} %get-tuple-element.79), channel_id=1, source_target_pairs={{0,96},{32,0},{64,32},{96,64},{1,97},{33,1},{65,33},{97,65},{2,98}... | collective-permute-start | bytes 983048 | tf_op jit(solution)/shard_map/ppermute | solution.py:58
  49.6 2.5 %collective-permute-done.4.refs_0_.refs_6_ = bf16[64,2560]{1,0:T(8,128)(2,1)S(1)} collective-permute-done((bf16[64,2560]{1,0:T(8,128)(2,1)S(1)}, bf16[64,2560]{1,0:T(8,128)(2,1)S(1)}, u32[]{:S(2)}, u32[]{:S(2)}) %collective-permute-start.4) | collective-permute-done | bytes 327712 | tf_op jit(solution)/shard_map/ppermute | solution.py:54
  52.2 2.7 %collective-permute-start.7 = (bf16[32,2560]{1,0:T(8,128)(2,1)S(1)}, bf16[32,2560]{1,0:T(8,128)(2,1)S(1)}, u32[]{:S(2)}, u32[]{:S(2)}) collective-permute-start(bf16[32,2560]{1,0:T(8,128)(2,1)S(1)} %slice.115), channel_id=1, source_target_pairs={{0,96},{32,0},{64,32},{96,64},{1,97},{33,1},{65,33},{97,65},{2,98}... | collective-permute-start | bytes 491528 | tf_op jit(solution)/shard_map/ppermute | solution.py:58
  54.9 2.6 %collective-permute-done.5.refs_0_.refs_4_ = bf16[32,2560]{1,0:T(8,128)(2,1)S(1)} collective-permute-done((bf16[32,2560]{1,0:T(8,128)(2,1)S(1)}, bf16[32,2560]{1,0:T(8,128)(2,1)S(1)}, u32[]{:S(2)}, u32[]{:S(2)}) %collective-permute-start.5) | collective-permute-done | bytes 163872 | tf_op jit(solution)/shard_map/ppermute | solution.py:54
  60.6 3.4 %collective-permute-start.9 = (bf16[32,2560]{1,0:T(8,128)(2,1)S(1)}, bf16[32,2560]{1,0:T(8,128)(2,1)S(1)}, u32[]{:S(2)}, u32[]{:S(2)}) collective-permute-start(bf16[32,2560]{1,0:T(8,128)(2,1)S(1)} %get-tuple-element.81), channel_id=1, source_target_pairs={{0,96},{32,0},{64,32},{96,64},{1,97},{33,1},{65,33},{97,65},{2,98}... | collective-permute-start | bytes 491528 | tf_op jit(solution)/shard_map/ppermute | solution.py:58
  67.2 2.7 %collective-permute-start.10 = (bf16[64,2560]{1,0:T(8,128)(2,1)S(1)}, bf16[64,2560]{1,0:T(8,128)(2,1)S(1)}, u32[]{:S(2)}, u32[]{:S(2)}) collective-permute-start(bf16[64,2560]{1,0:T(8,128)(2,1)S(1)} %pad_maximum_fusion.3), channel_id=1, source_target_pairs={{0,96},{32,0},{64,32},{96,64},{1,97},{33,1},{65,33},{97,65},{2,98}... | collective-permute-start | bytes 983048 | tf_op jit(solution)/shard_map/ppermute | solution.py:58
  69.9 2.7 %collective-permute-done.11 = bf16[64,2560]{1,0:T(8,128)(2,1)S(1)} collective-permute-done((bf16[64,2560]{1,0:T(8,128)(2,1)S(1)}, bf16[64,2560]{1,0:T(8,128)(2,1)S(1)}, u32[]{:S(2)}, u32[]{:S(2)}) %collective-permute-start.11) | collective-permute-done | bytes 327712 | tf_op jit(solution)/shard_map/ppermute | solution.py:62
  75.4 2.9 %collective-permute-start.12 = (bf16[64,2560]{1,0:T(8,128)(2,1)S(1)}, bf16[64,2560]{1,0:T(8,128)(2,1)S(1)}, u32[]{:S(2)}, u32[]{:S(2)}) collective-permute-start(bf16[64,2560]{1,0:T(8,128)(2,1)S(1)} %pad_maximum_fusion.4), channel_id=1, source_target_pairs={{0,96},{32,0},{64,32},{96,64},{1,97},{33,1},{65,33},{97,65},{2,98}... | collective-permute-start | bytes 983048 | tf_op jit(solution)/shard_map/ppermute | solution.py:58
  78.3 2.2 %collective-permute-done.16 = bf16[64,2560]{1,0:T(8,128)(2,1)S(1)} collective-permute-done((bf16[64,2560]{1,0:T(8,128)(2,1)S(1)}, bf16[64,2560]{1,0:T(8,128)(2,1)S(1)}, u32[]{:S(2)}, u32[]{:S(2)}) %collective-permute-start.16) | collective-permute-done | bytes 327712 | tf_op jit(solution)/shard_map/ppermute | solution.py:62
  80.5 2.2 %collective-permute-done.15 = bf16[64,2560]{1,0:T(8,128)(2,1)S(1)} collective-permute-done((bf16[64,2560]{1,0:T(8,128)(2,1)S(1)}, bf16[64,2560]{1,0:T(8,128)(2,1)S(1)}, u32[]{:S(2)}, u32[]{:S(2)}) %collective-permute-start.15) | collective-permute-done | bytes 327712 | tf_op jit(solution)/shard_map/ppermute | solution.py:54
  82.9 5.9 %collective-permute-start.17 = (bf16[32,2560]{1,0:T(8,128)(2,1)S(1)}, bf16[32,2560]{1,0:T(8,128)(2,1)S(1)}, u32[]{:S(2)}, u32[]{:S(2)}) collective-permute-start(bf16[32,2560]{1,0:T(8,128)(2,1)S(1)} %get-tuple-element.125), channel_id=1, source_target_pairs={{0,1},{1,0},{2,3},{3,2},{4,5},{5,4},{6,7},{7,6},{8,9},{9,8},{10,11... | collective-permute-start | bytes 491528 | tf_op jit(solution)/shard_map/ppermute | solution.py:66
  90.7 4.7 %all-to-all-start.1 = ((bf16[16,8,1280]{2,1,0:T(8,128)(2,1)}), bf16[16,8,1280]{2,1,0:T(8,128)(2,1)S(1)}, u32[]{:S(2)}, u32[]{:S(2)}) async-start(bf16[16,8,1280]{2,1,0:T(8,128)(2,1)} %bitcast.7), calls=%async_computation.1 | async-start | bytes 655360 | tf_op jit(solution)/shard_map/all_to_all | solution.py:50
  98.3 3.4 %shard_map.97 = (bf16[1280,640]{1,0:T(8,128)(2,1)}, bf16[640,1280]{1,0:T(8,128)(2,1)}) custom-call(bf16[64,2560]{1,0:T(8,128)(2,1)S(1)} %constant_dynamic-update-slice_fusion.refs_0_, bf16[64,2560]{1,0:T(8,128)(2,1)S(1)} %collective-permute-done.3.refs_1_, bf16[64,2560]{1,0:T(8,128)(2,1)S(1)} %collective-permute-done.2.refs_2_, ...), custom_call_target="tpu_custom_call" | custom-call | flops 1677721600 | bytes 8000000 | tf_op jit(solution)/shard_map/pallas_call | solution.py:180
  101.9 4.9 %all-to-all-done.1 = bf16[16,8,1280]{2,1,0:T(8,128)(2,1)S(1)} async-done(((bf16[16,8,1280]{2,1,0:T(8,128)(2,1)}), bf16[16,8,1280]{2,1,0:T(8,128)(2,1)S(1)}, u32[]{:S(2)}, u32[]{:S(2)}) %all-to-all-start.1) | async-done | bytes 327712 | tf_op jit(solution)/shard_map/all_to_all | solution.py:50
  108.1 12.9 %all_to_all.26 = bf16[16,2,1280]{2,1,0:T(2,128)(2,1)S(1)} all-to-all(bf16[16,2,1280]{2,1,0:T(2,128)(2,1)S(1)} %get-tuple-element.122), channel_id=1, replica_groups=mesh['yl'=2,'x'=4,'yh'=2,'z'=8,'c'=2] {'yl','x','c'}, dimensions={0} | all-to-all | bytes 163840 | tf_op jit(solution)/shard_map/all_to_all | solution.py:50
  121.2 13.7 %all_to_all.27 = bf16[16,2,1280]{2,1,0:T(2,128)(2,1)S(1)} all-to-all(bf16[16,2,1280]{2,1,0:T(2,128)(2,1)S(1)} %broadcast_in_dim.8), channel_id=1, replica_groups=mesh['yl'=2,'x'=4,'yh'=2,'z'=8,'c'=2] {'yh','z'}, dimensions={0} | all-to-all | bytes 163840 | tf_op jit(solution)/shard_map/all_to_all | solution.py:50
  135.6 5.1 %all-to-all-start.4 = ((bf16[16,2,1280]{2,1,0:T(2,128)(2,1)}), bf16[16,2,1280]{2,1,0:T(2,128)(2,1)S(1)}, u32[]{:S(2)}, u32[]{:S(2)}) async-start(bf16[16,2,1280]{2,1,0:T(2,128)(2,1)} %broadcast_in_dim.9), calls=%async_computation.4 | async-start | bytes 163840 | tf_op jit(solution)/shard_map/all_to_all | solution.py:50
  140.7 2.5 %shard_map.101 = (bf16[2,256,1280]{2,1,0:T(8,128)(2,1)}, bf16[2,256,1280]{2,1,0:T(8,128)(2,1)}) custom-call(s32[1]{0:T(128)} %bitcast.core, bf16[128,1280]{1,0:T(8,128)(2,1)S(1)} %bitcast.24, bf16[2,32,256]{2,1,0:T(8,128)(2,1)S(1)} %get-tuple-element.119.gates, f32[2,2,32,256]{3,2,1,0:T(8,128)S(1)} %shard_map.99.probs, bf16[32,1280]{1,0:T(8,128)(2,1)S(1)} %copy-done.5), custom_call_target="tpu_custom_call" | custom-call | flops 1000000000 | bytes 3000000 | tf_op jit(solution)/shard_map/pallas_call | solution.py:291
  143.2 3.4 %all-to-all-done.4 = bf16[16,2,1280]{2,1,0:T(2,128)(2,1)S(1)} async-done(((bf16[16,2,1280]{2,1,0:T(2,128)(2,1)}), bf16[16,2,1280]{2,1,0:T(2,128)(2,1)S(1)}, u32[]{:S(2)}, u32[]{:S(2)}) %all-to-all-start.4) | async-done | bytes 81952 | tf_op jit(solution)/shard_map/all_to_all | solution.py:50
  (84 shorter events, 24.0 us)
Async XLA Ops:
  28.5 3.7 %collective-permute-start = (bf16[32,2560]{1,0:T(8,128)(2,1)S(1)}, bf16[32,2560]{1,0:T(8,128)(2,1)S(1)}, u32[]{:S(2)}, u32[]{:S(2)}) collective-permute-start(bf16[32,2560]{1,0:T(8,128)(2,1)S(1)} %bitcast.30), channel_id=1, source_target_pairs={{0,1},{1,0},{2,3},{3,2},{4,5},{5,4},{6,7},{7,6},{8,9},{9,8},{10,11... | collective-permute-start | bytes 491528 | tf_op jit(solution)/shard_map/ppermute | solution.py:66
  32.2 11.7 %copy-start.1 = (bf16[1,640,1280]{2,1,0:T(8,128)(2,1)S(1)}, bf16[1,640,1280]{2,1,0:T(8,128)(2,1)}, u32[]{:S(2)}) copy-start(bf16[1,640,1280]{2,1,0:T(8,128)(2,1)} %param.8) | copy-start | bytes 4915204
  32.3 10.2 %collective-permute-start.3 = (bf16[64,2560]{1,0:T(8,128)(2,1)S(1)}, bf16[64,2560]{1,0:T(8,128)(2,1)S(1)}, u32[]{:S(2)}, u32[]{:S(2)}) collective-permute-start(bf16[64,2560]{1,0:T(8,128)(2,1)S(1)} %constant_dynamic-update-slice_fusion.refs_0_), channel_id=1, source_target_pairs={{0,32},{32,64},{64,96},{96,0},{1,33},{33,65},{65,97},{97,1},{2,34}... | collective-permute-start | bytes 983048 | tf_op jit(solution)/shard_map/ppermute | solution.py:54
  33.6 9.0 %collective-permute-start.2 = (bf16[64,2560]{1,0:T(8,128)(2,1)S(1)}, bf16[64,2560]{1,0:T(8,128)(2,1)S(1)}, u32[]{:S(2)}, u32[]{:S(2)}) collective-permute-start(bf16[64,2560]{1,0:T(8,128)(2,1)S(1)} %constant_dynamic-update-slice_fusion.refs_0_), channel_id=1, source_target_pairs={{0,96},{32,0},{64,32},{96,64},{1,97},{33,1},{65,33},{97,65},{2,98}... | collective-permute-start | bytes 983048 | tf_op jit(solution)/shard_map/ppermute | solution.py:58
  35.0 8.3 %collective-permute-start.1 = (bf16[64,2560]{1,0:T(8,128)(2,1)S(1)}, bf16[64,2560]{1,0:T(8,128)(2,1)S(1)}, u32[]{:S(2)}, u32[]{:S(2)}) collective-permute-start(bf16[64,2560]{1,0:T(8,128)(2,1)S(1)} %constant_dynamic-update-slice_fusion.refs_0_), channel_id=1, source_target_pairs={{0,128},{128,0},{1,129},{129,1},{2,130},{130,2},{3,131},{131,3},{4... | collective-permute-start | bytes 983048 | tf_op jit(solution)/shard_map/ppermute | solution.py:62
  43.4 8.7 %collective-permute-start.4 = (bf16[64,2560]{1,0:T(8,128)(2,1)S(1)}, bf16[64,2560]{1,0:T(8,128)(2,1)S(1)}, u32[]{:S(2)}, u32[]{:S(2)}) collective-permute-start(bf16[64,2560]{1,0:T(8,128)(2,1)S(1)} %get-tuple-element.138), channel_id=1, source_target_pairs={{0,32},{32,64},{64,96},{96,0},{1,33},{33,65},{65,97},{97,1},{2,34}... | collective-permute-start | bytes 983048 | tf_op jit(solution)/shard_map/ppermute | solution.py:54
  43.6 8.6 %collective-permute-start.6 = (bf16[64,2560]{1,0:T(8,128)(2,1)S(1)}, bf16[64,2560]{1,0:T(8,128)(2,1)S(1)}, u32[]{:S(2)}, u32[]{:S(2)}) collective-permute-start(bf16[64,2560]{1,0:T(8,128)(2,1)S(1)} %get-tuple-element.139), channel_id=1, source_target_pairs={{0,128},{128,0},{1,129},{129,1},{2,130},{130,2},{3,131},{131,3},{4... | collective-permute-start | bytes 983048 | tf_op jit(solution)/shard_map/ppermute | solution.py:62
  47.0 10.6 %copy-start.8 = (bf16[256,640]{1,0:T(8,128)(2,1)}, bf16[256,640]{1,0:T(8,128)(2,1)S(1)}, u32[]{:S(2)}) copy-start(bf16[256,640]{1,0:T(8,128)(2,1)S(1)} %get-tuple-element.104.refs_9_) | copy-start | bytes 983044
  47.0 17.0 %collective-permute-start.8 = (bf16[64,2560]{1,0:T(8,128)(2,1)S(1)}, bf16[64,2560]{1,0:T(8,128)(2,1)S(1)}, u32[]{:S(2)}, u32[]{:S(2)}) collective-permute-start(bf16[64,2560]{1,0:T(8,128)(2,1)S(1)} %get-tuple-element.79), channel_id=1, source_target_pairs={{0,96},{32,0},{64,32},{96,64},{1,97},{33,1},{65,33},{97,65},{2,98}... | collective-permute-start | bytes 983048 | tf_op jit(solution)/shard_map/ppermute | solution.py:58
  52.1 5.5 %collective-permute-start.5 = (bf16[32,2560]{1,0:T(8,128)(2,1)S(1)}, bf16[32,2560]{1,0:T(8,128)(2,1)S(1)}, u32[]{:S(2)}, u32[]{:S(2)}) collective-permute-start(bf16[32,2560]{1,0:T(8,128)(2,1)S(1)} %slice.113), channel_id=1, source_target_pairs={{0,32},{32,64},{64,96},{96,0},{1,33},{33,65},{65,97},{97,1},{2,34}... | collective-permute-start | bytes 491528 | tf_op jit(solution)/shard_map/ppermute | solution.py:54
  52.2 6.7 %collective-permute-start.7 = (bf16[32,2560]{1,0:T(8,128)(2,1)S(1)}, bf16[32,2560]{1,0:T(8,128)(2,1)S(1)}, u32[]{:S(2)}, u32[]{:S(2)}) collective-permute-start(bf16[32,2560]{1,0:T(8,128)(2,1)S(1)} %slice.115), channel_id=1, source_target_pairs={{0,96},{32,0},{64,32},{96,64},{1,97},{33,1},{65,33},{97,65},{2,98}... | collective-permute-start | bytes 491528 | tf_op jit(solution)/shard_map/ppermute | solution.py:58
  60.5 6.4 %collective-permute-start.13 = (bf16[32,2560]{1,0:T(8,128)(2,1)S(1)}, bf16[32,2560]{1,0:T(8,128)(2,1)S(1)}, u32[]{:S(2)}, u32[]{:S(2)}) collective-permute-start(bf16[32,2560]{1,0:T(8,128)(2,1)S(1)} %get-tuple-element.85), channel_id=1, source_target_pairs={{0,32},{32,64},{64,96},{96,0},{1,33},{33,65},{65,97},{97,1},{2,34}... | collective-permute-start | bytes 491528 | tf_op jit(solution)/shard_map/ppermute | solution.py:54
  60.6 6.5 %collective-permute-start.9 = (bf16[32,2560]{1,0:T(8,128)(2,1)S(1)}, bf16[32,2560]{1,0:T(8,128)(2,1)S(1)}, u32[]{:S(2)}, u32[]{:S(2)}) collective-permute-start(bf16[32,2560]{1,0:T(8,128)(2,1)S(1)} %get-tuple-element.81), channel_id=1, source_target_pairs={{0,96},{32,0},{64,32},{96,64},{1,97},{33,1},{65,33},{97,65},{2,98}... | collective-permute-start | bytes 491528 | tf_op jit(solution)/shard_map/ppermute | solution.py:58
  66.1 6.6 %collective-permute-start.11 = (bf16[64,2560]{1,0:T(8,128)(2,1)S(1)}, bf16[64,2560]{1,0:T(8,128)(2,1)S(1)}, u32[]{:S(2)}, u32[]{:S(2)}) collective-permute-start(bf16[64,2560]{1,0:T(8,128)(2,1)S(1)} %get-tuple-element.82), channel_id=1, source_target_pairs={{0,128},{128,0},{1,129},{129,1},{2,130},{130,2},{3,131},{131,3},{4... | collective-permute-start | bytes 983048 | tf_op jit(solution)/shard_map/ppermute | solution.py:62
  67.0 7.2 %collective-permute-start.14 = (bf16[64,2560]{1,0:T(8,128)(2,1)S(1)}, bf16[64,2560]{1,0:T(8,128)(2,1)S(1)}, u32[]{:S(2)}, u32[]{:S(2)}) collective-permute-start(bf16[64,2560]{1,0:T(8,128)(2,1)S(1)} %pad_maximum_fusion.5), channel_id=1, source_target_pairs={{0,32},{32,64},{64,96},{96,0},{1,33},{33,65},{65,97},{97,1},{2,34}... | collective-permute-start | bytes 983048 | tf_op jit(solution)/shard_map/ppermute | solution.py:54
  67.2 7.0 %collective-permute-start.10 = (bf16[64,2560]{1,0:T(8,128)(2,1)S(1)}, bf16[64,2560]{1,0:T(8,128)(2,1)S(1)}, u32[]{:S(2)}, u32[]{:S(2)}) collective-permute-start(bf16[64,2560]{1,0:T(8,128)(2,1)S(1)} %pad_maximum_fusion.3), channel_id=1, source_target_pairs={{0,96},{32,0},{64,32},{96,64},{1,97},{33,1},{65,33},{97,65},{2,98}... | collective-permute-start | bytes 983048 | tf_op jit(solution)/shard_map/ppermute | solution.py:58
  74.5 6.0 %collective-permute-start.16 = (bf16[64,2560]{1,0:T(8,128)(2,1)S(1)}, bf16[64,2560]{1,0:T(8,128)(2,1)S(1)}, u32[]{:S(2)}, u32[]{:S(2)}) collective-permute-start(bf16[64,2560]{1,0:T(8,128)(2,1)S(1)} %pad_maximum_fusion.7), channel_id=1, source_target_pairs={{0,128},{128,0},{1,129},{129,1},{2,130},{130,2},{3,131},{131,3},{4... | collective-permute-start | bytes 983048 | tf_op jit(solution)/shard_map/ppermute | solution.py:62
  75.3 7.4 %collective-permute-start.15 = (bf16[64,2560]{1,0:T(8,128)(2,1)S(1)}, bf16[64,2560]{1,0:T(8,128)(2,1)S(1)}, u32[]{:S(2)}, u32[]{:S(2)}) collective-permute-start(bf16[64,2560]{1,0:T(8,128)(2,1)S(1)} %pad_maximum_fusion.6), channel_id=1, source_target_pairs={{0,32},{32,64},{64,96},{96,0},{1,33},{33,65},{65,97},{97,1},{2,34}... | collective-permute-start | bytes 983048 | tf_op jit(solution)/shard_map/ppermute | solution.py:54
  75.4 7.2 %collective-permute-start.12 = (bf16[64,2560]{1,0:T(8,128)(2,1)S(1)}, bf16[64,2560]{1,0:T(8,128)(2,1)S(1)}, u32[]{:S(2)}, u32[]{:S(2)}) collective-permute-start(bf16[64,2560]{1,0:T(8,128)(2,1)S(1)} %pad_maximum_fusion.4), channel_id=1, source_target_pairs={{0,96},{32,0},{64,32},{96,64},{1,97},{33,1},{65,33},{97,65},{2,98}... | collective-permute-start | bytes 983048 | tf_op jit(solution)/shard_map/ppermute | solution.py:58
  82.9 6.9 %collective-permute-start.17 = (bf16[32,2560]{1,0:T(8,128)(2,1)S(1)}, bf16[32,2560]{1,0:T(8,128)(2,1)S(1)}, u32[]{:S(2)}, u32[]{:S(2)}) collective-permute-start(bf16[32,2560]{1,0:T(8,128)(2,1)S(1)} %get-tuple-element.125), channel_id=1, source_target_pairs={{0,1},{1,0},{2,3},{3,2},{4,5},{5,4},{6,7},{7,6},{8,9},{9,8},{10,11... | collective-permute-start | bytes 491528 | tf_op jit(solution)/shard_map/ppermute | solution.py:66
  90.7 16.1 %all-to-all-start.1 = ((bf16[16,8,1280]{2,1,0:T(8,128)(2,1)}), bf16[16,8,1280]{2,1,0:T(8,128)(2,1)S(1)}, u32[]{:S(2)}, u32[]{:S(2)}) async-start(bf16[16,8,1280]{2,1,0:T(8,128)(2,1)} %bitcast.7), calls=%async_computation.1 | async-start | bytes 655360 | tf_op jit(solution)/shard_map/all_to_all | solution.py:50
  98.3 3.4 %copy-start.3 = (bf16[2,256,1280]{2,1,0:T(8,128)(2,1)S(1)}, bf16[2,256,1280]{2,1,0:T(8,128)(2,1)}, u32[]{:S(2)}) copy-start(bf16[2,256,1280]{2,1,0:T(8,128)(2,1)} %cotangent.2) | copy-start | bytes 3932164
  106.8 33.9 %copy-start.5 = (bf16[32,1280]{1,0:T(8,128)(2,1)S(1)}, bf16[32,1280]{1,0:T(8,128)(2,1)}, u32[]{:S(2)}) copy-start(bf16[32,1280]{1,0:T(8,128)(2,1)} %router.3) | copy-start | bytes 245764
  135.6 11.0 %all-to-all-start.4 = ((bf16[16,2,1280]{2,1,0:T(2,128)(2,1)}), bf16[16,2,1280]{2,1,0:T(2,128)(2,1)S(1)}, u32[]{:S(2)}, u32[]{:S(2)}) async-start(bf16[16,2,1280]{2,1,0:T(2,128)(2,1)} %broadcast_in_dim.9), calls=%async_computation.4 | async-start | bytes 163840 | tf_op jit(solution)/shard_map/all_to_all | solution.py:50
  (8 other events, 13.1 us)

commit v5 on v4

--- a/solution.py
+++ b/solution.py
@@ -318,13 +318,29 @@
     return jnp.concatenate([a, b])
 
 
+def fold_kernel(parts, out):
+    total = parts[0].astype(F32)
+    for k in range(1, 16):
+        total += parts[k].astype(F32)
+    total = total.astype(BF16)
+    for k in range(16):
+        out[k] = total
+
+
+def fold(parts):
+    return pl.pallas_call(
+        fold_kernel,
+        in_specs=[VMEM],
+        out_specs=VMEM,
+        out_shape=jax.ShapeDtypeStruct((16, 2, D), BF16),
+        compiler_params=PARAMS,
+        cost_estimate=cost(10**6, 10**6),
+    )(parts)
+
+
 def sum_over_all(term):
-    part = exchange(term, PLANE)
-    part = jnp.sum(part.astype(F32), axis=0).astype(BF16)
-    part = exchange(jnp.broadcast_to(part[None], (16, 2, D)), COLUMN)
-    part = jnp.sum(part.astype(F32), axis=0).astype(BF16)
-    part = exchange(jnp.broadcast_to(part[None], (16, 2, D)), PLANE)
-    return part.reshape(SLOTS, D).astype(F32)
+    part = exchange(fold(exchange(term, PLANE)), COLUMN)
+    return exchange(fold(part), PLANE).reshape(SLOTS, D).astype(F32)
 
 
 def shards(tokens, router, w_in, w_out, cotangent):

time: 148 us -> 148 us (level)
  no operation moved by 1% of the time
where the time goes in v5:
time: 148 us; the launch traced here: 147 us
  blocking collectives  49.6 us (34%)
  starting transfers between devices  38.4 us (26%)
  waiting for transfers between devices  33.2 us (22%)
  Pallas kernels  19.3 us (13%)
  local copies, waits for them, and re-layouts  4.93 us (3%)
    all_to_all x3, blocking collectives, exchange(): return lax.all_to_all(x, axes, split_axis=0, concat_axis=0, tiled=True)  49.6 us
    ppermute x6, waiting for transfers between devices, x_up(): return lax.ppermute(a, 'x', [(i, (i + 1) % 4) for i in range(4)])  15.9 us
    ppermute x6, starting transfers between devices, x_down(): return lax.ppermute(a, 'x', [(i, (i + 3) % 4) for i in range(4)])  15.8 us
    all_to_all x2, starting transfers between devices, exchange(): return lax.all_to_all(x, axes, split_axis=0, concat_axis=0, tiled=True)  9.78 us
    ppermute x2, starting transfers between devices, core_swap(): return lax.ppermute(a, 'c', [(0, 1), (1, 0)])  8.56 us
    all_to_all x2, waiting for transfers between devices, exchange(): return lax.all_to_all(x, axes, split_axis=0, concat_axis=0, tiled=True)  8.25 us
    pallas_call x3, Pallas kernels, experts(): pl.pallas_call(functools.partial(experts_kernel, n, order), in_specs=[VME...  5.82 us
    ppermute x4, waiting for transfers between devices, y_swap(): return lax.ppermute(a, 'yl', [(0, 1), (1, 0)])  5.64 us
  transfers between devices with their start and end apart: 20, of which 13 were waited for; matrix products, arithmetic and copies ran while one was open for 0% of the time, Pallas kernels for 8%

profile of v5, /device:TPU:1, one launch (start us, length us, event | category | flops | bytes accessed | tf_op | source)
XLA Modules:
  0.0 147.1 jit_solution(7281714381383896350)
XLA Ops:
  0.6 4.4 %shard_map.92 = (bf16[128,1280]{1,0:T(8,128)(2,1)}, f32[2,2,32,256]{3,2,1,0:T(8,128)}) custom-call(s32[1]{0:T(128)} %bitcast.core, bf16[2,256,1280]{2,1,0:T(8,128)(2,1)} %tokens.2, bf16[32,1280]{1,0:T(8,128)(2,1)} %router.3, bf16[2,256,1280]{2,1,0:T(8,128)(2,1)} %cotangent.2), custom_call_target="tpu_custom_call" | custom-call | flops 1000000000 | bytes 3000000 | tf_op jit(solution)/shard_map/pallas_call | solution.py:110
  5.0 23.0 %all_to_all.25 = bf16[16,8,1280]{2,1,0:T(8,128)(2,1)S(1)} all-to-all(bf16[16,8,1280]{2,1,0:T(8,128)(2,1)} %bitcast.29), channel_id=1, replica_groups=mesh['yl'=2,'x'=4,'yh'=2,'z'=8,'c'=2] {'yh','z'}, dimensions={0} | all-to-all | bytes 655360 | tf_op jit(solution)/shard_map/all_to_all | solution.py:50
  28.5 2.7 %collective-permute-start = (bf16[32,2560]{1,0:T(8,128)(2,1)S(1)}, bf16[32,2560]{1,0:T(8,128)(2,1)S(1)}, u32[]{:S(2)}, u32[]{:S(2)}) collective-permute-start(bf16[32,2560]{1,0:T(8,128)(2,1)S(1)} %bitcast.30), channel_id=1, source_target_pairs={{0,1},{1,0},{2,3},{3,2},{4,5},{5,4},{6,7},{7,6},{8,9},{9,8},{10,11... | collective-permute-start | bytes 491528 | tf_op jit(solution)/shard_map/ppermute | solution.py:66
  35.4 7.1 %collective-permute-done.3.refs_1_ = bf16[64,2560]{1,0:T(8,128)(2,1)S(1)} collective-permute-done((bf16[64,2560]{1,0:T(8,128)(2,1)S(1)}, bf16[64,2560]{1,0:T(8,128)(2,1)S(1)}, u32[]{:S(2)}, u32[]{:S(2)}) %collective-permute-start.3) | collective-permute-done | bytes 327712 | tf_op jit(solution)/shard_map/ppermute | solution.py:54
  44.0 2.2 %shard_map.93 = (bf16[64,2560]{1,0:T(8,128)(2,1)S(1)}, bf16[64,2560]{1,0:T(8,128)(2,1)S(1)}, bf16[64,2560]{1,0:T(8,128)(2,1)S(1)}, bf16[64,2560]{1,0:T(8,128)(2,...) custom-call(bf16[64,2560]{1,0:T(8,128)(2,1)S(1)} %constant_dynamic-update-slice_fusion.refs_0_, ...), custom_call_target="tpu_custom_call" | custom-call | flops 1677721600 | bytes 4000000 | tf_op jit(solution)/shard_map/pallas_call | solution.py:157
  47.0 2.6 %collective-permute-start.8 = (bf16[64,2560]{1,0:T(8,128)(2,1)S(1)}, bf16[64,2560]{1,0:T(8,128)(2,1)S(1)}, u32[]{:S(2)}, u32[]{:S(2)}) collective-permute-start(bf16[64,2560]{1,0:T(8,128)(2,1)S(1)} %get-tuple-element.79), channel_id=1, source_target_pairs={{0,96},{32,0},{64,32},{96,64},{1,97},{33,1},{65,33},{97,65},{2,98}... | collective-permute-start | bytes 983048 | tf_op jit(solution)/shard_map/ppermute | solution.py:58
  49.6 2.5 %collective-permute-done.4.refs_0_.refs_6_ = bf16[64,2560]{1,0:T(8,128)(2,1)S(1)} collective-permute-done((bf16[64,2560]{1,0:T(8,128)(2,1)S(1)}, bf16[64,2560]{1,0:T(8,128)(2,1)S(1)}, u32[]{:S(2)}, u32[]{:S(2)}) %collective-permute-start.4) | collective-permute-done | bytes 327712 | tf_op jit(solution)/shard_map/ppermute | solution.py:54
  52.2 2.7 %collective-permute-start.7 = (bf16[32,2560]{1,0:T(8,128)(2,1)S(1)}, bf16[32,2560]{1,0:T(8,128)(2,1)S(1)}, u32[]{:S(2)}, u32[]{:S(2)}) collective-permute-start(bf16[32,2560]{1,0:T(8,128)(2,1)S(1)} %slice.115), channel_id=1, source_target_pairs={{0,96},{32,0},{64,32},{96,64},{1,97},{33,1},{65,33},{97,65},{2,98}... | collective-permute-start | bytes 491528 | tf_op jit(solution)/shard_map/ppermute | solution.py:58
  54.9 2.6 %collective-permute-done.5.refs_0_.refs_4_ = bf16[32,2560]{1,0:T(8,128)(2,1)S(1)} collective-permute-done((bf16[32,2560]{1,0:T(8,128)(2,1)S(1)}, bf16[32,2560]{1,0:T(8,128)(2,1)S(1)}, u32[]{:S(2)}, u32[]{:S(2)}) %collective-permute-start.5) | collective-permute-done | bytes 163872 | tf_op jit(solution)/shard_map/ppermute | solution.py:54
  60.6 3.4 %collective-permute-start.9 = (bf16[32,2560]{1,0:T(8,128)(2,1)S(1)}, bf16[32,2560]{1,0:T(8,128)(2,1)S(1)}, u32[]{:S(2)}, u32[]{:S(2)}) collective-permute-start(bf16[32,2560]{1,0:T(8,128)(2,1)S(1)} %get-tuple-element.81), channel_id=1, source_target_pairs={{0,96},{32,0},{64,32},{96,64},{1,97},{33,1},{65,33},{97,65},{2,98}... | collective-permute-start | bytes 491528 | tf_op jit(solution)/shard_map/ppermute | solution.py:58
  67.2 2.7 %collective-permute-start.10 = (bf16[64,2560]{1,0:T(8,128)(2,1)S(1)}, bf16[64,2560]{1,0:T(8,128)(2,1)S(1)}, u32[]{:S(2)}, u32[]{:S(2)}) collective-permute-start(bf16[64,2560]{1,0:T(8,128)(2,1)S(1)} %pad_maximum_fusion.3), channel_id=1, source_target_pairs={{0,96},{32,0},{64,32},{96,64},{1,97},{33,1},{65,33},{97,65},{2,98}... | collective-permute-start | bytes 983048 | tf_op jit(solution)/shard_map/ppermute | solution.py:58
  69.9 2.7 %collective-permute-done.11 = bf16[64,2560]{1,0:T(8,128)(2,1)S(1)} collective-permute-done((bf16[64,2560]{1,0:T(8,128)(2,1)S(1)}, bf16[64,2560]{1,0:T(8,128)(2,1)S(1)}, u32[]{:S(2)}, u32[]{:S(2)}) %collective-permute-start.11) | collective-permute-done | bytes 327712 | tf_op jit(solution)/shard_map/ppermute | solution.py:62
  75.4 2.9 %collective-permute-start.12 = (bf16[64,2560]{1,0:T(8,128)(2,1)S(1)}, bf16[64,2560]{1,0:T(8,128)(2,1)S(1)}, u32[]{:S(2)}, u32[]{:S(2)}) collective-permute-start(bf16[64,2560]{1,0:T(8,128)(2,1)S(1)} %pad_maximum_fusion.4), channel_id=1, source_target_pairs={{0,96},{32,0},{64,32},{96,64},{1,97},{33,1},{65,33},{97,65},{2,98}... | collective-permute-start | bytes 983048 | tf_op jit(solution)/shard_map/ppermute | solution.py:58
  78.3 2.2 %collective-permute-done.16 = bf16[64,2560]{1,0:T(8,128)(2,1)S(1)} collective-permute-done((bf16[64,2560]{1,0:T(8,128)(2,1)S(1)}, bf16[64,2560]{1,0:T(8,128)(2,1)S(1)}, u32[]{:S(2)}, u32[]{:S(2)}) %collective-permute-start.16) | collective-permute-done | bytes 327712 | tf_op jit(solution)/shard_map/ppermute | solution.py:62
  80.5 2.2 %collective-permute-done.15 = bf16[64,2560]{1,0:T(8,128)(2,1)S(1)} collective-permute-done((bf16[64,2560]{1,0:T(8,128)(2,1)S(1)}, bf16[64,2560]{1,0:T(8,128)(2,1)S(1)}, u32[]{:S(2)}, u32[]{:S(2)}) %collective-permute-start.15) | collective-permute-done | bytes 327712 | tf_op jit(solution)/shard_map/ppermute | solution.py:54
  82.9 5.9 %collective-permute-start.17 = (bf16[32,2560]{1,0:T(8,128)(2,1)S(1)}, bf16[32,2560]{1,0:T(8,128)(2,1)S(1)}, u32[]{:S(2)}, u32[]{:S(2)}) collective-permute-start(bf16[32,2560]{1,0:T(8,128)(2,1)S(1)} %get-tuple-element.125), channel_id=1, source_target_pairs={{0,1},{1,0},{2,3},{3,2},{4,5},{5,4},{6,7},{7,6},{8,9},{9,8},{10,11... | collective-permute-start | bytes 491528 | tf_op jit(solution)/shard_map/ppermute | solution.py:66
  90.7 4.7 %all-to-all-start.1 = ((bf16[16,8,1280]{2,1,0:T(8,128)(2,1)}), bf16[16,8,1280]{2,1,0:T(8,128)(2,1)S(1)}, u32[]{:S(2)}, u32[]{:S(2)}) async-start(bf16[16,8,1280]{2,1,0:T(8,128)(2,1)} %bitcast.7), calls=%async_computation.1 | async-start | bytes 655360 | tf_op jit(solution)/shard_map/all_to_all | solution.py:50
  98.3 3.4 %shard_map.97 = (bf16[1280,640]{1,0:T(8,128)(2,1)}, bf16[640,1280]{1,0:T(8,128)(2,1)}) custom-call(bf16[64,2560]{1,0:T(8,128)(2,1)S(1)} %constant_dynamic-update-slice_fusion.refs_0_, bf16[64,2560]{1,0:T(8,128)(2,1)S(1)} %collective-permute-done.3.refs_1_, bf16[64,2560]{1,0:T(8,128)(2,1)S(1)} %collective-permute-done.2.refs_2_, ...), custom_call_target="tpu_custom_call" | custom-call | flops 1677721600 | bytes 8000000 | tf_op jit(solution)/shard_map/pallas_call | solution.py:180
  101.9 4.9 %all-to-all-done.1 = bf16[16,8,1280]{2,1,0:T(8,128)(2,1)S(1)} async-done(((bf16[16,8,1280]{2,1,0:T(8,128)(2,1)}), bf16[16,8,1280]{2,1,0:T(8,128)(2,1)S(1)}, u32[]{:S(2)}, u32[]{:S(2)}) %all-to-all-start.1) | async-done | bytes 327712 | tf_op jit(solution)/shard_map/all_to_all | solution.py:50
  108.1 12.9 %all_to_all.26.parts = bf16[16,2,1280]{2,1,0:T(2,128)(2,1)S(1)} all-to-all(bf16[16,2,1280]{2,1,0:T(2,128)(2,1)S(1)} %get-tuple-element.122), channel_id=1, replica_groups=mesh['yl'=2,'x'=4,'yh'=2,'z'=8,'c'=2] {'yl','x','c'}, dimensions={0} | all-to-all | bytes 163840 | tf_op jit(solution)/shard_map/all_to_all | solution.py:50
  121.1 13.7 %all_to_all.27.parts = bf16[16,2,1280]{2,1,0:T(2,128)(2,1)S(1)} all-to-all(bf16[16,2,1280]{2,1,0:T(2,128)(2,1)S(1)} %shard_map.102), channel_id=1, replica_groups=mesh['yl'=2,'x'=4,'yh'=2,'z'=8,'c'=2] {'yh','z'}, dimensions={0} | all-to-all | bytes 163840 | tf_op jit(solution)/shard_map/all_to_all | solution.py:50
  135.4 5.1 %all-to-all-start.4 = ((bf16[16,2,1280]{2,1,0:T(2,128)(2,1)}), bf16[16,2,1280]{2,1,0:T(2,128)(2,1)S(1)}, u32[]{:S(2)}, u32[]{:S(2)}) async-start(bf16[16,2,1280]{2,1,0:T(2,128)(2,1)} %shard_map.103), calls=%async_computation.4 | async-start | bytes 163840 | tf_op jit(solution)/shard_map/all_to_all | solution.py:50
  140.5 2.5 %shard_map.101 = (bf16[2,256,1280]{2,1,0:T(8,128)(2,1)}, bf16[2,256,1280]{2,1,0:T(8,128)(2,1)}) custom-call(s32[1]{0:T(128)} %bitcast.core, bf16[128,1280]{1,0:T(8,128)(2,1)S(1)} %bitcast.24, bf16[2,32,256]{2,1,0:T(8,128)(2,1)S(1)} %get-tuple-element.119.gates, f32[2,2,32,256]{3,2,1,0:T(8,128)S(1)} %shard_map.99.probs, bf16[32,1280]{1,0:T(8,128)(2,1)S(1)} %copy-done.5), custom_call_target="tpu_custom_call" | custom-call | flops 1000000000 | bytes 3000000 | tf_op jit(solution)/shard_map/pallas_call | solution.py:291
  143.1 3.4 %all-to-all-done.4 = bf16[16,2,1280]{2,1,0:T(2,128)(2,1)S(1)} async-done(((bf16[16,2,1280]{2,1,0:T(2,128)(2,1)}), bf16[16,2,1280]{2,1,0:T(2,128)(2,1)S(1)}, u32[]{:S(2)}, u32[]{:S(2)}) %all-to-all-start.4) | async-done | bytes 81952 | tf_op jit(solution)/shard_map/all_to_all | solution.py:50
  (82 shorter events, 23.8 us)
Async XLA Ops:
  28.5 3.7 %collective-permute-start = (bf16[32,2560]{1,0:T(8,128)(2,1)S(1)}, bf16[32,2560]{1,0:T(8,128)(2,1)S(1)}, u32[]{:S(2)}, u32[]{:S(2)}) collective-permute-start(bf16[32,2560]{1,0:T(8,128)(2,1)S(1)} %bitcast.30), channel_id=1, source_target_pairs={{0,1},{1,0},{2,3},{3,2},{4,5},{5,4},{6,7},{7,6},{8,9},{9,8},{10,11... | collective-permute-start | bytes 491528 | tf_op jit(solution)/shard_map/ppermute | solution.py:66
  32.2 11.7 %copy-start.1 = (bf16[1,640,1280]{2,1,0:T(8,128)(2,1)S(1)}, bf16[1,640,1280]{2,1,0:T(8,128)(2,1)}, u32[]{:S(2)}) copy-start(bf16[1,640,1280]{2,1,0:T(8,128)(2,1)} %param.8) | copy-start | bytes 4915204
  32.3 10.2 %collective-permute-start.3 = (bf16[64,2560]{1,0:T(8,128)(2,1)S(1)}, bf16[64,2560]{1,0:T(8,128)(2,1)S(1)}, u32[]{:S(2)}, u32[]{:S(2)}) collective-permute-start(bf16[64,2560]{1,0:T(8,128)(2,1)S(1)} %constant_dynamic-update-slice_fusion.refs_0_), channel_id=1, source_target_pairs={{0,32},{32,64},{64,96},{96,0},{1,33},{33,65},{65,97},{97,1},{2,34}... | collective-permute-start | bytes 983048 | tf_op jit(solution)/shard_map/ppermute | solution.py:54
  33.6 9.0 %collective-permute-start.2 = (bf16[64,2560]{1,0:T(8,128)(2,1)S(1)}, bf16[64,2560]{1,0:T(8,128)(2,1)S(1)}, u32[]{:S(2)}, u32[]{:S(2)}) collective-permute-start(bf16[64,2560]{1,0:T(8,128)(2,1)S(1)} %constant_dynamic-update-slice_fusion.refs_0_), channel_id=1, source_target_pairs={{0,96},{32,0},{64,32},{96,64},{1,97},{33,1},{65,33},{97,65},{2,98}... | collective-permute-start | bytes 983048 | tf_op jit(solution)/shard_map/ppermute | solution.py:58
  35.0 8.3 %collective-permute-start.1 = (bf16[64,2560]{1,0:T(8,128)(2,1)S(1)}, bf16[64,2560]{1,0:T(8,128)(2,1)S(1)}, u32[]{:S(2)}, u32[]{:S(2)}) collective-permute-start(bf16[64,2560]{1,0:T(8,128)(2,1)S(1)} %constant_dynamic-update-slice_fusion.refs_0_), channel_id=1, source_target_pairs={{0,128},{128,0},{1,129},{129,1},{2,130},{130,2},{3,131},{131,3},{4... | collective-permute-start | bytes 983048 | tf_op jit(solution)/shard_map/ppermute | solution.py:62
  43.4 8.7 %collective-permute-start.4 = (bf16[64,2560]{1,0:T(8,128)(2,1)S(1)}, bf16[64,2560]{1,0:T(8,128)(2,1)S(1)}, u32[]{:S(2)}, u32[]{:S(2)}) collective-permute-start(bf16[64,2560]{1,0:T(8,128)(2,1)S(1)} %get-tuple-element.138), channel_id=1, source_target_pairs={{0,32},{32,64},{64,96},{96,0},{1,33},{33,65},{65,97},{97,1},{2,34}... | collective-permute-start | bytes 983048 | tf_op jit(solution)/shard_map/ppermute | solution.py:54
  43.6 8.6 %collective-permute-start.6 = (bf16[64,2560]{1,0:T(8,128)(2,1)S(1)}, bf16[64,2560]{1,0:T(8,128)(2,1)S(1)}, u32[]{:S(2)}, u32[]{:S(2)}) collective-permute-start(bf16[64,2560]{1,0:T(8,128)(2,1)S(1)} %get-tuple-element.139), channel_id=1, source_target_pairs={{0,128},{128,0},{1,129},{129,1},{2,130},{130,2},{3,131},{131,3},{4... | collective-permute-start | bytes 983048 | tf_op jit(solution)/shard_map/ppermute | solution.py:62
  47.0 10.6 %copy-start.8 = (bf16[256,640]{1,0:T(8,128)(2,1)}, bf16[256,640]{1,0:T(8,128)(2,1)S(1)}, u32[]{:S(2)}) copy-start(bf16[256,640]{1,0:T(8,128)(2,1)S(1)} %get-tuple-element.104.refs_9_) | copy-start | bytes 983044
  47.0 17.0 %collective-permute-start.8 = (bf16[64,2560]{1,0:T(8,128)(2,1)S(1)}, bf16[64,2560]{1,0:T(8,128)(2,1)S(1)}, u32[]{:S(2)}, u32[]{:S(2)}) collective-permute-start(bf16[64,2560]{1,0:T(8,128)(2,1)S(1)} %get-tuple-element.79), channel_id=1, source_target_pairs={{0,96},{32,0},{64,32},{96,64},{1,97},{33,1},{65,33},{97,65},{2,98}... | collective-permute-start | bytes 983048 | tf_op jit(solution)/shard_map/ppermute | solution.py:58
  52.1 5.5 %collective-permute-start.5 = (bf16[32,2560]{1,0:T(8,128)(2,1)S(1)}, bf16[32,2560]{1,0:T(8,128)(2,1)S(1)}, u32[]{:S(2)}, u32[]{:S(2)}) collective-permute-start(bf16[32,2560]{1,0:T(8,128)(2,1)S(1)} %slice.113), channel_id=1, source_target_pairs={{0,32},{32,64},{64,96},{96,0},{1,33},{33,65},{65,97},{97,1},{2,34}... | collective-permute-start | bytes 491528 | tf_op jit(solution)/shard_map/ppermute | solution.py:54
  52.2 6.7 %collective-permute-start.7 = (bf16[32,2560]{1,0:T(8,128)(2,1)S(1)}, bf16[32,2560]{1,0:T(8,128)(2,1)S(1)}, u32[]{:S(2)}, u32[]{:S(2)}) collective-permute-start(bf16[32,2560]{1,0:T(8,128)(2,1)S(1)} %slice.115), channel_id=1, source_target_pairs={{0,96},{32,0},{64,32},{96,64},{1,97},{33,1},{65,33},{97,65},{2,98}... | collective-permute-start | bytes 491528 | tf_op jit(solution)/shard_map/ppermute | solution.py:58
  60.5 6.4 %collective-permute-start.13 = (bf16[32,2560]{1,0:T(8,128)(2,1)S(1)}, bf16[32,2560]{1,0:T(8,128)(2,1)S(1)}, u32[]{:S(2)}, u32[]{:S(2)}) collective-permute-start(bf16[32,2560]{1,0:T(8,128)(2,1)S(1)} %get-tuple-element.85), channel_id=1, source_target_pairs={{0,32},{32,64},{64,96},{96,0},{1,33},{33,65},{65,97},{97,1},{2,34}... | collective-permute-start | bytes 491528 | tf_op jit(solution)/shard_map/ppermute | solution.py:54
  60.6 6.5 %collective-permute-start.9 = (bf16[32,2560]{1,0:T(8,128)(2,1)S(1)}, bf16[32,2560]{1,0:T(8,128)(2,1)S(1)}, u32[]{:S(2)}, u32[]{:S(2)}) collective-permute-start(bf16[32,2560]{1,0:T(8,128)(2,1)S(1)} %get-tuple-element.81), channel_id=1, source_target_pairs={{0,96},{32,0},{64,32},{96,64},{1,97},{33,1},{65,33},{97,65},{2,98}... | collective-permute-start | bytes 491528 | tf_op jit(solution)/shard_map/ppermute | solution.py:58
  66.1 6.6 %collective-permute-start.11 = (bf16[64,2560]{1,0:T(8,128)(2,1)S(1)}, bf16[64,2560]{1,0:T(8,128)(2,1)S(1)}, u32[]{:S(2)}, u32[]{:S(2)}) collective-permute-start(bf16[64,2560]{1,0:T(8,128)(2,1)S(1)} %get-tuple-element.82), channel_id=1, source_target_pairs={{0,128},{128,0},{1,129},{129,1},{2,130},{130,2},{3,131},{131,3},{4... | collective-permute-start | bytes 983048 | tf_op jit(solution)/shard_map/ppermute | solution.py:62
  67.0 7.2 %collective-permute-start.14 = (bf16[64,2560]{1,0:T(8,128)(2,1)S(1)}, bf16[64,2560]{1,0:T(8,128)(2,1)S(1)}, u32[]{:S(2)}, u32[]{:S(2)}) collective-permute-start(bf16[64,2560]{1,0:T(8,128)(2,1)S(1)} %pad_maximum_fusion.5), channel_id=1, source_target_pairs={{0,32},{32,64},{64,96},{96,0},{1,33},{33,65},{65,97},{97,1},{2,34}... | collective-permute-start | bytes 983048 | tf_op jit(solution)/shard_map/ppermute | solution.py:54
  67.2 7.0 %collective-permute-start.10 = (bf16[64,2560]{1,0:T(8,128)(2,1)S(1)}, bf16[64,2560]{1,0:T(8,128)(2,1)S(1)}, u32[]{:S(2)}, u32[]{:S(2)}) collective-permute-start(bf16[64,2560]{1,0:T(8,128)(2,1)S(1)} %pad_maximum_fusion.3), channel_id=1, source_target_pairs={{0,96},{32,0},{64,32},{96,64},{1,97},{33,1},{65,33},{97,65},{2,98}... | collective-permute-start | bytes 983048 | tf_op jit(solution)/shard_map/ppermute | solution.py:58
  74.5 6.0 %collective-permute-start.16 = (bf16[64,2560]{1,0:T(8,128)(2,1)S(1)}, bf16[64,2560]{1,0:T(8,128)(2,1)S(1)}, u32[]{:S(2)}, u32[]{:S(2)}) collective-permute-start(bf16[64,2560]{1,0:T(8,128)(2,1)S(1)} %pad_maximum_fusion.7), channel_id=1, source_target_pairs={{0,128},{128,0},{1,129},{129,1},{2,130},{130,2},{3,131},{131,3},{4... | collective-permute-start | bytes 983048 | tf_op jit(solution)/shard_map/ppermute | solution.py:62
  75.3 7.4 %collective-permute-start.15 = (bf16[64,2560]{1,0:T(8,128)(2,1)S(1)}, bf16[64,2560]{1,0:T(8,128)(2,1)S(1)}, u32[]{:S(2)}, u32[]{:S(2)}) collective-permute-start(bf16[64,2560]{1,0:T(8,128)(2,1)S(1)} %pad_maximum_fusion.6), channel_id=1, source_target_pairs={{0,32},{32,64},{64,96},{96,0},{1,33},{33,65},{65,97},{97,1},{2,34}... | collective-permute-start | bytes 983048 | tf_op jit(solution)/shard_map/ppermute | solution.py:54
  75.4 7.2 %collective-permute-start.12 = (bf16[64,2560]{1,0:T(8,128)(2,1)S(1)}, bf16[64,2560]{1,0:T(8,128)(2,1)S(1)}, u32[]{:S(2)}, u32[]{:S(2)}) collective-permute-start(bf16[64,2560]{1,0:T(8,128)(2,1)S(1)} %pad_maximum_fusion.4), channel_id=1, source_target_pairs={{0,96},{32,0},{64,32},{96,64},{1,97},{33,1},{65,33},{97,65},{2,98}... | collective-permute-start | bytes 983048 | tf_op jit(solution)/shard_map/ppermute | solution.py:58
  82.9 6.9 %collective-permute-start.17 = (bf16[32,2560]{1,0:T(8,128)(2,1)S(1)}, bf16[32,2560]{1,0:T(8,128)(2,1)S(1)}, u32[]{:S(2)}, u32[]{:S(2)}) collective-permute-start(bf16[32,2560]{1,0:T(8,128)(2,1)S(1)} %get-tuple-element.125), channel_id=1, source_target_pairs={{0,1},{1,0},{2,3},{3,2},{4,5},{5,4},{6,7},{7,6},{8,9},{9,8},{10,11... | collective-permute-start | bytes 491528 | tf_op jit(solution)/shard_map/ppermute | solution.py:66
  90.7 16.1 %all-to-all-start.1 = ((bf16[16,8,1280]{2,1,0:T(8,128)(2,1)}), bf16[16,8,1280]{2,1,0:T(8,128)(2,1)S(1)}, u32[]{:S(2)}, u32[]{:S(2)}) async-start(bf16[16,8,1280]{2,1,0:T(8,128)(2,1)} %bitcast.7), calls=%async_computation.1 | async-start | bytes 655360 | tf_op jit(solution)/shard_map/all_to_all | solution.py:50
  98.3 3.4 %copy-start.3 = (bf16[2,256,1280]{2,1,0:T(8,128)(2,1)S(1)}, bf16[2,256,1280]{2,1,0:T(8,128)(2,1)}, u32[]{:S(2)}) copy-start(bf16[2,256,1280]{2,1,0:T(8,128)(2,1)} %cotangent.2) | copy-start | bytes 3932164
  106.8 33.7 %copy-start.5 = (bf16[32,1280]{1,0:T(8,128)(2,1)S(1)}, bf16[32,1280]{1,0:T(8,128)(2,1)}, u32[]{:S(2)}) copy-start(bf16[32,1280]{1,0:T(8,128)(2,1)} %router.3) | copy-start | bytes 245764
  135.4 11.0 %all-to-all-start.4 = ((bf16[16,2,1280]{2,1,0:T(2,128)(2,1)}), bf16[16,2,1280]{2,1,0:T(2,128)(2,1)S(1)}, u32[]{:S(2)}, u32[]{:S(2)}) async-start(bf16[16,2,1280]{2,1,0:T(2,128)(2,1)} %shard_map.103), calls=%async_computation.4 | async-start | bytes 163840 | tf_op jit(solution)/shard_map/all_to_all | solution.py:50
  (8 other events, 13.1 us)

commit v6 on v4

--- a/solution.py
+++ b/solution.py
@@ -190,7 +190,8 @@
     )(*pieces, *hidden, *grad_preact)
 
 
-def pack_kernel(stay, go, message):
+def pack_kernel(own, down, up, side, go, message):
+    stay = add(own[:32], down[:32], up[:32], side[:32])
     rows = jnp.concatenate([stay[:, :D], stay[:, D:], go[:, :D], go[:, D:]], axis=0)
     r = lax.broadcasted_iota(jnp.int32, (128, 128), 0)
     n = lax.broadcasted_iota(jnp.int32, (128, 128), 1)
@@ -198,15 +199,15 @@
     message[...] = mm(pick.astype(F32).astype(BF16), rows).astype(BF16)
 
 
-def pack(stay, go):
+def pack(own, down, up, side, go):
     return pl.pallas_call(
         pack_kernel,
-        in_specs=[VMEM] * 2,
+        in_specs=[VMEM] * 5,
         out_specs=VMEM,
         out_shape=jax.ShapeDtypeStruct((128, D), BF16),
         compiler_params=PARAMS,
         cost_estimate=cost(10**8, 10**6),
-    )(stay, go)
+    )(own, down, up, side, go)
 
 
 def hold_kernel(probs, out):
@@ -362,9 +363,8 @@
     side_in = y_swap(
         join(add(low(side_sum), low(first_in)), add(high(side_sum), low(second_in)))
     )
-    summed = add(own_sum, down_in, up_in, side_in)
-
-    leaving = pack(low(summed), core_swap(high(summed)))
+    go = core_swap(add(high(own_sum), high(down_in), high(up_in), high(side_in)))
+    leaving = pack(own_sum, down_in, up_in, side_in, go)
     pieces = (own, down, up, side, far_low, far_high, first, second, third)
     acts = [(call[1], call[2]) for call in (near, far, middle)]
     leaving, probs, pieces, acts = lax.optimization_barrier((leaving, probs, pieces, acts))

time: 148 us -> 151 us (1.020)
  waiting for transfers between devices: 33.2 us -> 36.3 us
  starting transfers between devices: 38.4 us -> 40.3 us
    ppermute x6, waiting for transfers between devices: 1.35 us -> 8.72 us  [x_down(): return lax.ppermute(a, 'x', [(i, (i + 3) % 4) for i in range(4)])]
    ppermute x6, waiting for transfers between devices: 15.9 us -> 12.5 us  [x_up(): return lax.ppermute(a, 'x', [(i, (i + 1) % 4) for i in range(4)])]
    ppermute x2, starting transfers between devices: 8.56 us -> 11.5 us  [core_swap(): return lax.ppermute(a, 'c', [(0, 1), (1, 0)])]
where the time goes in v6:
time: 151 us; the launch traced here: 150 us
  blocking collectives  48.1 us (32%)
  starting transfers between devices  40.3 us (27%)
  waiting for transfers between devices  36.3 us (24%)
  Pallas kernels  18.6 us (12%)
  local copies, waits for them, and re-layouts  4.93 us (3%)
    all_to_all x3, blocking collectives, exchange(): return lax.all_to_all(x, axes, split_axis=0, concat_axis=0, tiled=True)  48.1 us
    ppermute x6, starting transfers between devices, x_down(): return lax.ppermute(a, 'x', [(i, (i + 3) % 4) for i in range(4)])  14.5 us
    ppermute x6, waiting for transfers between devices, x_up(): return lax.ppermute(a, 'x', [(i, (i + 1) % 4) for i in range(4)])  12.5 us
    ppermute x2, starting transfers between devices, core_swap(): return lax.ppermute(a, 'c', [(0, 1), (1, 0)])  11.5 us
    all_to_all x2, starting transfers between devices, exchange(): return lax.all_to_all(x, axes, split_axis=0, concat_axis=0, tiled=True)  10 us
    ppermute x6, waiting for transfers between devices, x_down(): return lax.ppermute(a, 'x', [(i, (i + 3) % 4) for i in range(4)])  8.72 us
    all_to_all x2, waiting for transfers between devices, exchange(): return lax.all_to_all(x, axes, split_axis=0, concat_axis=0, tiled=True)  8.25 us
    pallas_call x3, Pallas kernels, experts(): pl.pallas_call(functools.partial(experts_kernel, n, order), in_specs=[VME...  5.82 us
  transfers between devices with their start and end apart: 20, of which 13 were waited for; matrix products, arithmetic and copies ran while one was open for 0% of the time, Pallas kernels for 8%

profile of v6, /device:TPU:1, one launch (start us, length us, event | category | flops | bytes accessed | tf_op | source)
XLA Modules:
  0.0 150.0 jit_solution(1775462054366844735)
XLA Ops:
  0.6 4.4 %shard_map.92 = (bf16[128,1280]{1,0:T(8,128)(2,1)}, f32[2,2,32,256]{3,2,1,0:T(8,128)}) custom-call(s32[1]{0:T(128)} %bitcast.core, bf16[2,256,1280]{2,1,0:T(8,128)(2,1)} %tokens.2, bf16[32,1280]{1,0:T(8,128)(2,1)} %router.3, bf16[2,256,1280]{2,1,0:T(8,128)(2,1)} %cotangent.2), custom_call_target="tpu_custom_call" | custom-call | flops 1000000000 | bytes 3000000 | tf_op jit(solution)/shard_map/pallas_call | solution.py:110
  5.0 23.0 %all_to_all.25 = bf16[16,8,1280]{2,1,0:T(8,128)(2,1)S(1)} all-to-all(bf16[16,8,1280]{2,1,0:T(8,128)(2,1)} %bitcast.29), channel_id=1, replica_groups=mesh['yl'=2,'x'=4,'yh'=2,'z'=8,'c'=2] {'yh','z'}, dimensions={0} | all-to-all | bytes 655360 | tf_op jit(solution)/shard_map/all_to_all | solution.py:50
  28.5 2.7 %collective-permute-start = (bf16[32,2560]{1,0:T(8,128)(2,1)S(1)}, bf16[32,2560]{1,0:T(8,128)(2,1)S(1)}, u32[]{:S(2)}, u32[]{:S(2)}) collective-permute-start(bf16[32,2560]{1,0:T(8,128)(2,1)S(1)} %bitcast.30), channel_id=1, source_target_pairs={{0,1},{1,0},{2,3},{3,2},{4,5},{5,4},{6,7},{7,6},{8,9},{9,8},{10,11... | collective-permute-start | bytes 491528 | tf_op jit(solution)/shard_map/ppermute | solution.py:66
  35.4 7.1 %collective-permute-done.3.refs_1_ = bf16[64,2560]{1,0:T(8,128)(2,1)S(1)} collective-permute-done((bf16[64,2560]{1,0:T(8,128)(2,1)S(1)}, bf16[64,2560]{1,0:T(8,128)(2,1)S(1)}, u32[]{:S(2)}, u32[]{:S(2)}) %collective-permute-start.3) | collective-permute-done | bytes 327712 | tf_op jit(solution)/shard_map/ppermute | solution.py:54
  44.0 2.2 %shard_map.93 = (bf16[64,2560]{1,0:T(8,128)(2,1)S(1)}, bf16[64,2560]{1,0:T(8,128)(2,1)S(1)}, bf16[64,2560]{1,0:T(8,128)(2,1)S(1)}, bf16[64,2560]{1,0:T(8,128)(2,...) custom-call(bf16[64,2560]{1,0:T(8,128)(2,1)S(1)} %constant_dynamic-update-slice_fusion.refs_0_, ...), custom_call_target="tpu_custom_call" | custom-call | flops 1677721600 | bytes 4000000 | tf_op jit(solution)/shard_map/pallas_call | solution.py:157
  46.3 2.7 %collective-permute-start.8 = (bf16[64,2560]{1,0:T(8,128)(2,1)S(1)}, bf16[64,2560]{1,0:T(8,128)(2,1)S(1)}, u32[]{:S(2)}, u32[]{:S(2)}) collective-permute-start(bf16[64,2560]{1,0:T(8,128)(2,1)S(1)} %get-tuple-element.79), channel_id=1, source_target_pairs={{0,96},{32,0},{64,32},{96,64},{1,97},{33,1},{65,33},{97,65},{2,98}... | collective-permute-start | bytes 983048 | tf_op jit(solution)/shard_map/ppermute | solution.py:58
  48.9 1.9 %collective-permute-done.6.refs_2_.refs_8_ = bf16[64,2560]{1,0:T(8,128)(2,1)S(1)} collective-permute-done((bf16[64,2560]{1,0:T(8,128)(2,1)S(1)}, bf16[64,2560]{1,0:T(8,128)(2,1)S(1)}, u32[]{:S(2)}, u32[]{:S(2)}) %collective-permute-start.6) | collective-permute-done | bytes 327712 | tf_op jit(solution)/shard_map/ppermute | solution.py:62
  52.9 4.3 %collective-permute-done.7.refs_1_.refs_5_ = bf16[32,2560]{1,0:T(8,128)(2,1)S(1)} collective-permute-done((bf16[32,2560]{1,0:T(8,128)(2,1)S(1)}, bf16[32,2560]{1,0:T(8,128)(2,1)S(1)}, u32[]{:S(2)}, u32[]{:S(2)}) %collective-permute-start.7) | collective-permute-done | bytes 163872 | tf_op jit(solution)/shard_map/ppermute | solution.py:58
  60.0 2.7 %collective-permute-start.9 = (bf16[32,2560]{1,0:T(8,128)(2,1)S(1)}, bf16[32,2560]{1,0:T(8,128)(2,1)S(1)}, u32[]{:S(2)}, u32[]{:S(2)}) collective-permute-start(bf16[32,2560]{1,0:T(8,128)(2,1)S(1)} %get-tuple-element.81), channel_id=1, source_target_pairs={{0,96},{32,0},{64,32},{96,64},{1,97},{33,1},{65,33},{97,65},{2,98}... | collective-permute-start | bytes 491528 | tf_op jit(solution)/shard_map/ppermute | solution.py:58
  62.6 2.0 %shard_map.95 = (bf16[64,2560]{1,0:T(8,128)(2,1)S(1)}, bf16[64,2560]{1,0:T(8,128)(2,1)S(1)}, bf16[64,2560]{1,0:T(8,128)(2,1)S(1)}, bf16[192,640]{1,0:T(8,128)(2,1)S(1)}, bf16[192,640]{1,0:T(8,128)(2,1)S(1)}) custom-call(bf16[64,2560]{1,0:T(8,128)(2,1)S(1)} %collective-permute-done.4.refs_0_.refs_6_, ...), custom_call_target="tpu_custom_call" | custom-call | flops 1258291200 | bytes 4000000 | tf_op jit(solution)/shard_map/pallas_call | solution.py:157
  65.9 2.7 %collective-permute-start.10 = (bf16[64,2560]{1,0:T(8,128)(2,1)S(1)}, bf16[64,2560]{1,0:T(8,128)(2,1)S(1)}, u32[]{:S(2)}, u32[]{:S(2)}) collective-permute-start(bf16[64,2560]{1,0:T(8,128)(2,1)S(1)} %pad_maximum_fusion.3), channel_id=1, source_target_pairs={{0,96},{32,0},{64,32},{96,64},{1,97},{33,1},{65,33},{97,65},{2,98}... | collective-permute-start | bytes 983048 | tf_op jit(solution)/shard_map/ppermute | solution.py:58
  68.6 2.1 %collective-permute-done.11 = bf16[64,2560]{1,0:T(8,128)(2,1)S(1)} collective-permute-done((bf16[64,2560]{1,0:T(8,128)(2,1)S(1)}, bf16[64,2560]{1,0:T(8,128)(2,1)S(1)}, u32[]{:S(2)}, u32[]{:S(2)}) %collective-permute-start.11) | collective-permute-done | bytes 327712 | tf_op jit(solution)/shard_map/ppermute | solution.py:62
  70.7 2.5 %collective-permute-done.14 = bf16[64,2560]{1,0:T(8,128)(2,1)S(1)} collective-permute-done((bf16[64,2560]{1,0:T(8,128)(2,1)S(1)}, bf16[64,2560]{1,0:T(8,128)(2,1)S(1)}, u32[]{:S(2)}, u32[]{:S(2)}) %collective-permute-start.14) | collective-permute-done | bytes 327712 | tf_op jit(solution)/shard_map/ppermute | solution.py:54
  73.5 3.0 %collective-permute-start.12 = (bf16[64,2560]{1,0:T(8,128)(2,1)S(1)}, bf16[64,2560]{1,0:T(8,128)(2,1)S(1)}, u32[]{:S(2)}, u32[]{:S(2)}) collective-permute-start(bf16[64,2560]{1,0:T(8,128)(2,1)S(1)} %pad_maximum_fusion.4), channel_id=1, source_target_pairs={{0,96},{32,0},{64,32},{96,64},{1,97},{33,1},{65,33},{97,65},{2,98}... | collective-permute-start | bytes 983048 | tf_op jit(solution)/shard_map/ppermute | solution.py:58
  77.5 4.4 %collective-permute-done.12.down = bf16[64,2560]{1,0:T(8,128)(2,1)S(1)} collective-permute-done((bf16[64,2560]{1,0:T(8,128)(2,1)S(1)}, bf16[64,2560]{1,0:T(8,128)(2,1)S(1)}, u32[]{:S(2)}, u32[]{:S(2)}) %collective-permute-start.12) | collective-permute-done | bytes 327712 | tf_op jit(solution)/shard_map/ppermute | solution.py:58
  83.8 8.8 %collective-permute-start.17 = (bf16[32,2560]{1,0:T(8,128)(2,1)S(1)}, bf16[32,2560]{1,0:T(8,128)(2,1)S(1)}, u32[]{:S(2)}, u32[]{:S(2)}) collective-permute-start(bf16[32,2560]{1,0:T(8,128)(2,1)S(1)} %add_convert_fusion), channel_id=1, source_target_pairs={{0,1},{1,0},{2,3},{3,2},{4,5},{5,4},{6,7},{7,6},{8,9},{9,8},{10,11... | collective-permute-start | bytes 491528 | tf_op jit(solution)/shard_map/ppermute | solution.py:66
  94.7 4.9 %all-to-all-start.1 = ((bf16[16,8,1280]{2,1,0:T(8,128)(2,1)}), bf16[16,8,1280]{2,1,0:T(8,128)(2,1)S(1)}, u32[]{:S(2)}, u32[]{:S(2)}) async-start(bf16[16,8,1280]{2,1,0:T(8,128)(2,1)} %bitcast.7), calls=%async_computation.1 | async-start | bytes 655360 | tf_op jit(solution)/shard_map/all_to_all | solution.py:50
  102.5 3.4 %shard_map.97 = (bf16[1280,640]{1,0:T(8,128)(2,1)}, bf16[640,1280]{1,0:T(8,128)(2,1)}) custom-call(bf16[64,2560]{1,0:T(8,128)(2,1)S(1)} %constant_dynamic-update-slice_fusion.refs_0_, bf16[64,2560]{1,0:T(8,128)(2,1)S(1)} %collective-permute-done.3.refs_1_, bf16[64,2560]{1,0:T(8,128)(2,1)S(1)} %collective-permute-done.2.refs_2_, ...), custom_call_target="tpu_custom_call" | custom-call | flops 1677721600 | bytes 8000000 | tf_op jit(solution)/shard_map/pallas_call | solution.py:180
  106.1 4.9 %all-to-all-done.1 = bf16[16,8,1280]{2,1,0:T(8,128)(2,1)S(1)} async-done(((bf16[16,8,1280]{2,1,0:T(8,128)(2,1)}), bf16[16,8,1280]{2,1,0:T(8,128)(2,1)S(1)}, u32[]{:S(2)}, u32[]{:S(2)}) %all-to-all-start.1) | async-done | bytes 327712 | tf_op jit(solution)/shard_map/all_to_all | solution.py:50
  112.3 11.5 %all_to_all.26 = bf16[16,2,1280]{2,1,0:T(2,128)(2,1)S(1)} all-to-all(bf16[16,2,1280]{2,1,0:T(2,128)(2,1)S(1)} %get-tuple-element.122), channel_id=1, replica_groups=mesh['yl'=2,'x'=4,'yh'=2,'z'=8,'c'=2] {'yl','x','c'}, dimensions={0} | all-to-all | bytes 163840 | tf_op jit(solution)/shard_map/all_to_all | solution.py:50
  123.9 13.6 %all_to_all.27 = bf16[16,2,1280]{2,1,0:T(2,128)(2,1)S(1)} all-to-all(bf16[16,2,1280]{2,1,0:T(2,128)(2,1)S(1)} %broadcast_in_dim.8), channel_id=1, replica_groups=mesh['yl'=2,'x'=4,'yh'=2,'z'=8,'c'=2] {'yh','z'}, dimensions={0} | all-to-all | bytes 163840 | tf_op jit(solution)/shard_map/all_to_all | solution.py:50
  138.3 5.1 %all-to-all-start.4 = ((bf16[16,2,1280]{2,1,0:T(2,128)(2,1)}), bf16[16,2,1280]{2,1,0:T(2,128)(2,1)S(1)}, u32[]{:S(2)}, u32[]{:S(2)}) async-start(bf16[16,2,1280]{2,1,0:T(2,128)(2,1)} %broadcast_in_dim.9), calls=%async_computation.4 | async-start | bytes 163840 | tf_op jit(solution)/shard_map/all_to_all | solution.py:50
  143.4 2.5 %shard_map.101 = (bf16[2,256,1280]{2,1,0:T(8,128)(2,1)}, bf16[2,256,1280]{2,1,0:T(8,128)(2,1)}) custom-call(s32[1]{0:T(128)} %bitcast.core, bf16[128,1280]{1,0:T(8,128)(2,1)S(1)} %bitcast.24, bf16[2,32,256]{2,1,0:T(8,128)(2,1)S(1)} %get-tuple-element.119.gates, f32[2,2,32,256]{3,2,1,0:T(8,128)S(1)} %shard_map.99.probs, bf16[32,1280]{1,0:T(8,128)(2,1)S(1)} %copy-done.5), custom_call_target="tpu_custom_call" | custom-call | flops 1000000000 | bytes 3000000 | tf_op jit(solution)/shard_map/pallas_call | solution.py:292
  146.0 3.4 %all-to-all-done.4 = bf16[16,2,1280]{2,1,0:T(2,128)(2,1)S(1)} async-done(((bf16[16,2,1280]{2,1,0:T(2,128)(2,1)}), bf16[16,2,1280]{2,1,0:T(2,128)(2,1)S(1)}, u32[]{:S(2)}, u32[]{:S(2)}) %all-to-all-start.4) | async-done | bytes 81952 | tf_op jit(solution)/shard_map/all_to_all | solution.py:50
  (83 shorter events, 23.3 us)
Async XLA Ops:
  28.5 3.7 %collective-permute-start = (bf16[32,2560]{1,0:T(8,128)(2,1)S(1)}, bf16[32,2560]{1,0:T(8,128)(2,1)S(1)}, u32[]{:S(2)}, u32[]{:S(2)}) collective-permute-start(bf16[32,2560]{1,0:T(8,128)(2,1)S(1)} %bitcast.30), channel_id=1, source_target_pairs={{0,1},{1,0},{2,3},{3,2},{4,5},{5,4},{6,7},{7,6},{8,9},{9,8},{10,11... | collective-permute-start | bytes 491528 | tf_op jit(solution)/shard_map/ppermute | solution.py:66
  32.2 11.7 %copy-start.1 = (bf16[1,640,1280]{2,1,0:T(8,128)(2,1)S(1)}, bf16[1,640,1280]{2,1,0:T(8,128)(2,1)}, u32[]{:S(2)}) copy-start(bf16[1,640,1280]{2,1,0:T(8,128)(2,1)} %param.8) | copy-start | bytes 4915204
  32.3 10.2 %collective-permute-start.3 = (bf16[64,2560]{1,0:T(8,128)(2,1)S(1)}, bf16[64,2560]{1,0:T(8,128)(2,1)S(1)}, u32[]{:S(2)}, u32[]{:S(2)}) collective-permute-start(bf16[64,2560]{1,0:T(8,128)(2,1)S(1)} %constant_dynamic-update-slice_fusion.refs_0_), channel_id=1, source_target_pairs={{0,32},{32,64},{64,96},{96,0},{1,33},{33,65},{65,97},{97,1},{2,34}... | collective-permute-start | bytes 983048 | tf_op jit(solution)/shard_map/ppermute | solution.py:54
  33.6 9.0 %collective-permute-start.2 = (bf16[64,2560]{1,0:T(8,128)(2,1)S(1)}, bf16[64,2560]{1,0:T(8,128)(2,1)S(1)}, u32[]{:S(2)}, u32[]{:S(2)}) collective-permute-start(bf16[64,2560]{1,0:T(8,128)(2,1)S(1)} %constant_dynamic-update-slice_fusion.refs_0_), channel_id=1, source_target_pairs={{0,96},{32,0},{64,32},{96,64},{1,97},{33,1},{65,33},{97,65},{2,98}... | collective-permute-start | bytes 983048 | tf_op jit(solution)/shard_map/ppermute | solution.py:58
  35.0 8.3 %collective-permute-start.1 = (bf16[64,2560]{1,0:T(8,128)(2,1)S(1)}, bf16[64,2560]{1,0:T(8,128)(2,1)S(1)}, u32[]{:S(2)}, u32[]{:S(2)}) collective-permute-start(bf16[64,2560]{1,0:T(8,128)(2,1)S(1)} %constant_dynamic-update-slice_fusion.refs_0_), channel_id=1, source_target_pairs={{0,128},{128,0},{1,129},{129,1},{2,130},{130,2},{3,131},{131,3},{4... | collective-permute-start | bytes 983048 | tf_op jit(solution)/shard_map/ppermute | solution.py:62
  43.4 7.5 %collective-permute-start.6 = (bf16[64,2560]{1,0:T(8,128)(2,1)S(1)}, bf16[64,2560]{1,0:T(8,128)(2,1)S(1)}, u32[]{:S(2)}, u32[]{:S(2)}) collective-permute-start(bf16[64,2560]{1,0:T(8,128)(2,1)S(1)} %get-tuple-element.135), channel_id=1, source_target_pairs={{0,128},{128,0},{1,129},{129,1},{2,130},{130,2},{3,131},{131,3},{4... | collective-permute-start | bytes 983048 | tf_op jit(solution)/shard_map/ppermute | solution.py:62
  43.9 8.9 %collective-permute-start.4 = (bf16[64,2560]{1,0:T(8,128)(2,1)S(1)}, bf16[64,2560]{1,0:T(8,128)(2,1)S(1)}, u32[]{:S(2)}, u32[]{:S(2)}) collective-permute-start(bf16[64,2560]{1,0:T(8,128)(2,1)S(1)} %get-tuple-element.137), channel_id=1, source_target_pairs={{0,32},{32,64},{64,96},{96,0},{1,33},{33,65},{65,97},{97,1},{2,34}... | collective-permute-start | bytes 983048 | tf_op jit(solution)/shard_map/ppermute | solution.py:54
  46.2 13.6 %copy-start.8 = (bf16[256,640]{1,0:T(8,128)(2,1)}, bf16[256,640]{1,0:T(8,128)(2,1)S(1)}, u32[]{:S(2)}) copy-start(bf16[256,640]{1,0:T(8,128)(2,1)S(1)} %get-tuple-element.104.refs_9_) | copy-start | bytes 983044
  46.3 13.6 %copy-start.10 = (bf16[256,640]{1,0:T(8,128)(2,1)}, bf16[256,640]{1,0:T(8,128)(2,1)S(1)}, u32[]{:S(2)}) copy-start(bf16[256,640]{1,0:T(8,128)(2,1)S(1)} %get-tuple-element.107.refs_12_) | copy-start | bytes 983044
  46.3 16.4 %collective-permute-start.8 = (bf16[64,2560]{1,0:T(8,128)(2,1)S(1)}, bf16[64,2560]{1,0:T(8,128)(2,1)S(1)}, u32[]{:S(2)}, u32[]{:S(2)}) collective-permute-start(bf16[64,2560]{1,0:T(8,128)(2,1)S(1)} %get-tuple-element.79), channel_id=1, source_target_pairs={{0,96},{32,0},{64,32},{96,64},{1,97},{33,1},{65,33},{97,65},{2,98}... | collective-permute-start | bytes 983048 | tf_op jit(solution)/shard_map/ppermute | solution.py:58
  50.9 6.4 %collective-permute-start.7 = (bf16[32,2560]{1,0:T(8,128)(2,1)S(1)}, bf16[32,2560]{1,0:T(8,128)(2,1)S(1)}, u32[]{:S(2)}, u32[]{:S(2)}) collective-permute-start(bf16[32,2560]{1,0:T(8,128)(2,1)S(1)} %slice.123), channel_id=1, source_target_pairs={{0,96},{32,0},{64,32},{96,64},{1,97},{33,1},{65,33},{97,65},{2,98}... | collective-permute-start | bytes 491528 | tf_op jit(solution)/shard_map/ppermute | solution.py:58
  52.8 5.5 %collective-permute-start.5 = (bf16[32,2560]{1,0:T(8,128)(2,1)S(1)}, bf16[32,2560]{1,0:T(8,128)(2,1)S(1)}, u32[]{:S(2)}, u32[]{:S(2)}) collective-permute-start(bf16[32,2560]{1,0:T(8,128)(2,1)S(1)} %slice.121), channel_id=1, source_target_pairs={{0,32},{32,64},{64,96},{96,0},{1,33},{33,65},{65,97},{97,1},{2,34}... | collective-permute-start | bytes 491528 | tf_op jit(solution)/shard_map/ppermute | solution.py:54
  59.9 5.7 %collective-permute-start.13 = (bf16[32,2560]{1,0:T(8,128)(2,1)S(1)}, bf16[32,2560]{1,0:T(8,128)(2,1)S(1)}, u32[]{:S(2)}, u32[]{:S(2)}) collective-permute-start(bf16[32,2560]{1,0:T(8,128)(2,1)S(1)} %get-tuple-element.85), channel_id=1, source_target_pairs={{0,32},{32,64},{64,96},{96,0},{1,33},{33,65},{65,97},{97,1},{2,34}... | collective-permute-start | bytes 491528 | tf_op jit(solution)/shard_map/ppermute | solution.py:54
  60.0 5.8 %collective-permute-start.9 = (bf16[32,2560]{1,0:T(8,128)(2,1)S(1)}, bf16[32,2560]{1,0:T(8,128)(2,1)S(1)}, u32[]{:S(2)}, u32[]{:S(2)}) collective-permute-start(bf16[32,2560]{1,0:T(8,128)(2,1)S(1)} %get-tuple-element.81), channel_id=1, source_target_pairs={{0,96},{32,0},{64,32},{96,64},{1,97},{33,1},{65,33},{97,65},{2,98}... | collective-permute-start | bytes 491528 | tf_op jit(solution)/shard_map/ppermute | solution.py:58
  64.7 6.0 %collective-permute-start.11 = (bf16[64,2560]{1,0:T(8,128)(2,1)S(1)}, bf16[64,2560]{1,0:T(8,128)(2,1)S(1)}, u32[]{:S(2)}, u32[]{:S(2)}) collective-permute-start(bf16[64,2560]{1,0:T(8,128)(2,1)S(1)} %get-tuple-element.82), channel_id=1, source_target_pairs={{0,128},{128,0},{1,129},{129,1},{2,130},{130,2},{3,131},{131,3},{4... | collective-permute-start | bytes 983048 | tf_op jit(solution)/shard_map/ppermute | solution.py:62
  65.7 7.5 %collective-permute-start.14 = (bf16[64,2560]{1,0:T(8,128)(2,1)S(1)}, bf16[64,2560]{1,0:T(8,128)(2,1)S(1)}, u32[]{:S(2)}, u32[]{:S(2)}) collective-permute-start(bf16[64,2560]{1,0:T(8,128)(2,1)S(1)} %pad_maximum_fusion.5), channel_id=1, source_target_pairs={{0,32},{32,64},{64,96},{96,0},{1,33},{33,65},{65,97},{97,1},{2,34}... | collective-permute-start | bytes 983048 | tf_op jit(solution)/shard_map/ppermute | solution.py:54
  65.9 7.3 %collective-permute-start.10 = (bf16[64,2560]{1,0:T(8,128)(2,1)S(1)}, bf16[64,2560]{1,0:T(8,128)(2,1)S(1)}, u32[]{:S(2)}, u32[]{:S(2)}) collective-permute-start(bf16[64,2560]{1,0:T(8,128)(2,1)S(1)} %pad_maximum_fusion.3), channel_id=1, source_target_pairs={{0,96},{32,0},{64,32},{96,64},{1,97},{33,1},{65,33},{97,65},{2,98}... | collective-permute-start | bytes 983048 | tf_op jit(solution)/shard_map/ppermute | solution.py:58
  73.5 8.4 %collective-permute-start.12 = (bf16[64,2560]{1,0:T(8,128)(2,1)S(1)}, bf16[64,2560]{1,0:T(8,128)(2,1)S(1)}, u32[]{:S(2)}, u32[]{:S(2)}) collective-permute-start(bf16[64,2560]{1,0:T(8,128)(2,1)S(1)} %pad_maximum_fusion.4), channel_id=1, source_target_pairs={{0,96},{32,0},{64,32},{96,64},{1,97},{33,1},{65,33},{97,65},{2,98}... | collective-permute-start | bytes 983048 | tf_op jit(solution)/shard_map/ppermute | solution.py:58
  76.5 7.2 %collective-permute-start.15 = (bf16[64,2560]{1,0:T(8,128)(2,1)S(1)}, bf16[64,2560]{1,0:T(8,128)(2,1)S(1)}, u32[]{:S(2)}, u32[]{:S(2)}) collective-permute-start(bf16[64,2560]{1,0:T(8,128)(2,1)S(1)} %pad_maximum_fusion.6), channel_id=1, source_target_pairs={{0,32},{32,64},{64,96},{96,0},{1,33},{33,65},{65,97},{97,1},{2,34}... | collective-permute-start | bytes 983048 | tf_op jit(solution)/shard_map/ppermute | solution.py:54
  76.7 7.1 %collective-permute-start.16 = (bf16[64,2560]{1,0:T(8,128)(2,1)S(1)}, bf16[64,2560]{1,0:T(8,128)(2,1)S(1)}, u32[]{:S(2)}, u32[]{:S(2)}) collective-permute-start(bf16[64,2560]{1,0:T(8,128)(2,1)S(1)} %pad_maximum_fusion.7), channel_id=1, source_target_pairs={{0,128},{128,0},{1,129},{129,1},{2,130},{130,2},{3,131},{131,3},{4... | collective-permute-start | bytes 983048 | tf_op jit(solution)/shard_map/ppermute | solution.py:62
  83.8 9.8 %collective-permute-start.17 = (bf16[32,2560]{1,0:T(8,128)(2,1)S(1)}, bf16[32,2560]{1,0:T(8,128)(2,1)S(1)}, u32[]{:S(2)}, u32[]{:S(2)}) collective-permute-start(bf16[32,2560]{1,0:T(8,128)(2,1)S(1)} %add_convert_fusion), channel_id=1, source_target_pairs={{0,1},{1,0},{2,3},{3,2},{4,5},{5,4},{6,7},{7,6},{8,9},{9,8},{10,11... | collective-permute-start | bytes 491528 | tf_op jit(solution)/shard_map/ppermute | solution.py:66
  94.7 16.3 %all-to-all-start.1 = ((bf16[16,8,1280]{2,1,0:T(8,128)(2,1)}), bf16[16,8,1280]{2,1,0:T(8,128)(2,1)S(1)}, u32[]{:S(2)}, u32[]{:S(2)}) async-start(bf16[16,8,1280]{2,1,0:T(8,128)(2,1)} %bitcast.7), calls=%async_computation.1 | async-start | bytes 655360 | tf_op jit(solution)/shard_map/all_to_all | solution.py:50
  111.0 32.5 %copy-start.5 = (bf16[32,1280]{1,0:T(8,128)(2,1)S(1)}, bf16[32,1280]{1,0:T(8,128)(2,1)}, u32[]{:S(2)}) copy-start(bf16[32,1280]{1,0:T(8,128)(2,1)} %router.3) | copy-start | bytes 245764
  138.3 11.0 %all-to-all-start.4 = ((bf16[16,2,1280]{2,1,0:T(2,128)(2,1)}), bf16[16,2,1280]{2,1,0:T(2,128)(2,1)S(1)}, u32[]{:S(2)}, u32[]{:S(2)}) async-start(bf16[16,2,1280]{2,1,0:T(2,128)(2,1)} %broadcast_in_dim.9), calls=%async_computation.4 | async-start | bytes 163840 | tf_op jit(solution)/shard_map/all_to_all | solution.py:50
  (8 other events, 15.9 us)
